TPU v7x, 32 devices: a whole 2x2x4 slice. The times are simulated.
32 devices in a mesh: space: 4 (over x, core), term: 8 (over z, y).
Axes of the slice: x: 2, y: 2, z: 4, core: 2. Of those that a mesh axis runs over, the one named last changes fastest.
Arguments:
- right_modes: float32 [32, 64, 256], P(('space', 'term')), may hold values from -0.0625 to 0.0625
- adjoint_modes: float32 [32, 64, 256], P(('space', 'term')), may hold values from -6 to 6
- conductivity_terms: float32 [32, 256, 256], P('space', 'term'), may hold values from -6 to 6
Outputs:
- reduced_blocks: float32 [256, 4096], P('term', 'space')
All inputs are finite; a program needn't handle non-finite values.
Results may differ from a plain program's by a relative error of at most 0.000098.
Values sent between devices are 32-bit elements; how exact they have to be, the bound alone decides.
No kernel may reach another device: no remote copies, remote signals or barrier semaphores. Data moves between devices by JAX's collectives and lax.ppermute only.
A program may use at most 64 MiB of HBM per device.

v0:
```python
import math

import jax
import jax.numpy as jnp
from jax import lax
from jax.sharding import PartitionSpec as P

GY = 32


def extended(block, sides, width):
    for axis, dim in sides:
        count = lax.axis_size(axis)
        forward = [(i, i + 1) for i in range(count - 1)]
        backward = [(target, source) for source, target in forward]
        low = lax.ppermute(
            lax.slice_in_dim(block, block.shape[dim] - width, None, axis=dim), axis, forward
        )
        high = lax.ppermute(lax.slice_in_dim(block, 0, width, axis=dim), axis, backward)
        block = jnp.concatenate([low, block, high], axis=dim)
    return block


def swapped(block, axis, apart):
    count = lax.axis_size(axis)
    route = []
    for low in range(count):
        high = low | 1 << apart
        if high != low and high < count:
            route += [(low, high), (high, low)]
    return lax.ppermute(block, axis, route)


def shifted_cells(values, offset):
    zeros = jnp.zeros(values.shape[:-1] + (abs(offset),), jnp.float32)
    if offset > 0:
        return jnp.concatenate([values[..., offset:], zeros], axis=-1)
    return jnp.concatenate([zeros, values[..., :offset]], axis=-1)


def apply_terms(field_pad, coeff_pad, row_len):
    width = field_pad.shape[-1]
    column = jnp.arange(width) % row_len
    keep_next = (column != row_len - 1).astype(jnp.float32)
    keep_prev = (column != 0).astype(jnp.float32)
    centre = field_pad[None, 1:-1]
    coeff = coeff_pad[:, 1:-1, None, :]
    pairs = [
        (field_pad[None, 2:], coeff_pad[:, 2:, None, :]),
        (field_pad[None, :-2], coeff_pad[:, :-2, None, :]),
        (shifted_cells(centre, row_len), shifted_cells(coeff, row_len)),
        (shifted_cells(centre, -row_len), shifted_cells(coeff, -row_len)),
        (shifted_cells(centre, 1) * keep_next, shifted_cells(coeff, 1) * keep_next),
        (shifted_cells(centre, -1) * keep_prev, shifted_cells(coeff, -1) * keep_prev),
    ]
    result = jnp.zeros(coeff.shape[:2] + centre.shape[2:], jnp.float32)
    for other_field, other_coeff in pairs:
        result = result + 0.5 * (coeff + other_coeff) * (centre - other_field)
    return result


def assemble(field_pad, coeff_pad, adjoint, per_turn):
    modes = field_pad.shape[1]
    terms = coeff_pad.shape[1]
    ordered = jnp.moveaxis(coeff_pad, 1, 0)
    ordered = ordered.reshape((terms // per_turn, per_turn) + ordered.shape[1:])

    def one_block(coeff_block):
        image = apply_terms(field_pad, coeff_block, GY)
        return jnp.einsum("zrp,gzsp->grs", adjoint, image, precision=lax.Precision.HIGHEST)

    blocks = lax.map(one_block, ordered)
    return blocks.reshape(terms, modes * modes)


def split_halves(values, upper):
    halves = values.reshape((2, values.shape[0] // 2) + values.shape[1:])
    kept = jnp.where(upper, halves[1], halves[0])
    sent = jnp.where(upper, halves[0], halves[1])
    return (kept, sent)


def local(right_modes, adjoint_modes, conductivity_terms):
    n_term = lax.axis_size("term")
    term_index = lax.axis_index("term")
    top_bit = n_term.bit_length() - 1
    rim_right = extended(right_modes, ((("space", "term"), 0),), 1)
    many_right = rim_right[None]
    many_adjoint = adjoint_modes[None]
    for bit in range(2):
        upper = term_index // (1 << bit) % 2 == 1
        other_right, other_adjoint = swapped((many_right, many_adjoint), "term", bit)
        many_right = jnp.where(
            upper,
            jnp.concatenate([other_right, many_right], 0),
            jnp.concatenate([many_right, other_right], 0),
        )
        many_adjoint = jnp.where(
            upper,
            jnp.concatenate([other_adjoint, many_adjoint], 0),
            jnp.concatenate([many_adjoint, other_adjoint], 0),
        )
    inner = many_right[:, 1:-1].reshape((-1,) + right_modes.shape[1:])
    tile_right = jnp.concatenate([many_right[0, :1], inner, many_right[-1, -1:]], 0)
    tile_adjoint = many_adjoint.reshape((-1,) + adjoint_modes.shape[1:])
    span = tile_adjoint.shape[0]
    slab_pad = extended(conductivity_terms, (("space", 0),), 1)
    windows = jnp.stack(
        [slab_pad[group * span : group * span + span + 2] for group in range(n_term // 4)], 0
    )
    for bit in range(top_bit - 1, 1, -1):
        upper = term_index // (1 << bit) % 2 == 1
        kept, sent = split_halves(windows, upper)
        came = swapped(sent, "term", bit)
        windows = jnp.where(
            upper, jnp.concatenate([came, kept], 2), jnp.concatenate([kept, came], 2)
        )
    tile_coeff = windows[0]
    levels = top_bit - 2
    local_terms = conductivity_terms.shape[1]
    rows = tile_coeff.shape[0]
    plane = tile_coeff.shape[2]
    split = tile_coeff.reshape((rows,) + (2,) * levels + (local_terms, plane))
    order = (0,) + tuple(range(levels, 0, -1)) + (levels + 1, levels + 2)
    tile_coeff = jnp.transpose(split, order).reshape(rows, local_terms << levels, plane)
    partial_value = assemble(tile_right, tile_coeff, tile_adjoint, math.gcd(tile_coeff.shape[1], 8))
    for bit in range(top_bit - 1, 1, -1):
        upper = term_index // (1 << bit) % 2 == 1
        kept, sent = split_halves(partial_value, upper)
        came = swapped(sent, "term", bit)
        partial_value = kept + came
    return lax.psum_scatter(partial_value, "space", scatter_dimension=1, tiled=True)


def solution(mesh):
    placed = (
        P(("space", "term"), None, None),
        P(("space", "term"), None, None),
        P("space", "term", None),
    )
    return jax.shard_map(
        local, mesh=mesh, in_specs=placed, out_specs=P("term", "space"), check_vma=False
    )
```

profile of v0, /device:TPU:0, one launch (start us, length us, event | category | flops | bytes accessed | tf_op | source)
XLA Modules:
  0.0 136.7 jit_solution(1289821301915548012)
XLA Ops:
  6.5 5.0 %collective-permute-start.3 = (f32[1,64,256]{2,1,0:T(8,128)}, f32[1,64,256]{2,1,0:T(8,128)S(1)}, u32[]{:S(2)}, u32[]{:S(2)}) collective-permute-start(f32[1,64,256]{2,1,0:T(8,128)} %param.5), channel_id=1, source_target_pairs={{0,1},{1,2},{2,3},{3,4},{4,5},{5,6},{6,7},{7,8},{8,9},{9,10},{10,1... | collective-permute-start | bytes 196616 | tf_op jit(solution)/shard_map/ppermute | solution.py:16
  11.5 1.3 collective-permute-start.4
  12.8 2.7 %collective-permute-start.7 = (f32[1,1,64,256]{3,2,1,0:T(8,128)}, f32[1,1,64,256]{3,2,1,0:T(8,128)S(1)}, u32[]{:S(2)}, u32[]{:S(2)}) collective-permute-start(f32[1,1,64,256]{3,2,1,0:T(8,128)} %bitcast.88), channel_id=1, source_target_pairs={{0,1},{1,0},{2,3},{3,2},{4,5},{5,4},{6,7},{7,6},{8,9},{9,8},{10,11... | collective-permute-start | bytes 196616 | tf_op jit(solution)/shard_map/ppermute | solution.py:31
  15.6 2.4 %collective-permute-done.4 = f32[1,64,256]{2,1,0:T(8,128)S(1)} collective-permute-done((f32[1,64,256]{2,1,0:T(8,128)}, f32[1,64,256]{2,1,0:T(8,128)S(1)}, u32[]{:S(2)}, u32[]{:S(2)}) %collective-permute-start.4) | collective-permute-done | bytes 65568 | tf_op jit(solution)/shard_map/ppermute | solution.py:19
  17.9 0.9 maximum_bitcast_fusion
  18.8 2.6 %collective-permute-start.5 = (f32[1,3,64,256]{3,2,1,0:T(8,128)S(1)}, f32[1,3,64,256]{3,2,1,0:T(8,128)S(1)}, u32[]{:S(2)}, u32[]{:S(2)}) collective-permute-start(f32[1,3,64,256]{3,2,1,0:T(8,128)S(1)} %maximum_bitcast_fusion), channel_id=1, source_target_pairs={{0,1},{1,0},{2,3},{3,2},{4,5},{5,4},{6,7},{7,6},{8,9},{9,8},{10,11... | collective-permute-start | bytes 589832 | tf_op jit(solution)/shard_map/ppermute | solution.py:31
  21.4 0.8 fusion.41
  22.1 1.3 collective-permute-start
  23.4 1.3 collective-permute-start.1
  24.8 0.9 maximum_select_fusion.4
  25.8 1.6 %collective-permute-start.8 = (f32[2,1,64,256]{3,2,1,0:T(8,128)S(1)}, f32[2,1,64,256]{3,2,1,0:T(8,128)S(1)}, u32[]{:S(2)}, u32[]{:S(2)}) collective-permute-start(f32[2,1,64,256]{3,2,1,0:T(8,128)S(1)} %maximum_select_fusion.4), channel_id=1, source_target_pairs={{0,2},{2,0},{1,3},{3,1},{4,6},{6,4},{5,7},{7,5},{8,10},{10,8},{9,1... | collective-permute-start | bytes 393224 | tf_op jit(solution)/shard_map/ppermute | solution.py:31
  28.2 1.0 select_bitcast_fusion
  29.2 4.0 %collective-permute-start.2 = (f32[1,6,32,256]{3,2,1,0:T(8,128)S(1)}, f32[1,6,32,256]{3,2,1,0:T(8,128)S(1)}, u32[]{:S(2)}, u32[]{:S(2)}) collective-permute-start(f32[1,6,32,256]{3,2,1,0:T(8,128)S(1)} %get-tuple-element.133), channel_id=1, source_target_pairs={{0,4},{4,0},{1,5},{5,1},{2,6},{6,2},{3,7},{7,3},{8,12},{12,8},{9,1... | collective-permute-start | bytes 589832 | tf_op jit(solution)/shard_map/ppermute | solution.py:31
  33.3 0.7 maximum_select_fusion.3
  34.0 8.0 %collective-permute-done.2 = f32[1,6,32,256]{3,2,1,0:T(8,128)S(1)} collective-permute-done((f32[1,6,32,256]{3,2,1,0:T(8,128)S(1)}, f32[1,6,32,256]{3,2,1,0:T(8,128)S(1)}, u32[]{:S(2)}, u32[]{:S(2)}) %collective-permute-start.2) | collective-permute-done | bytes 196640 | tf_op jit(solution)/shard_map/ppermute | solution.py:31
  42.3 1.3 collective-permute-done.6
  43.7 30.8 %while.12 = (s32[]{:T(128)}, f32[8,8,64,64]{2,3,1,0:T(8,128)S(1)}, f32[8,8,6,256]{3,2,1,0:T(8,128)S(1)}, f32[4,64,256]{2,1,0:T(8,128)S(1)}, f32[4,64,256]{2,1,0:...) while((s32[]{:T(128)}, f32[8,8,64,64]{2,3,1,0:T(8,128)S(1)}, ...), condition=%wide.region_1.2_spmd, body=%wide.region_0.1_spmd.sunk | while | flops 408930816 | bytes 8428921 | solution.py:72
  45.0 2.5 %fusion.57 = f32[8,8,64,64]{2,3,1,0:T(8,128)S(1)} fusion(f32[8,8,64,64]{2,3,1,0:T(8,128)S(1)} %get-tuple-element.233, s32[]{:T(128)} %get-tuple-element.232, f32[4,64,256]{2,1,0:T(8,128)S(1)} %get-tuple-element.209, f32[8,4,256]{2,1,0:T(4,128)S(1)} %get-tuple-element.215, f32[4,64,256]{2,1,0:T(8,128)S(1)} %get-tuple-element.216, ...), kind=kOutput, calls=%fused_computation.13.clone.1 | convolution fusion | flops 408420352 | bytes 2293764 | tf_op jit(solution)/shard_map/while/body/eval_jaxpr/zrp,gzsp->grs/dot_general | solution.py:70
  48.9 2.5 %fusion.57 = f32[8,8,64,64]{2,3,1,0:T(8,128)S(1)} fusion(f32[8,8,64,64]{2,3,1,0:T(8,128)S(1)} %get-tuple-element.233, s32[]{:T(128)} %get-tuple-element.232, f32[4,64,256]{2,1,0:T(8,128)S(1)} %get-tuple-element.209, f32[8,4,256]{2,1,0:T(4,128)S(1)} %get-tuple-element.215, f32[4,64,256]{2,1,0:T(8,128)S(1)} %get-tuple-element.216, ...), kind=kOutput, calls=%fused_computation.13.clone.1 | convolution fusion | flops 408420352 | bytes 2293764 | tf_op jit(solution)/shard_map/while/body/eval_jaxpr/zrp,gzsp->grs/dot_general | solution.py:70
  52.8 2.5 %fusion.57 = f32[8,8,64,64]{2,3,1,0:T(8,128)S(1)} fusion(f32[8,8,64,64]{2,3,1,0:T(8,128)S(1)} %get-tuple-element.233, s32[]{:T(128)} %get-tuple-element.232, f32[4,64,256]{2,1,0:T(8,128)S(1)} %get-tuple-element.209, f32[8,4,256]{2,1,0:T(4,128)S(1)} %get-tuple-element.215, f32[4,64,256]{2,1,0:T(8,128)S(1)} %get-tuple-element.216, ...), kind=kOutput, calls=%fused_computation.13.clone.1 | convolution fusion | flops 408420352 | bytes 2293764 | tf_op jit(solution)/shard_map/while/body/eval_jaxpr/zrp,gzsp->grs/dot_general | solution.py:70
  56.6 2.5 %fusion.57 = f32[8,8,64,64]{2,3,1,0:T(8,128)S(1)} fusion(f32[8,8,64,64]{2,3,1,0:T(8,128)S(1)} %get-tuple-element.233, s32[]{:T(128)} %get-tuple-element.232, f32[4,64,256]{2,1,0:T(8,128)S(1)} %get-tuple-element.209, f32[8,4,256]{2,1,0:T(4,128)S(1)} %get-tuple-element.215, f32[4,64,256]{2,1,0:T(8,128)S(1)} %get-tuple-element.216, ...), kind=kOutput, calls=%fused_computation.13.clone.1 | convolution fusion | flops 408420352 | bytes 2293764 | tf_op jit(solution)/shard_map/while/body/eval_jaxpr/zrp,gzsp->grs/dot_general | solution.py:70
  60.5 2.5 %fusion.57 = f32[8,8,64,64]{2,3,1,0:T(8,128)S(1)} fusion(f32[8,8,64,64]{2,3,1,0:T(8,128)S(1)} %get-tuple-element.233, s32[]{:T(128)} %get-tuple-element.232, f32[4,64,256]{2,1,0:T(8,128)S(1)} %get-tuple-element.209, f32[8,4,256]{2,1,0:T(4,128)S(1)} %get-tuple-element.215, f32[4,64,256]{2,1,0:T(8,128)S(1)} %get-tuple-element.216, ...), kind=kOutput, calls=%fused_computation.13.clone.1 | convolution fusion | flops 408420352 | bytes 2293764 | tf_op jit(solution)/shard_map/while/body/eval_jaxpr/zrp,gzsp->grs/dot_general | solution.py:70
  64.3 2.5 %fusion.57 = f32[8,8,64,64]{2,3,1,0:T(8,128)S(1)} fusion(f32[8,8,64,64]{2,3,1,0:T(8,128)S(1)} %get-tuple-element.233, s32[]{:T(128)} %get-tuple-element.232, f32[4,64,256]{2,1,0:T(8,128)S(1)} %get-tuple-element.209, f32[8,4,256]{2,1,0:T(4,128)S(1)} %get-tuple-element.215, f32[4,64,256]{2,1,0:T(8,128)S(1)} %get-tuple-element.216, ...), kind=kOutput, calls=%fused_computation.13.clone.1 | convolution fusion | flops 408420352 | bytes 2293764 | tf_op jit(solution)/shard_map/while/body/eval_jaxpr/zrp,gzsp->grs/dot_general | solution.py:70
  68.2 2.5 %fusion.57 = f32[8,8,64,64]{2,3,1,0:T(8,128)S(1)} fusion(f32[8,8,64,64]{2,3,1,0:T(8,128)S(1)} %get-tuple-element.233, s32[]{:T(128)} %get-tuple-element.232, f32[4,64,256]{2,1,0:T(8,128)S(1)} %get-tuple-element.209, f32[8,4,256]{2,1,0:T(4,128)S(1)} %get-tuple-element.215, f32[4,64,256]{2,1,0:T(8,128)S(1)} %get-tuple-element.216, ...), kind=kOutput, calls=%fused_computation.13.clone.1 | convolution fusion | flops 408420352 | bytes 2293764 | tf_op jit(solution)/shard_map/while/body/eval_jaxpr/zrp,gzsp->grs/dot_general | solution.py:70
  72.0 2.5 %fusion.57 = f32[8,8,64,64]{2,3,1,0:T(8,128)S(1)} fusion(f32[8,8,64,64]{2,3,1,0:T(8,128)S(1)} %get-tuple-element.233, s32[]{:T(128)} %get-tuple-element.232, f32[4,64,256]{2,1,0:T(8,128)S(1)} %get-tuple-element.209, f32[8,4,256]{2,1,0:T(4,128)S(1)} %get-tuple-element.215, f32[4,64,256]{2,1,0:T(8,128)S(1)} %get-tuple-element.216, ...), kind=kOutput, calls=%fused_computation.13.clone.1 | convolution fusion | flops 408420352 | bytes 2293764 | tf_op jit(solution)/shard_map/while/body/eval_jaxpr/zrp,gzsp->grs/dot_general | solution.py:70
  74.6 1.3 copy-done
  75.9 1.7 %slice_select_fusion = (f32[4,8,64,64]{2,3,1,0:T(8,128)S(1)}, f32[4,8,64,64]{2,3,1,0:T(8,128)S(1)}) fusion(f32[8,8,64,64]{2,3,1,0:T(8,128)} %copy-done, pred[]{:T(512)S(6)} %eq.19), kind=kLoop, calls=%fused_computation.44 | loop fusion | flops 262144 | bytes 2097153 | tf_op jit(solution)/shard_map/jit(_where)/select_n | solution.py:79
  78.0 1.2 select_n.172
  79.2 4.8 %collective-permute-start.9 = (f32[32,4096]{1,0:T(8,128)}, f32[32,4096]{1,0:T(8,128)S(1)}, u32[]{:S(2)}, u32[]{:S(2)}) collective-permute-start(f32[32,4096]{1,0:T(8,128)} %select_n.172), channel_id=1, source_target_pairs={{0,4},{4,0},{1,5},{5,1},{2,6},{6,2},{3,7},{7,3},{8,12},{12,8},{9,1... | collective-permute-start | bytes 1572872 | tf_op jit(solution)/shard_map/ppermute | solution.py:31
  84.7 23.2 %collective-permute-done.9 = f32[32,4096]{1,0:T(8,128)S(1)} collective-permute-done((f32[32,4096]{1,0:T(8,128)}, f32[32,4096]{1,0:T(8,128)S(1)}, u32[]{:S(2)}, u32[]{:S(2)}) %collective-permute-start.9) | collective-permute-done | bytes 524320 | tf_op jit(solution)/shard_map/ppermute | solution.py:31
  107.9 0.9 add.137
  108.8 21.1 %reduce-scatter.2.cloned.1.call-done = f32[32,1024]{1,0:T(8,128)} async-done(((f32[32,4096]{1,0:T(8,128)}), f32[32,1024]{1,0:T(8,128)}) %reduce-scatter.2.cloned.1.call-update) | async-done | bytes 131088 | tf_op jit(solution)/shard_map/reduce_scatter | solution.py:132
  (112 shorter events, 12.1 us)
Async XLA Ops:
  6.5 26.7 %copy-start.2 = (f32[1,64,256]{2,1,0:T(8,128)S(1)}, f32[1,64,256]{2,1,0:T(8,128)}, u32[]{:S(2)}) copy-start(f32[1,64,256]{2,1,0:T(8,128)} %param.6) | copy-start | bytes 196612
  6.5 123.4 %reduce-scatter.2.cloned.1.call-start = ((), (), s32[]{:S(2)}) async-start(), calls=%async_computation.1 | async-start | bytes 655360 | tf_op jit(solution)/shard_map/reduce_scatter | solution.py:132
  6.5 9.0 %collective-permute-start.3 = (f32[1,64,256]{2,1,0:T(8,128)}, f32[1,64,256]{2,1,0:T(8,128)S(1)}, u32[]{:S(2)}, u32[]{:S(2)}) collective-permute-start(f32[1,64,256]{2,1,0:T(8,128)} %param.5), channel_id=1, source_target_pairs={{0,1},{1,2},{2,3},{3,4},{4,5},{5,6},{6,7},{7,8},{8,9},{9,10},{10,1... | collective-permute-start | bytes 196616 | tf_op jit(solution)/shard_map/ppermute | solution.py:16
  11.5 6.4 %collective-permute-start.4 = (f32[1,64,256]{2,1,0:T(8,128)}, f32[1,64,256]{2,1,0:T(8,128)S(1)}, u32[]{:S(2)}, u32[]{:S(2)}) collective-permute-start(f32[1,64,256]{2,1,0:T(8,128)} %param.5), channel_id=1, source_target_pairs={{1,0},{2,1},{3,2},{4,3},{5,4},{6,5},{7,6},{8,7},{9,8},{10,9},{11,1... | collective-permute-start | bytes 196616 | tf_op jit(solution)/shard_map/ppermute | solution.py:19
  12.8 12.0 %collective-permute-start.7 = (f32[1,1,64,256]{3,2,1,0:T(8,128)}, f32[1,1,64,256]{3,2,1,0:T(8,128)S(1)}, u32[]{:S(2)}, u32[]{:S(2)}) collective-permute-start(f32[1,1,64,256]{3,2,1,0:T(8,128)} %bitcast.88), channel_id=1, source_target_pairs={{0,1},{1,0},{2,3},{3,2},{4,5},{5,4},{6,7},{7,6},{8,9},{9,8},{10,11... | collective-permute-start | bytes 196616 | tf_op jit(solution)/shard_map/ppermute | solution.py:31
  18.8 8.6 %collective-permute-start.5 = (f32[1,3,64,256]{3,2,1,0:T(8,128)S(1)}, f32[1,3,64,256]{3,2,1,0:T(8,128)S(1)}, u32[]{:S(2)}, u32[]{:S(2)}) collective-permute-start(f32[1,3,64,256]{3,2,1,0:T(8,128)S(1)} %maximum_bitcast_fusion), channel_id=1, source_target_pairs={{0,1},{1,0},{2,3},{3,2},{4,5},{5,4},{6,7},{7,6},{8,9},{9,8},{10,11... | collective-permute-start | bytes 589832 | tf_op jit(solution)/shard_map/ppermute | solution.py:31
  22.1 5.8 %collective-permute-start = (f32[1,32,256]{2,1,0:T(8,128)S(1)}, f32[1,32,256]{2,1,0:T(8,128)S(1)}, u32[]{:S(2)}, u32[]{:S(2)}) collective-permute-start(f32[1,32,256]{2,1,0:T(8,128)S(1)} %get-tuple-element.138), channel_id=1, source_target_pairs={{0,8},{8,16},{16,24},{1,9},{9,17},{17,25},{2,10},{10,18},{18,26},{... | collective-permute-start | bytes 98312 | tf_op jit(solution)/shard_map/ppermute | solution.py:16
  23.4 4.8 %collective-permute-start.1 = (f32[1,32,256]{2,1,0:T(8,128)S(1)}, f32[1,32,256]{2,1,0:T(8,128)S(1)}, u32[]{:S(2)}, u32[]{:S(2)}) collective-permute-start(f32[1,32,256]{2,1,0:T(8,128)S(1)} %get-tuple-element.137), channel_id=1, source_target_pairs={{8,0},{16,8},{24,16},{9,1},{17,9},{25,17},{10,2},{18,10},{26,18},{... | collective-permute-start | bytes 98312 | tf_op jit(solution)/shard_map/ppermute | solution.py:19
  25.8 7.5 %collective-permute-start.8 = (f32[2,1,64,256]{3,2,1,0:T(8,128)S(1)}, f32[2,1,64,256]{3,2,1,0:T(8,128)S(1)}, u32[]{:S(2)}, u32[]{:S(2)}) collective-permute-start(f32[2,1,64,256]{3,2,1,0:T(8,128)S(1)} %maximum_select_fusion.4), channel_id=1, source_target_pairs={{0,2},{2,0},{1,3},{3,1},{4,6},{6,4},{5,7},{7,5},{8,10},{10,8},{9,1... | collective-permute-start | bytes 393224 | tf_op jit(solution)/shard_map/ppermute | solution.py:31
  27.4 16.1 %collective-permute-start.6 = (f32[2,3,64,256]{3,2,1,0:T(8,128)S(1)}, f32[2,3,64,256]{3,2,1,0:T(8,128)S(1)}, u32[]{:S(2)}, u32[]{:S(2)}) collective-permute-start(f32[2,3,64,256]{3,2,1,0:T(8,128)S(1)} %maximum_select_fusion.2), channel_id=1, source_target_pairs={{0,2},{2,0},{1,3},{3,1},{4,6},{6,4},{5,7},{7,5},{8,10},{10,8},{9,1... | collective-permute-start | bytes 1179656 | tf_op jit(solution)/shard_map/ppermute | solution.py:31
  29.2 12.8 %collective-permute-start.2 = (f32[1,6,32,256]{3,2,1,0:T(8,128)S(1)}, f32[1,6,32,256]{3,2,1,0:T(8,128)S(1)}, u32[]{:S(2)}, u32[]{:S(2)}) collective-permute-start(f32[1,6,32,256]{3,2,1,0:T(8,128)S(1)} %get-tuple-element.133), channel_id=1, source_target_pairs={{0,4},{4,0},{1,5},{5,1},{2,6},{6,2},{3,7},{7,3},{8,12},{12,8},{9,1... | collective-permute-start | bytes 589832 | tf_op jit(solution)/shard_map/ppermute | solution.py:31
  44.1 1.0 copy-start.1
  47.9 1.0 copy-start.1
  51.8 1.0 copy-start.1
  55.7 1.0 copy-start.1
  59.5 1.0 copy-start.1
  63.4 1.0 copy-start.1
  67.2 1.0 copy-start.1
  71.1 1.0 copy-start.1
  74.6 1.3 copy-start
  79.2 28.7 %collective-permute-start.9 = (f32[32,4096]{1,0:T(8,128)}, f32[32,4096]{1,0:T(8,128)S(1)}, u32[]{:S(2)}, u32[]{:S(2)}) collective-permute-start(f32[32,4096]{1,0:T(8,128)} %select_n.172), channel_id=1, source_target_pairs={{0,4},{4,0},{1,5},{5,1},{2,6},{6,2},{3,7},{7,3},{8,12},{12,8},{9,1... | collective-permute-start | bytes 1572872 | tf_op jit(solution)/shard_map/ppermute | solution.py:31
Sparse Core Ops, SparseCore 0:
  108.9 20.9 reduce-scatter.1
where the time goes:
time: 137 us
  waiting for transfers between devices  56.2 us (41%)
  starting transfers between devices  25.1 us (18%)
  matrix products  20.4 us (15%)
  between operations  13.6 us (10%)
  local copies, waits for them, and re-layouts  11.7 us (9%)
  other arithmetic  9.05 us (7%)
    ppermute x6, waiting for transfers between devices, swapped(): return lax.ppermute(block, axis, route)  32.4 us
    reduce_scatter x1, waiting for transfers between devices, local(): lax.psum_scatter(partial_value, 'space', scatter_dimension=1, tiled=True)  21.1 us
    dot_general x8, matrix products, one_block(): jnp.einsum('zrp,gzsp->grs', adjoint, image, precision=lax.Precision.HIGHEST)  20.4 us
    ppermute x6, starting transfers between devices, swapped(): return lax.ppermute(block, axis, route)  16.3 us
    ppermute x2, starting transfers between devices, extended(): lax.ppermute(lax.slice_in_dim(block, block.shape[dim] - width, None, axis...  6.27 us
    while x16, local copies, waits for them, and re-layouts  3.6 us
    slice x32, local copies, waits for them, and re-layouts, shifted_cells(): return jnp.concatenate([values[..., offset:], zeros], axis=-1)  3.4 us
  transfers between devices with their start and end apart: 11, of which 6 were waited for; matrix products, arithmetic and copies ran while one was open for 4% of the time, Pallas kernels for 0%

commit v1 on v0

v1 whole, which is shorter than its diff:
```python
import functools

import jax
import jax.numpy as jnp
from jax import lax
from jax.experimental import pallas as pl
from jax.experimental.pallas import tpu as pltpu
from jax.sharding import PartitionSpec as P

GY = 32
OFFSETS = (GY, -GY, 1, -1)
NT = (((1,), (1,)), ((), ()))
F32 = jnp.float32
BF16 = jnp.bfloat16


def shifted(values, offset):
    width = values.shape[-1]
    lane = lax.broadcasted_iota(jnp.int32, values.shape, values.ndim - 1)
    moved = pltpu.roll(values, (-offset) % width, values.ndim - 1)
    if offset == GY:
        keep = lane < width - GY
    elif offset == -GY:
        keep = lane >= GY
    elif offset == 1:
        keep = lane % GY != GY - 1
    else:
        keep = lane % GY != 0
    return jnp.where(keep, moved, 0.0)


def split(values):
    high = values.astype(BF16)
    return high, (values - high.astype(F32)).astype(BF16)


def stage_kernel(stage, first, last, n_term, n_space, chunk, *refs):
    k_ref = refs[0]
    blocks = refs[1 : 3 + 2 * stage]
    rest = list(refs[3 + 2 * stage :])
    pairs = n_term // 2
    far = stage >= pairs // 2
    halo_ref = rest.pop(0) if far else None
    before_ref = None if first else rest.pop(0)
    if last:
        keep_ref, send_ref, acc_ref = rest[:3]
        rest = rest[3:]
    else:
        acc_ref = rest.pop(0)
    da_ref, kb_ref, w_ref, wz_ref = rest
    modes = blocks[0].shape[1]
    terms = k_ref.shape[1]
    cells = k_ref.shape[2]
    term_at = lax.axis_index("term")
    space_at = lax.axis_index("space")
    z, y = term_at // 2, term_at % 2
    w = z ^ stage
    own_ref, other_ref = blocks[2 * stage], blocks[2 * stage + 1]

    coeffs = (k_ref[2 * w + y], k_ref[2 * w + 1 - y])
    for m, ref in enumerate((own_ref, other_ref)):
        a = ref[1]
        for d, offset in enumerate(OFFSETS):
            da_ref[4 * m + d] = a - shifted(a, offset)
            kb_ref[4 * m + d] = 0.5 * (coeffs[m] + shifted(coeffs[m], offset))
        high, low = split(ref[0])
        both = jnp.concatenate([high, low], 0)
        w_ref[:, 2 * m * cells : (2 * m + 1) * cells] = both
        w_ref[:, (2 * m + 1) * cells : (2 * m + 2) * cells] = both
    da_ref[8] = own_ref[1] - other_ref[1]
    kb_ref[8] = 0.5 * (coeffs[0] + coeffs[1])

    def body(c, carry):
        rows_a, rows_b = [], []
        for step in range(chunk):
            def term_of(d):
                return kb_ref[d] * da_ref[d, pl.ds(c * chunk + step, 1), :]

            across = term_of(8)
            rows_a.append(term_of(0) + term_of(1) + term_of(2) + term_of(3) + across)
            rows_b.append(term_of(4) + term_of(5) + term_of(6) + term_of(7) - across)
        left = jnp.concatenate(
            split(jnp.concatenate(rows_a, 0)) + split(jnp.concatenate(rows_b, 0)), 1
        )
        out = lax.dot_general(left, w_ref[...], NT, preferred_element_type=F32)
        out = out.reshape(chunk, terms, 2 * modes)
        at = pl.ds(c * chunk, chunk)
        acc_ref[at] = out if first else before_ref[at] + out
        return carry

    lax.fori_loop(0, modes // chunk, body, 0)

    def layer():
        def layer_body(c, carry):
            rows = [
                kb_ref[8] * da_ref[8, pl.ds(c * chunk + step, 1), :] for step in range(chunk)
            ]
            left = jnp.concatenate(split(jnp.concatenate(rows, 0)), 1)
            out = lax.dot_general(left, wz_ref[...], NT, preferred_element_type=F32)
            acc_ref[pl.ds(c * chunk, chunk)] += out.reshape(chunk, terms, 2 * modes)
            return carry

        lax.fori_loop(0, modes // chunk, layer_body, 0)

    def edge(first_side, second_side, coeff):
        da_ref[8] = first_side[1] - second_side[1]
        kb_ref[8] = coeff
        high, low = split(first_side[0] - second_side[0])
        both = jnp.concatenate([high, low], 0)
        wz_ref[:, :cells] = both
        wz_ref[:, cells:] = both

    for upward in (0, 1):
        near_w = w + 1 if upward else w - 1
        for j in range(stage):
            for parity in (0, 1):
                @pl.when((near_w >= 0) & (near_w < pairs) & (near_w ^ z == j) & (y == parity))
                def _():
                    here = own_ref if parity == upward else other_ref
                    there = blocks[2 * j] if parity == 1 - upward else blocks[2 * j + 1]
                    plane = 2 * w + upward
                    edge(
                        here,
                        there,
                        0.5 * (k_ref[plane] + k_ref[plane + (1 if upward else -1)]),
                    )

        if stage:
            @pl.when((near_w >= 0) & (near_w < pairs) & (near_w ^ z < stage))
            def _():
                layer()

    is_low = term_at < n_term // 2
    for upward in (0, 1):
        at_rim = w == (pairs - 1 if upward else 0)
        plane = n_term - 1 if upward else 0
        near_side = jnp.logical_not(is_low) if upward else is_low
        if far:
            used = at_rim & jnp.logical_not(near_side)
        else:
            used = at_rim & near_side & (space_at == (n_space - 1 if upward else 0))
        for parity in (0, 1):
            @pl.when(used & (y == parity))
            def _():
                here = own_ref if parity == upward else other_ref
                if far:
                    halo = (halo_ref[:modes], halo_ref[modes : 2 * modes])
                    edge(here, halo, 0.5 * (k_ref[plane] + halo_ref[2 * modes :]))
                else:
                    edge(here, (0.0, 0.0), 0.5 * k_ref[plane])

        @pl.when(used)
        def _():
            layer()

    if last:
        core = space_at % 2
        rows = modes // n_space
        lane = lax.broadcasted_iota(jnp.int32, (terms, 2 * modes), 1)

        def pack(block, out_ref, index):
            for j in range(rows // 2):
                even = acc_ref[block * rows + 2 * j]
                odd = acc_ref[block * rows + 2 * j + 1]
                even = even + pltpu.roll(even, modes, 1)
                odd = odd + pltpu.roll(odd, modes, 1)
                out_ref[index, j] = jnp.where(lane < modes, even, odd)

        def pack_body(index, carry):
            pack(2 * index + core, keep_ref, index)
            pack(2 * index + 1 - core, send_ref, index)
            return carry

        lax.fori_loop(0, n_space // 2, pack_body, 0)


def run_stage(stage, n_term, n_space, coeffs, blocks, halo, before):
    pairs = n_term // 2
    first, last = stage == 0, stage == pairs - 1
    modes, cells = blocks[0].shape[1:]
    terms = coeffs.shape[1]
    chunk = 16
    acc_shape = (modes, terms, 2 * modes)
    operands = [coeffs] + list(blocks)
    if stage >= pairs // 2:
        operands.append(halo)
    if not first:
        operands.append(before)
    scratch = [
        pltpu.VMEM((9, modes, cells), F32),
        pltpu.VMEM((9, terms, cells), F32),
        pltpu.VMEM((2 * modes, 4 * cells), BF16),
        pltpu.VMEM((2 * modes, 2 * cells), BF16),
    ]
    if last:
        part = jax.ShapeDtypeStruct(
            (n_space // 2, modes // n_space // 2, terms, 2 * modes), F32
        )
        out_shape = [part, part]
        scratch = [pltpu.VMEM(acc_shape, F32)] + scratch
    else:
        out_shape = jax.ShapeDtypeStruct(acc_shape, F32)
    whole = pl.BlockSpec(memory_space=pltpu.VMEM)
    return pl.pallas_call(
        functools.partial(stage_kernel, stage, first, last, n_term, n_space, chunk),
        out_shape=out_shape,
        in_specs=[whole] * len(operands),
        out_specs=[whole, whole] if last else whole,
        scratch_shapes=scratch,
        compiler_params=pltpu.CompilerParams(vmem_limit_bytes=40 << 20),
        cost_estimate=pl.CostEstimate(
            flops=2 * 2 * 2 * terms * modes * 2 * modes * cells,
            bytes_accessed=4 << 20,
            transcendentals=0,
        ),
    )(*operands)


def exchange(values, axis, apart):
    count = lax.axis_size(axis)
    return lax.ppermute(values, axis, [(i, i ^ apart) for i in range(count)])


def local(right_modes, adjoint_modes, conductivity_terms):
    n_term, n_space = lax.axis_size("term"), lax.axis_size("space")
    term_at, space_at = lax.axis_index("term"), lax.axis_index("space")
    pairs = n_term // 2
    z, y = term_at // 2, term_at % 2
    modes, cells = right_modes.shape[1:]
    terms = conductivity_terms.shape[1]

    own = jnp.concatenate([right_modes, adjoint_modes], 0)
    blocks = [own, exchange(own, "term", 1)]
    for stage in range(1, pairs):
        came = exchange(own, "term", 2 * stage)
        blocks += [came, exchange(came, "term", 1)]

    is_low = term_at < n_term // 2
    wanted = jnp.where(is_low, z, (pairs - 1) ^ z)
    takes_own = (y == 0) == is_low
    rim = blocks[0]
    for j in range(pairs // 2):
        block = jnp.where(takes_own, blocks[2 * j], blocks[2 * j + 1])
        rim = block if j == 0 else jnp.where(wanted == j, block, rim)
    rim_coeff = jnp.where(is_low, conductivity_terms[0], conductivity_terms[-1])
    rim = jnp.concatenate([rim.reshape(2 * modes, cells), rim_coeff], 0)
    route = []
    for s in range(n_space - 1):
        for t in range(n_term):
            low, high = s * n_term + t, (s + 1) * n_term + t
            route.append((high, low) if t < n_term // 2 else (low, high))
    halo = lax.ppermute(rim, ("space", "term"), route)

    value = None
    for stage in range(pairs):
        value = run_stage(
            stage, n_term, n_space, conductivity_terms, blocks[: 2 * stage + 2], halo, value
        )
    keep, send = value
    total = keep + exchange(send, "space", 1)
    apart = 2
    while apart < n_space:
        bit = space_at // apart % 2
        halves = total.reshape((total.shape[0] // 2, 2) + total.shape[1:])
        send = lax.dynamic_index_in_dim(halves, 1 - bit, 1, keepdims=False)
        keep = lax.dynamic_index_in_dim(halves, bit, 1, keepdims=False)
        total = keep + exchange(send, "space", apart)
        apart *= 2
    return jnp.transpose(total[0], (1, 0, 2)).reshape(terms, -1)


def solution(mesh):
    placed = (
        P(("space", "term"), None, None),
        P(("space", "term"), None, None),
        P("space", "term", None),
    )
    return jax.shard_map(
        local, mesh=mesh, in_specs=placed, out_specs=P("term", "space"), check_vma=False
    )
```

time: 137 us -> 46.6 us (0.34)
  waiting for transfers between devices: 56.2 us -> 12.6 us
  matrix products: 20.4 us -> 0 us
  Pallas kernels: 0 us -> 17.9 us
  between operations: 13.6 us -> 0.15 us
  starting transfers between devices: 25.1 us -> 13.3 us
  local copies, waits for them, and re-layouts: 11.7 us -> 1.75 us
  other arithmetic: 9.05 us -> 0.76 us
    ppermute x10, waiting for transfers between devices: 35.1 us -> 12.6 us  [the longest x9 12.6 us: exchange(): return lax.ppermute(values, axis, [(i, i ^ apart) for i in range(count)])]
    reduce_scatter x1 -> x0, waiting for transfers between devices: 21.1 us -> none  [local(): lax.psum_scatter(partial_value, 'space', scatter_dimension=1, tiled=True)]
    dot_general x8 -> x0, matrix products: 20.4 us -> none  [one_block(): jnp.einsum('zrp,gzsp->grs', adjoint, image, precision=lax.Precision.HIGHEST)]
    pallas_call x0 -> x4, Pallas kernels: none -> 17.9 us  [run_stage(): pl.pallas_call(functools.partial(stage_kernel, stage, first, last, n_term...]
    ppermute x10, starting transfers between devices: 25.1 us -> 13.3 us  [the longest x9 12 us: exchange(): return lax.ppermute(values, axis, [(i, i ^ apart) for i in range(count)])]
    select_n x7 -> x2, other arithmetic: 4.5 us -> 0.04 us  [the longest x1 0.03 us: local(): rim = block if j == 0 else jnp.where(wanted == j, block, rim)]
    slice x33 -> x0, local copies, waits for them, and re-layouts: 4.18 us -> none  [the longest x32 3.4 us: shifted_cells(): return jnp.concatenate([values[..., offset:], zeros], axis=-1)]
    while x16 -> x0, local copies, waits for them, and re-layouts: 3.6 us -> none
  transfers between devices with their start and end apart: 11 -> 10, of which waited for: 6 -> 4; matrix products, arithmetic and copies ran while one was open for 4% -> 0% of each run, Pallas kernels for 0% -> 26%
where the time goes in v1:
time: 46.6 us; the launch traced here: 46.4 us
  Pallas kernels  17.9 us (38%)
  starting transfers between devices  13.3 us (29%)
  waiting for transfers between devices  12.6 us (27%)
  local copies, waits for them, and re-layouts  1.75 us (4%)
  other arithmetic  0.76 us (2%)
    pallas_call x4, Pallas kernels, run_stage(): pl.pallas_call(functools.partial(stage_kernel, stage, first, last, n_term...  17.9 us
    ppermute x9, waiting for transfers between devices, exchange(): return lax.ppermute(values, axis, [(i, i ^ apart) for i in range(count)])  12.6 us
    ppermute x9, starting transfers between devices, exchange(): return lax.ppermute(values, axis, [(i, i ^ apart) for i in range(count)])  12 us
    ppermute x1, starting transfers between devices, local(): halo = lax.ppermute(rim, ('space', 'term'), route)  1.29 us
  transfers between devices with their start and end apart: 10, of which 4 were waited for; matrix products, arithmetic and copies ran while one was open for 0% of the time, Pallas kernels for 26%

profile of v1, /device:TPU:0, one launch (start us, length us, event | category | flops | bytes accessed | tf_op | source)
XLA Modules:
  0.0 46.4 jit_solution(10274292822729559181)
XLA Ops:
  0.0 0.0 copy-start
  0.0 0.9 %constant_dynamic-update-slice_fusion.1 = f32[2,64,256]{2,1,0:T(8,128)S(1)} fusion(f32[1,64,256]{2,1,0:T(8,128)} %param.3), kind=kLoop, calls=%fused_computation.6 | loop fusion | bytes 131072
  0.9 0.8 %constant_dynamic-update-slice_fusion.refs_1_ = f32[2,64,256]{2,1,0:T(8,128)S(1)} fusion(f32[2,64,256]{2,1,0:T(8,128)S(1)} %constant_dynamic-update-slice_fusion.1, f32[1,64,256]{2,1,0:T(8,128)} %param.4), kind=kLoop, calls=%fused_computation.5 | loop fusion | bytes 131072 | tf_op jit(solution)/shard_map/concatenate | solution.py:232
  1.7 3.0 %collective-permute-start.1 = (f32[2,64,256]{2,1,0:T(8,128)S(1)}, f32[2,64,256]{2,1,0:T(8,128)S(1)}, u32[]{:S(2)}, u32[]{:S(2)}) collective-permute-start(f32[2,64,256]{2,1,0:T(8,128)S(1)} %constant_dynamic-update-slice_fusion.refs_1_), channel_id=1, source_target_pairs={{0,2},{1,3},{2,0},{3,1},{4,6},{5,7},{6,4},{7,5},{8,10},{9,11},{10,... | collective-permute-start | bytes 393224 | tf_op jit(solution)/shard_map/ppermute | solution.py:221
  4.8 1.5 %collective-permute-start = (f32[2,64,256]{2,1,0:T(8,128)S(1)}, f32[2,64,256]{2,1,0:T(8,128)S(1)}, u32[]{:S(2)}, u32[]{:S(2)}) collective-permute-start(f32[2,64,256]{2,1,0:T(8,128)S(1)} %constant_dynamic-update-slice_fusion.refs_1_), channel_id=1, source_target_pairs={{0,1},{1,0},{2,3},{3,2},{4,5},{5,4},{6,7},{7,6},{8,9},{9,8},{10,11... | collective-permute-start | bytes 393224 | tf_op jit(solution)/shard_map/ppermute | solution.py:221
  6.3 2.6 %collective-permute-start.3 = (f32[2,64,256]{2,1,0:T(8,128)S(1)}, f32[2,64,256]{2,1,0:T(8,128)S(1)}, u32[]{:S(2)}, u32[]{:S(2)}) collective-permute-start(f32[2,64,256]{2,1,0:T(8,128)S(1)} %constant_dynamic-update-slice_fusion.refs_1_), channel_id=1, source_target_pairs={{0,4},{1,5},{2,6},{3,7},{4,0},{5,1},{6,2},{7,3},{8,12},{9,13},{10,... | collective-permute-start | bytes 393224 | tf_op jit(solution)/shard_map/ppermute | solution.py:221
  8.9 0.2 collective-permute-start.5
  9.1 0.0 collective-permute-done.1.refs_3_
  9.1 2.2 %collective-permute-start.2 = (f32[2,64,256]{2,1,0:T(8,128)S(1)}, f32[2,64,256]{2,1,0:T(8,128)S(1)}, u32[]{:S(2)}, u32[]{:S(2)}) collective-permute-start(f32[2,64,256]{2,1,0:T(8,128)S(1)} %collective-permute-done.1.refs_3_), channel_id=1, source_target_pairs={{0,1},{1,0},{2,3},{3,2},{4,5},{5,4},{6,7},{7,6},{8,9},{9,8},{10,11... | collective-permute-start | bytes 393224 | tf_op jit(solution)/shard_map/ppermute | solution.py:221
  11.3 0.0 copy-done
  11.4 0.0 collective-permute-done.refs_2_
  11.4 2.9 %collective-permute-done.2.refs_4_ = f32[2,64,256]{2,1,0:T(8,128)S(1)} collective-permute-done((f32[2,64,256]{2,1,0:T(8,128)S(1)}, f32[2,64,256]{2,1,0:T(8,128)S(1)}, u32[]{:S(2)}, u32[]{:S(2)}) %collective-permute-start.2) | collective-permute-done | bytes 131104 | tf_op jit(solution)/shard_map/ppermute | solution.py:221
  14.3 1.3 %collective-permute-start.7 = (f32[160,256]{1,0:T(8,128)S(1)}, f32[160,256]{1,0:T(8,128)S(1)}, u32[]{:S(2)}, u32[]{:S(2)}) collective-permute-start(f32[160,256]{1,0:T(8,128)S(1)} %pad_maximum_fusion), channel_id=1, source_target_pairs={{8,0},{9,1},{10,2},{11,3},{4,12},{5,13},{6,14},{7,15},{16,8},{17,9... | collective-permute-start | bytes 491528 | tf_op jit(solution)/shard_map/ppermute | solution.py:252
  15.6 2.9 %collective-permute-done.3.refs_5_ = f32[2,64,256]{2,1,0:T(8,128)S(1)} collective-permute-done((f32[2,64,256]{2,1,0:T(8,128)S(1)}, f32[2,64,256]{2,1,0:T(8,128)S(1)}, u32[]{:S(2)}, u32[]{:S(2)}) %collective-permute-start.3) | collective-permute-done | bytes 131104 | tf_op jit(solution)/shard_map/ppermute | solution.py:221
  18.5 0.9 %collective-permute-start.4 = (f32[2,64,256]{2,1,0:T(8,128)S(1)}, f32[2,64,256]{2,1,0:T(8,128)S(1)}, u32[]{:S(2)}, u32[]{:S(2)}) collective-permute-start(f32[2,64,256]{2,1,0:T(8,128)S(1)} %collective-permute-done.3.refs_5_), channel_id=1, source_target_pairs={{0,1},{1,0},{2,3},{3,2},{4,5},{5,4},{6,7},{7,6},{8,9},{9,8},{10,11... | collective-permute-start | bytes 393224 | tf_op jit(solution)/shard_map/ppermute | solution.py:221
  19.4 0.0 collective-permute-done.5.refs_7_
  19.4 1.1 %collective-permute-start.6 = (f32[2,64,256]{2,1,0:T(8,128)S(1)}, f32[2,64,256]{2,1,0:T(8,128)S(1)}, u32[]{:S(2)}, u32[]{:S(2)}) collective-permute-start(f32[2,64,256]{2,1,0:T(8,128)S(1)} %collective-permute-done.5.refs_7_), channel_id=1, source_target_pairs={{0,1},{1,0},{2,3},{3,2},{4,5},{5,4},{6,7},{7,6},{8,9},{9,8},{10,11... | collective-permute-start | bytes 393224 | tf_op jit(solution)/shard_map/ppermute | solution.py:221
  20.5 4.2 %shard_map.37.refs_5_ = f32[64,32,128]{2,1,0:T(8,128)S(1)} custom-call(f32[8,32,256]{2,1,0:T(8,128)S(1)} %copy-done, f32[2,64,256]{2,1,0:T(8,128)S(1)} %constant_dynamic-update-slice_fusion.refs_1_, f32[2,64,256]{2,1,0:T(8,128)S(1)} %collective-permute-done.refs_2_), custom_call_target="tpu_custom_call" | custom-call | flops 536870912 | bytes 4194304 | tf_op jit(solution)/shard_map/pallas_call | solution.py:204
  24.7 4.0 %shard_map.38.refs_8_ = f32[64,32,128]{2,1,0:T(8,128)S(1)} custom-call(f32[8,32,256]{2,1,0:T(8,128)S(1)} %copy-done, f32[2,64,256]{2,1,0:T(8,128)S(1)} %constant_dynamic-update-slice_fusion.refs_1_, f32[2,64,256]{2,1,0:T(8,128)S(1)} %collective-permute-done.refs_2_, f32[2,64,256]{2,1,0:T(8,128)S(1)} %collective-permute-done.1.refs_3_, ...), custom_call_target="tpu_custom_call" | custom-call | flops 536870912 | bytes 4194304 | tf_op jit(solution)/shard_map/pallas_call | solution.py:204
  28.7 0.0 collective-permute-done.4.refs_6_
  28.7 0.0 collective-permute-done.7.refs_7_.refs_9_
  28.8 4.0 %shard_map.39.refs_10_ = f32[64,32,128]{2,1,0:T(8,128)S(1)} custom-call(f32[8,32,256]{2,1,0:T(8,128)S(1)} %copy-done, f32[2,64,256]{2,1,0:T(8,128)S(1)} %constant_dynamic-update-slice_fusion.refs_1_, f32[2,64,256]{2,1,0:T(8,128)S(1)} %collective-permute-done.refs_2_, f32[2,64,256]{2,1,0:T(8,128)S(1)} %collective-permute-done.1.refs_3_, ...), custom_call_target="tpu_custom_call" | custom-call | flops 536870912 | bytes 4194304 | tf_op jit(solution)/shard_map/pallas_call | solution.py:204
  32.8 0.0 collective-permute-done.6.refs_8_
  32.8 5.7 %shard_map.40 = (f32[2,8,32,128]{3,2,1,0:T(8,128)S(1)}, f32[2,8,32,128]{3,2,1,0:T(8,128)S(1)}) custom-call(f32[8,32,256]{2,1,0:T(8,128)S(1)} %copy-done, f32[2,64,256]{2,1,0:T(8,128)S(1)} %constant_dynamic-update-slice_fusion.refs_1_, f32[2,64,256]{2,1,0:T(8,128)S(1)} %collective-permute-done.refs_2_, f32[2,64,256]{2,1,0:T(8,128)S(1)} %collective-permute-done.1.refs_3_, ...), custom_call_target="tpu_custom_call" | custom-call | flops 536870912 | bytes 4194304 | tf_op jit(solution)/shard_map/pallas_call | solution.py:204
  38.5 0.1 collective-permute-start.8
  38.6 1.5 %collective-permute-done.8 = f32[2,8,32,128]{3,2,1,0:T(8,128)S(1)} collective-permute-done((f32[2,8,32,128]{3,2,1,0:T(8,128)S(1)}, f32[2,8,32,128]{3,2,1,0:T(8,128)S(1)}, u32[]{:S(2)}, u32[]{:S(2)}) %collective-permute-start.8) | collective-permute-done | bytes 262176 | tf_op jit(solution)/shard_map/ppermute | solution.py:221
  40.2 0.3 collective-permute-start.9
  40.5 5.3 %collective-permute-done.9 = f32[1,8,32,128]{3,2,1,0:T(8,128)S(1)} collective-permute-done((f32[1,8,32,128]{3,2,1,0:T(8,128)S(1)}, f32[1,8,32,128]{3,2,1,0:T(8,128)S(1)}, u32[]{:S(2)}, u32[]{:S(2)}) %collective-permute-start.9) | collective-permute-done | bytes 131104 | tf_op jit(solution)/shard_map/ppermute | solution.py:221
  45.8 0.7 %copy_bitcast_fusion = f32[32,1024]{1,0:T(8,128)} fusion(f32[1,8,32,128]{3,2,1,0:T(8,128)S(1)} %collective-permute-done.9, f32[2,8,32,128]{3,2,1,0:T(8,128)S(1)} %add.24, s32[]{:T(128)S(6)} %select_n.70), kind=kLoop, calls=%fused_computation.1 | loop fusion | flops 32768 | bytes 393220 | tf_op jit(solution)/shard_map/reshape | solution.py:269
  (5 shorter events, 0.1 us)
Async XLA Ops:
  0.0 11.3 %copy-start = (f32[8,32,256]{2,1,0:T(8,128)S(1)}, f32[8,32,256]{2,1,0:T(8,128)}, u32[]{:S(2)}) copy-start(f32[8,32,256]{2,1,0:T(8,128)} %refs_0_.7) | copy-start | bytes 786436
  1.7 7.4 %collective-permute-start.1 = (f32[2,64,256]{2,1,0:T(8,128)S(1)}, f32[2,64,256]{2,1,0:T(8,128)S(1)}, u32[]{:S(2)}, u32[]{:S(2)}) collective-permute-start(f32[2,64,256]{2,1,0:T(8,128)S(1)} %constant_dynamic-update-slice_fusion.refs_1_), channel_id=1, source_target_pairs={{0,2},{1,3},{2,0},{3,1},{4,6},{5,7},{6,4},{7,5},{8,10},{9,11},{10,... | collective-permute-start | bytes 393224 | tf_op jit(solution)/shard_map/ppermute | solution.py:221
  4.8 6.6 %collective-permute-start = (f32[2,64,256]{2,1,0:T(8,128)S(1)}, f32[2,64,256]{2,1,0:T(8,128)S(1)}, u32[]{:S(2)}, u32[]{:S(2)}) collective-permute-start(f32[2,64,256]{2,1,0:T(8,128)S(1)} %constant_dynamic-update-slice_fusion.refs_1_), channel_id=1, source_target_pairs={{0,1},{1,0},{2,3},{3,2},{4,5},{5,4},{6,7},{7,6},{8,9},{9,8},{10,11... | collective-permute-start | bytes 393224 | tf_op jit(solution)/shard_map/ppermute | solution.py:221
  6.3 12.2 %collective-permute-start.3 = (f32[2,64,256]{2,1,0:T(8,128)S(1)}, f32[2,64,256]{2,1,0:T(8,128)S(1)}, u32[]{:S(2)}, u32[]{:S(2)}) collective-permute-start(f32[2,64,256]{2,1,0:T(8,128)S(1)} %constant_dynamic-update-slice_fusion.refs_1_), channel_id=1, source_target_pairs={{0,4},{1,5},{2,6},{3,7},{4,0},{5,1},{6,2},{7,3},{8,12},{9,13},{10,... | collective-permute-start | bytes 393224 | tf_op jit(solution)/shard_map/ppermute | solution.py:221
  8.9 10.6 %collective-permute-start.5 = (f32[2,64,256]{2,1,0:T(8,128)S(1)}, f32[2,64,256]{2,1,0:T(8,128)S(1)}, u32[]{:S(2)}, u32[]{:S(2)}) collective-permute-start(f32[2,64,256]{2,1,0:T(8,128)S(1)} %constant_dynamic-update-slice_fusion.refs_1_), channel_id=1, source_target_pairs={{0,6},{1,7},{2,4},{3,5},{4,2},{5,3},{6,0},{7,1},{8,14},{9,15},{10,... | collective-permute-start | bytes 393224 | tf_op jit(solution)/shard_map/ppermute | solution.py:221
  9.1 5.2 %collective-permute-start.2 = (f32[2,64,256]{2,1,0:T(8,128)S(1)}, f32[2,64,256]{2,1,0:T(8,128)S(1)}, u32[]{:S(2)}, u32[]{:S(2)}) collective-permute-start(f32[2,64,256]{2,1,0:T(8,128)S(1)} %collective-permute-done.1.refs_3_), channel_id=1, source_target_pairs={{0,1},{1,0},{2,3},{3,2},{4,5},{5,4},{6,7},{7,6},{8,9},{9,8},{10,11... | collective-permute-start | bytes 393224 | tf_op jit(solution)/shard_map/ppermute | solution.py:221
  14.3 14.4 %collective-permute-start.7 = (f32[160,256]{1,0:T(8,128)S(1)}, f32[160,256]{1,0:T(8,128)S(1)}, u32[]{:S(2)}, u32[]{:S(2)}) collective-permute-start(f32[160,256]{1,0:T(8,128)S(1)} %pad_maximum_fusion), channel_id=1, source_target_pairs={{8,0},{9,1},{10,2},{11,3},{4,12},{5,13},{6,14},{7,15},{16,8},{17,9... | collective-permute-start | bytes 491528 | tf_op jit(solution)/shard_map/ppermute | solution.py:252
  18.5 10.2 %collective-permute-start.4 = (f32[2,64,256]{2,1,0:T(8,128)S(1)}, f32[2,64,256]{2,1,0:T(8,128)S(1)}, u32[]{:S(2)}, u32[]{:S(2)}) collective-permute-start(f32[2,64,256]{2,1,0:T(8,128)S(1)} %collective-permute-done.3.refs_5_), channel_id=1, source_target_pairs={{0,1},{1,0},{2,3},{3,2},{4,5},{5,4},{6,7},{7,6},{8,9},{9,8},{10,11... | collective-permute-start | bytes 393224 | tf_op jit(solution)/shard_map/ppermute | solution.py:221
  19.4 13.3 %collective-permute-start.6 = (f32[2,64,256]{2,1,0:T(8,128)S(1)}, f32[2,64,256]{2,1,0:T(8,128)S(1)}, u32[]{:S(2)}, u32[]{:S(2)}) collective-permute-start(f32[2,64,256]{2,1,0:T(8,128)S(1)} %collective-permute-done.5.refs_7_), channel_id=1, source_target_pairs={{0,1},{1,0},{2,3},{3,2},{4,5},{5,4},{6,7},{7,6},{8,9},{9,8},{10,11... | collective-permute-start | bytes 393224 | tf_op jit(solution)/shard_map/ppermute | solution.py:221
  38.5 1.6 %collective-permute-start.8 = (f32[2,8,32,128]{3,2,1,0:T(8,128)S(1)}, f32[2,8,32,128]{3,2,1,0:T(8,128)S(1)}, u32[]{:S(2)}, u32[]{:S(2)}) collective-permute-start(f32[2,8,32,128]{3,2,1,0:T(8,128)S(1)} %get-tuple-element.8), channel_id=1, source_target_pairs={{0,8},{8,0},{16,24},{24,16},{1,9},{9,1},{17,25},{25,17},{2,10},{10... | collective-permute-start | bytes 786440 | tf_op jit(solution)/shard_map/ppermute | solution.py:221
  40.2 5.6 %collective-permute-start.9 = (f32[1,8,32,128]{3,2,1,0:T(8,128)S(1)}, f32[1,8,32,128]{3,2,1,0:T(8,128)S(1)}, u32[]{:S(2)}, u32[]{:S(2)}) collective-permute-start(f32[1,8,32,128]{3,2,1,0:T(8,128)S(1)} %constant_dynamic-slice_fusion), channel_id=1, source_target_pairs={{0,16},{8,24},{16,0},{24,8},{1,17},{9,25},{17,1},{25,9},{2,18},{10... | collective-permute-start | bytes 393224 | tf_op jit(solution)/shard_map/ppermute | solution.py:221

commit v2 on v1

v2 whole, which is shorter than its diff:
```python
import functools

import jax
import jax.numpy as jnp
from jax import lax
from jax.experimental import pallas as pl
from jax.experimental.pallas import tpu as pltpu
from jax.sharding import PartitionSpec as P

GY = 32
OFFSETS = (GY, -GY, 1, -1)
NT = (((1,), (1,)), ((), ()))
F32 = jnp.float32
BF16 = jnp.bfloat16


def shifted(values, offset):
    width = values.shape[-1]
    lane = lax.broadcasted_iota(jnp.int32, values.shape, values.ndim - 1)
    moved = pltpu.roll(values, (-offset) % width, values.ndim - 1)
    if offset == GY:
        keep = lane < width - GY
    elif offset == -GY:
        keep = lane >= GY
    elif offset == 1:
        keep = lane % GY != GY - 1
    else:
        keep = lane % GY != 0
    return jnp.where(keep, moved, 0.0)


def split(values):
    high = values.astype(BF16)
    return high, (values - high.astype(F32)).astype(BF16)


def stage_kernel(stage, first, last, n_term, n_space, *refs):
    k_ref = refs[0]
    blocks = refs[1 : 3 + 2 * stage]
    rest = list(refs[3 + 2 * stage :])
    pairs = n_term // 2
    far = stage >= pairs // 2
    halo_ref = rest.pop(0) if far else None
    before_ref = None if first else rest.pop(0)
    if last:
        keep_ref, send_ref, acc_ref = rest[:3]
        rest = rest[3:]
    else:
        acc_ref = rest.pop(0)
    da_ref, kb_ref, w_ref, dz_ref, kz_ref, wz_ref = rest
    modes = blocks[0].shape[1]
    terms = k_ref.shape[1]
    cells = k_ref.shape[2]
    group = 16
    term_at = lax.axis_index("term")
    space_at = lax.axis_index("space")
    z, y = term_at // 2, term_at % 2
    w = z ^ stage
    own_ref, other_ref = blocks[2 * stage], blocks[2 * stage + 1]

    coeffs = (k_ref[2 * w + y], k_ref[2 * w + 1 - y])
    fields = [ref[1] for ref in (own_ref, other_ref)]
    for m, ref in enumerate((own_ref, other_ref)):
        for d, offset in enumerate(OFFSETS):
            da_ref[4 * m + d] = fields[m] - shifted(fields[m], offset)
            kb_ref[4 * m + d] = 0.5 * (coeffs[m] + shifted(coeffs[m], offset))
        both = jnp.concatenate(split(ref[0]), 0)
        w_ref[:, 2 * m * cells : (2 * m + 1) * cells] = both
        w_ref[:, (2 * m + 1) * cells : (2 * m + 2) * cells] = both
    da_ref[8] = fields[0] - fields[1]
    kb_ref[8] = 0.5 * (coeffs[0] + coeffs[1])

    for r in range(0, modes, group):
        da = [da_ref[d, r : r + group, :] for d in range(9)]
        rows_a, rows_b = [], []
        for q in range(terms):
            part = [da[d] * kb_ref[d, q : q + 1, :] for d in range(9)]
            rows_a.append((part[0] + part[1]) + (part[2] + part[3]) + part[8])
            rows_b.append((part[4] + part[5]) + (part[6] + part[7]) - part[8])
        left = jnp.concatenate(
            split(jnp.concatenate(rows_a, 0)) + split(jnp.concatenate(rows_b, 0)), 1
        )
        out = lax.dot_general(left, w_ref[...], NT, preferred_element_type=F32)
        out = out.reshape(terms, group, 2 * modes)
        acc_ref[:, r : r + group] = out if first else before_ref[:, r : r + group] + out

    def edge(slot, here, there, coeff):
        dz_ref[slot] = here[1] - (0.0 if there is None else there[1])
        kz_ref[slot] = coeff
        both = jnp.concatenate(split(here[0] - (0.0 if there is None else there[0])), 0)
        wz_ref[slot, :, :cells] = both
        wz_ref[slot, :, cells:] = both

    count = 0
    for upward in (0, 1):
        near_w = w + 1 if upward else w - 1
        inside = (near_w >= 0) & (near_w < pairs)
        for j in range(stage):
            for parity in (0, 1):
                @pl.when(inside & (near_w ^ z == j) & (y == parity))
                def _(slot=count):
                    here = own_ref if parity == upward else other_ref
                    there = blocks[2 * j] if parity == 1 - upward else blocks[2 * j + 1]
                    plane = 2 * w + upward
                    edge(
                        slot,
                        here,
                        there,
                        0.5 * (k_ref[plane] + k_ref[plane + (1 if upward else -1)]),
                    )

        count = count + jnp.where(inside & (near_w ^ z < stage), 1, 0)

    is_low = term_at < n_term // 2
    for upward in (0, 1):
        at_rim = w == (pairs - 1 if upward else 0)
        plane = n_term - 1 if upward else 0
        near_side = jnp.logical_not(is_low) if upward else is_low
        if far:
            used = at_rim & jnp.logical_not(near_side)
        else:
            used = at_rim & near_side & (space_at == (n_space - 1 if upward else 0))
        for parity in (0, 1):
            @pl.when(used & (y == parity))
            def _(slot=count):
                here = own_ref if parity == upward else other_ref
                if far:
                    halo = halo_ref.at[: 2 * modes].reshape(2, modes, cells)
                    edge(slot, here, halo, 0.5 * (k_ref[plane] + halo_ref[2 * modes :]))
                else:
                    edge(slot, here, None, 0.5 * k_ref[plane])

        count = count + jnp.where(used, 1, 0)

    def layer(slot, carry):
        for r in range(0, modes, group):
            dz = dz_ref[slot, r : r + group, :]
            rows = [dz * kz_ref[slot, q : q + 1, :] for q in range(terms)]
            left = jnp.concatenate(split(jnp.concatenate(rows, 0)), 1)
            out = lax.dot_general(left, wz_ref[slot], NT, preferred_element_type=F32)
            acc_ref[:, r : r + group] += out.reshape(terms, group, 2 * modes)
        return carry

    lax.fori_loop(0, count, layer, 0)

    if last:
        core = space_at % 2
        lane = lax.broadcasted_iota(jnp.int32, (terms, 8, 2 * modes), 2)
        groups = []
        for r in range(0, modes, group):
            even = acc_ref[:, pl.ds(r, 8, stride=2), :]
            odd = acc_ref[:, pl.ds(r + 1, 8, stride=2), :]
            even = even + pltpu.roll(even, modes, 2)
            odd = odd + pltpu.roll(odd, modes, 2)
            groups.append(jnp.where(lane < modes, even, odd))
        packed = jnp.concatenate(groups, 1)
        width = packed.shape[1] // n_space
        for index in range(n_space // 2):
            low = packed[:, 2 * index * width : (2 * index + 1) * width]
            high = packed[:, (2 * index + 1) * width : (2 * index + 2) * width]
            keep_ref[index] = jnp.where(core == 0, low, high)
            send_ref[index] = jnp.where(core == 0, high, low)


def run_stage(stage, n_term, n_space, coeffs, blocks, halo, before):
    pairs = n_term // 2
    first, last = stage == 0, stage == pairs - 1
    modes, cells = blocks[0].shape[1:]
    terms = coeffs.shape[1]
    acc_shape = (terms, modes, 2 * modes)
    operands = [coeffs] + list(blocks)
    if stage >= pairs // 2:
        operands.append(halo)
    if not first:
        operands.append(before)
    scratch = [
        pltpu.VMEM((9, modes, cells), F32),
        pltpu.VMEM((9, terms, cells), F32),
        pltpu.VMEM((2 * modes, 4 * cells), BF16),
        pltpu.VMEM((3, modes, cells), F32),
        pltpu.VMEM((3, terms, cells), F32),
        pltpu.VMEM((3, 2 * modes, 2 * cells), BF16),
    ]
    if last:
        part = jax.ShapeDtypeStruct(
            (n_space // 2, terms, modes // n_space // 2, 2 * modes), F32
        )
        out_shape = [part, part]
        scratch = [pltpu.VMEM(acc_shape, F32)] + scratch
    else:
        out_shape = jax.ShapeDtypeStruct(acc_shape, F32)
    whole = pl.BlockSpec(memory_space=pltpu.VMEM)
    return pl.pallas_call(
        functools.partial(stage_kernel, stage, first, last, n_term, n_space),
        out_shape=out_shape,
        in_specs=[whole] * len(operands),
        out_specs=[whole, whole] if last else whole,
        scratch_shapes=scratch,
        compiler_params=pltpu.CompilerParams(vmem_limit_bytes=40 << 20),
        cost_estimate=pl.CostEstimate(
            flops=16 * 2 * 2 * 2 * terms * modes * 2 * modes * cells,
            bytes_accessed=4 << 20,
            transcendentals=0,
        ),
    )(*operands)


def exchange(values, axis, apart):
    count = lax.axis_size(axis)
    return lax.ppermute(values, axis, [(i, i ^ apart) for i in range(count)])


def local(right_modes, adjoint_modes, conductivity_terms):
    n_term, n_space = lax.axis_size("term"), lax.axis_size("space")
    term_at, space_at = lax.axis_index("term"), lax.axis_index("space")
    pairs = n_term // 2
    z, y = term_at // 2, term_at % 2
    modes, cells = right_modes.shape[1:]
    terms = conductivity_terms.shape[1]

    def after(x, *deps):
        return lax.optimization_barrier((x,) + deps)[0]

    def go(stage, before, halo=None):
        return run_stage(stage, n_term, n_space, conductivity_terms, blocks[: 2 * stage + 2], halo, before)

    which = lax.broadcasted_iota(jnp.int32, (2, 1, 1), 0)
    own = jnp.where(which == 0, right_modes, adjoint_modes)
    half = pairs // 2
    column = {half: exchange(own, "term", 2 * half)}
    blocks = [own, exchange(own, "term", 1)]
    for stage in range(1, half):
        column[stage] = exchange(own, "term", 2 * stage)
    for stage in range(half + 1, pairs):
        column[stage] = exchange(after(own, blocks[1]), "term", 2 * stage)
    value = go(0, None)
    for stage in range(1, half):
        came = after(column[stage], value)
        blocks += [came, exchange(came, "term", 1)]
    came = after(column[half], blocks[2 * half - 1])
    ahead = [came, exchange(came, "term", 1)]
    for stage in range(1, half):
        value = go(stage, value)
    for stage in range(half + 1, pairs):
        came = after(column[stage], value)
        ahead += [came, exchange(came, "term", 1)]
    blocks += ahead

    is_low = term_at < n_term // 2
    wanted = jnp.where(is_low, z, (pairs - 1) ^ z)
    takes_own = (y == 0) == is_low
    rim = blocks[0]
    for j in range(pairs // 2):
        block = jnp.where(takes_own, blocks[2 * j], blocks[2 * j + 1])
        rim = block if j == 0 else jnp.where(wanted == j, block, rim)
    rim_coeff = jnp.where(is_low, conductivity_terms[0], conductivity_terms[-1])
    rim = jnp.concatenate([rim.reshape(2 * modes, cells), rim_coeff], 0)
    route = []
    for s in range(n_space - 1):
        for t in range(n_term):
            low, high = s * n_term + t, (s + 1) * n_term + t
            route.append((high, low) if t < n_term // 2 else (low, high))
    halo = lax.ppermute(rim, ("space", "term"), route)

    for stage in range(half, pairs):
        value = go(stage, value, halo)
    keep, send = value
    total = keep + exchange(send, "space", 1)
    apart = 2
    while apart < n_space:
        bit = space_at // apart % 2
        halves = total.reshape((total.shape[0] // 2, 2) + total.shape[1:])
        send = lax.dynamic_index_in_dim(halves, 1 - bit, 1, keepdims=False)
        keep = lax.dynamic_index_in_dim(halves, bit, 1, keepdims=False)
        total = keep + exchange(send, "space", apart)
        apart *= 2
    return total[0].reshape(terms, -1)


def solution(mesh):
    placed = (
        P(("space", "term"), None, None),
        P(("space", "term"), None, None),
        P("space", "term", None),
    )
    return jax.shard_map(
        local, mesh=mesh, in_specs=placed, out_specs=P("term", "space"), check_vma=False
    )
```

time: 46.6 us -> 39.9 us (0.86)
  Pallas kernels: 17.9 us -> 12.5 us
  waiting for transfers between devices: 12.6 us -> 9.72 us
  starting transfers between devices: 13.3 us -> 15.6 us
  local copies, waits for them, and re-layouts: 1.75 us -> 0.71 us
    pallas_call x4, Pallas kernels: 17.9 us -> 12.5 us  [run_stage(): pl.pallas_call(functools.partial(stage_kernel, stage, first, last, n_term...]
    ppermute x9, waiting for transfers between devices: 12.6 us -> 9.72 us  [exchange(): return lax.ppermute(values, axis, [(i, i ^ apart) for i in range(count)])]
    ppermute x9, starting transfers between devices: 12 us -> 14.3 us  [exchange(): return lax.ppermute(values, axis, [(i, i ^ apart) for i in range(count)])]
    select_n x0 -> x1, other arithmetic: none -> 0.99 us  [local(): own = jnp.where(which == 0, right_modes, adjoint_modes)]
    concatenate x1 -> x0, local copies, waits for them, and re-layouts: 0.84 us -> none  [local(): own = jnp.concatenate([right_modes, adjoint_modes], 0)]
    reshape x1 -> x0, other arithmetic: 0.67 us -> none  [local(): return jnp.transpose(total[0], (1, 0, 2)).reshape(terms, -1)]
  transfers between devices with their start and end apart: 10 -> 10, of which waited for: 4 -> 5; matrix products, arithmetic and copies ran while one was open for 0% -> 0% of each run, Pallas kernels for 26% -> 21%
where the time goes in v2:
time: 39.9 us; the launch traced here: 39.8 us
  starting transfers between devices  15.6 us (39%)
  Pallas kernels  12.5 us (31%)
  waiting for transfers between devices  9.72 us (24%)
  other arithmetic  1.14 us (3%)
  local copies, waits for them, and re-layouts  0.71 us (2%)
    ppermute x9, starting transfers between devices, exchange(): return lax.ppermute(values, axis, [(i, i ^ apart) for i in range(count)])  14.3 us
    pallas_call x4, Pallas kernels, run_stage(): pl.pallas_call(functools.partial(stage_kernel, stage, first, last, n_term...  12.5 us
    ppermute x9, waiting for transfers between devices, exchange(): return lax.ppermute(values, axis, [(i, i ^ apart) for i in range(count)])  9.72 us
    ppermute x1, starting transfers between devices, local(): halo = lax.ppermute(rim, ('space', 'term'), route)  1.29 us
    select_n x1, other arithmetic, local(): own = jnp.where(which == 0, right_modes, adjoint_modes)  0.99 us
  transfers between devices with their start and end apart: 10, of which 5 were waited for; matrix products, arithmetic and copies ran while one was open for 0% of the time, Pallas kernels for 21%

profile of v2, /device:TPU:0, one launch (start us, length us, event | category | flops | bytes accessed | tf_op | source)
XLA Modules:
  0.0 39.8 jit_solution(13487391757977884036)
XLA Ops:
  0.0 0.0 copy-start
  0.0 1.0 %broadcast_select_fusion.refs_1_ = f32[2,64,256]{2,1,0:T(8,128)S(1)} fusion(f32[64,256]{1,0:T(8,128)} %bitcast.12, f32[64,256]{1,0:T(8,128)} %bitcast.14, pred[2]{0:T(512)(128)(4,1)S(1)} %iota_compare_fusion), kind=kLoop, calls=%fused_computation.4 | loop fusion | flops 32768 | bytes 262146 | tf_op jit(solution)/shard_map/jit(_where)/select_n | solution.py:228
  1.0 3.0 %collective-permute-start = (f32[2,64,256]{2,1,0:T(8,128)S(1)}, f32[2,64,256]{2,1,0:T(8,128)S(1)}, u32[]{:S(2)}, u32[]{:S(2)}) collective-permute-start(f32[2,64,256]{2,1,0:T(8,128)S(1)} %broadcast_select_fusion.refs_1_), channel_id=1, source_target_pairs={{0,1},{1,0},{2,3},{3,2},{4,5},{5,4},{6,7},{7,6},{8,9},{9,8},{10,11... | collective-permute-start | bytes 393224 | tf_op jit(solution)/shard_map/ppermute | solution.py:210
  4.0 1.6 %collective-permute-start.1 = (f32[2,64,256]{2,1,0:T(8,128)S(1)}, f32[2,64,256]{2,1,0:T(8,128)S(1)}, u32[]{:S(2)}, u32[]{:S(2)}) collective-permute-start(f32[2,64,256]{2,1,0:T(8,128)S(1)} %broadcast_select_fusion.refs_1_), channel_id=1, source_target_pairs={{0,2},{1,3},{2,0},{3,1},{4,6},{5,7},{6,4},{7,5},{8,10},{9,11},{10,... | collective-permute-start | bytes 393224 | tf_op jit(solution)/shard_map/ppermute | solution.py:210
  5.6 2.6 %collective-permute-start.3 = (f32[2,64,256]{2,1,0:T(8,128)S(1)}, f32[2,64,256]{2,1,0:T(8,128)S(1)}, u32[]{:S(2)}, u32[]{:S(2)}) collective-permute-start(f32[2,64,256]{2,1,0:T(8,128)S(1)} %broadcast_select_fusion.refs_1_), channel_id=1, source_target_pairs={{0,4},{1,5},{2,6},{3,7},{4,0},{5,1},{6,2},{7,3},{8,12},{9,13},{10,... | collective-permute-start | bytes 393224 | tf_op jit(solution)/shard_map/ppermute | solution.py:210
  8.2 0.0 collective-permute-done.refs_2_
  8.2 0.0 copy-done
  8.2 2.9 %shard_map.37.refs_5_ = f32[32,64,128]{2,1,0:T(8,128)S(1)} custom-call(f32[8,32,256]{2,1,0:T(8,128)S(1)} %copy-done, f32[2,64,256]{2,1,0:T(8,128)S(1)} %broadcast_select_fusion.refs_1_, f32[2,64,256]{2,1,0:T(8,128)S(1)} %collective-permute-done.refs_2_), custom_call_target="tpu_custom_call" | custom-call | flops 8589934592 | bytes 4194304 | tf_op jit(solution)/shard_map/pallas_call | solution.py:193
  11.1 0.0 copy-start.1
  11.1 0.0 collective-permute-done.1.refs_3_
  11.1 1.1 %collective-permute-start.2 = (f32[2,64,256]{2,1,0:T(8,128)S(1)}, f32[2,64,256]{2,1,0:T(8,128)S(1)}, u32[]{:S(2)}, u32[]{:S(2)}) collective-permute-start(f32[2,64,256]{2,1,0:T(8,128)S(1)} %collective-permute-done.1.refs_3_), channel_id=1, source_target_pairs={{0,1},{1,0},{2,3},{3,2},{4,5},{5,4},{6,7},{7,6},{8,9},{9,8},{10,11... | collective-permute-start | bytes 393224 | tf_op jit(solution)/shard_map/ppermute | solution.py:210
  12.2 2.9 %collective-permute-start.5 = (f32[2,64,256]{2,1,0:T(8,128)S(1)}, f32[2,64,256]{2,1,0:T(8,128)S(1)}, u32[]{:S(2)}, u32[]{:S(2)}) collective-permute-start(f32[2,64,256]{2,1,0:T(8,128)S(1)} %broadcast_select_fusion.refs_1_), channel_id=1, source_target_pairs={{0,6},{1,7},{2,4},{3,5},{4,2},{5,3},{6,0},{7,1},{8,14},{9,15},{10,... | collective-permute-start | bytes 393224 | tf_op jit(solution)/shard_map/ppermute | solution.py:210
  15.1 1.0 %collective-permute-done.2.refs_4_ = f32[2,64,256]{2,1,0:T(8,128)S(1)} collective-permute-done((f32[2,64,256]{2,1,0:T(8,128)S(1)}, f32[2,64,256]{2,1,0:T(8,128)S(1)}, u32[]{:S(2)}, u32[]{:S(2)}) %collective-permute-start.2) | collective-permute-done | bytes 131104 | tf_op jit(solution)/shard_map/ppermute | solution.py:210
  16.1 0.0 copy-done.2
  16.1 0.0 copy-done.1
  16.1 0.1 select_select_fusion
  16.2 1.3 %collective-permute-start.7 = (f32[160,256]{1,0:T(8,128)S(1)}, f32[160,256]{1,0:T(8,128)S(1)}, u32[]{:S(2)}, u32[]{:S(2)}) collective-permute-start(f32[160,256]{1,0:T(8,128)S(1)} %pad_maximum_fusion), channel_id=1, source_target_pairs={{8,0},{9,1},{10,2},{11,3},{4,12},{5,13},{6,14},{7,15},{16,8},{17,9... | collective-permute-start | bytes 491528 | tf_op jit(solution)/shard_map/ppermute | solution.py:263
  17.5 0.0 collective-permute-done.3.refs_5_
  17.6 1.1 %collective-permute-start.4 = (f32[2,64,256]{2,1,0:T(8,128)S(1)}, f32[2,64,256]{2,1,0:T(8,128)S(1)}, u32[]{:S(2)}, u32[]{:S(2)}) collective-permute-start(f32[2,64,256]{2,1,0:T(8,128)S(1)} %collective-permute-done.3.refs_5_), channel_id=1, source_target_pairs={{0,1},{1,0},{2,3},{3,2},{4,5},{5,4},{6,7},{7,6},{8,9},{9,8},{10,11... | collective-permute-start | bytes 393224 | tf_op jit(solution)/shard_map/ppermute | solution.py:210
  18.7 2.8 %shard_map.38.refs_8_ = f32[32,64,128]{2,1,0:T(8,128)S(1)} custom-call(f32[8,32,256]{2,1,0:T(8,128)S(1)} %copy-done, f32[2,64,256]{2,1,0:T(8,128)S(1)} %broadcast_select_fusion.refs_1_, f32[2,64,256]{2,1,0:T(8,128)S(1)} %collective-permute-done.refs_2_, f32[2,64,256]{2,1,0:T(8,128)S(1)} %collective-permute-done.1.refs_3_, ...), custom_call_target="tpu_custom_call" | custom-call | flops 8589934592 | bytes 4194304 | tf_op jit(solution)/shard_map/pallas_call | solution.py:193
  21.5 0.0 collective-permute-done.5.refs_7_
  21.5 1.0 %collective-permute-start.6 = (f32[2,64,256]{2,1,0:T(8,128)S(1)}, f32[2,64,256]{2,1,0:T(8,128)S(1)}, u32[]{:S(2)}, u32[]{:S(2)}) collective-permute-start(f32[2,64,256]{2,1,0:T(8,128)S(1)} %collective-permute-done.5.refs_7_), channel_id=1, source_target_pairs={{0,1},{1,0},{2,3},{3,2},{4,5},{5,4},{6,7},{7,6},{8,9},{9,8},{10,11... | collective-permute-start | bytes 393224 | tf_op jit(solution)/shard_map/ppermute | solution.py:210
  22.5 1.3 %collective-permute-done.4.refs_6_ = f32[2,64,256]{2,1,0:T(8,128)S(1)} collective-permute-done((f32[2,64,256]{2,1,0:T(8,128)S(1)}, f32[2,64,256]{2,1,0:T(8,128)S(1)}, u32[]{:S(2)}, u32[]{:S(2)}) %collective-permute-start.4) | collective-permute-done | bytes 131104 | tf_op jit(solution)/shard_map/ppermute | solution.py:210
  23.8 0.0 collective-permute-done.7.refs_7_.refs_9_
  23.8 2.8 %shard_map.39.refs_10_ = f32[32,64,128]{2,1,0:T(8,128)S(1)} custom-call(f32[8,32,256]{2,1,0:T(8,128)S(1)} %copy-done, f32[2,64,256]{2,1,0:T(8,128)S(1)} %broadcast_select_fusion.refs_1_, f32[2,64,256]{2,1,0:T(8,128)S(1)} %collective-permute-done.refs_2_, f32[2,64,256]{2,1,0:T(8,128)S(1)} %collective-permute-done.1.refs_3_, ...), custom_call_target="tpu_custom_call" | custom-call | flops 8589934592 | bytes 4194304 | tf_op jit(solution)/shard_map/pallas_call | solution.py:193
  26.7 1.2 %collective-permute-done.6.refs_8_ = f32[2,64,256]{2,1,0:T(8,128)S(1)} collective-permute-done((f32[2,64,256]{2,1,0:T(8,128)S(1)}, f32[2,64,256]{2,1,0:T(8,128)S(1)}, u32[]{:S(2)}, u32[]{:S(2)}) %collective-permute-start.6) | collective-permute-done | bytes 131104 | tf_op jit(solution)/shard_map/ppermute | solution.py:210
  27.8 4.0 %shard_map.40 = (f32[2,32,8,128]{3,2,1,0:T(8,128)S(1)}, f32[2,32,8,128]{3,2,1,0:T(8,128)S(1)}) custom-call(f32[8,32,256]{2,1,0:T(8,128)S(1)} %copy-done, f32[2,64,256]{2,1,0:T(8,128)S(1)} %broadcast_select_fusion.refs_1_, f32[2,64,256]{2,1,0:T(8,128)S(1)} %collective-permute-done.refs_2_, f32[2,64,256]{2,1,0:T(8,128)S(1)} %collective-permute-done.1.refs_3_, ...), custom_call_target="tpu_custom_call" | custom-call | flops 8589934592 | bytes 4194304 | tf_op jit(solution)/shard_map/pallas_call | solution.py:193
  31.8 0.1 collective-permute-start.8
  31.9 1.5 %collective-permute-done.8 = f32[2,32,8,128]{3,2,1,0:T(8,128)S(1)} collective-permute-done((f32[2,32,8,128]{3,2,1,0:T(8,128)S(1)}, f32[2,32,8,128]{3,2,1,0:T(8,128)S(1)}, u32[]{:S(2)}, u32[]{:S(2)}) %collective-permute-start.8) | collective-permute-done | bytes 262176 | tf_op jit(solution)/shard_map/ppermute | solution.py:210
  33.5 0.8 %collective-permute-start.9 = (f32[1,32,8,128]{3,2,1,0:T(8,128)S(1)}, f32[1,32,8,128]{3,2,1,0:T(8,128)S(1)}, u32[]{:S(2)}, u32[]{:S(2)}) collective-permute-start(f32[1,32,8,128]{3,2,1,0:T(8,128)S(1)} %constant_dynamic-slice_fusion), channel_id=1, source_target_pairs={{0,16},{8,24},{16,0},{24,8},{1,17},{9,25},{17,1},{25,9},{2,18},{10... | collective-permute-start | bytes 393224 | tf_op jit(solution)/shard_map/ppermute | solution.py:210
  34.3 4.8 %collective-permute-done.9 = f32[1,32,8,128]{3,2,1,0:T(8,128)S(1)} collective-permute-done((f32[1,32,8,128]{3,2,1,0:T(8,128)S(1)}, f32[1,32,8,128]{3,2,1,0:T(8,128)S(1)}, u32[]{:S(2)}, u32[]{:S(2)}) %collective-permute-start.9) | collective-permute-done | bytes 131104 | tf_op jit(solution)/shard_map/ppermute | solution.py:210
  39.1 0.7 %copy.6 = f32[4,8,8,128]{3,1,2,0:T(8,128)} copy(f32[4,8,8,128]{3,2,1,0:T(8,128)S(1)} %bitcast.10) | data formatting | bytes 262144
  (7 shorter events, 0.1 us)
Async XLA Ops:
  0.0 8.2 %copy-start = (f32[8,32,256]{2,1,0:T(8,128)S(1)}, f32[8,32,256]{2,1,0:T(8,128)}, u32[]{:S(2)}) copy-start(f32[8,32,256]{2,1,0:T(8,128)} %refs_0_.7) | copy-start | bytes 786436
  1.0 7.2 %collective-permute-start = (f32[2,64,256]{2,1,0:T(8,128)S(1)}, f32[2,64,256]{2,1,0:T(8,128)S(1)}, u32[]{:S(2)}, u32[]{:S(2)}) collective-permute-start(f32[2,64,256]{2,1,0:T(8,128)S(1)} %broadcast_select_fusion.refs_1_), channel_id=1, source_target_pairs={{0,1},{1,0},{2,3},{3,2},{4,5},{5,4},{6,7},{7,6},{8,9},{9,8},{10,11... | collective-permute-start | bytes 393224 | tf_op jit(solution)/shard_map/ppermute | solution.py:210
  4.0 7.0 %collective-permute-start.1 = (f32[2,64,256]{2,1,0:T(8,128)S(1)}, f32[2,64,256]{2,1,0:T(8,128)S(1)}, u32[]{:S(2)}, u32[]{:S(2)}) collective-permute-start(f32[2,64,256]{2,1,0:T(8,128)S(1)} %broadcast_select_fusion.refs_1_), channel_id=1, source_target_pairs={{0,2},{1,3},{2,0},{3,1},{4,6},{5,7},{6,4},{7,5},{8,10},{9,11},{10,... | collective-permute-start | bytes 393224 | tf_op jit(solution)/shard_map/ppermute | solution.py:210
  5.6 11.9 %collective-permute-start.3 = (f32[2,64,256]{2,1,0:T(8,128)S(1)}, f32[2,64,256]{2,1,0:T(8,128)S(1)}, u32[]{:S(2)}, u32[]{:S(2)}) collective-permute-start(f32[2,64,256]{2,1,0:T(8,128)S(1)} %broadcast_select_fusion.refs_1_), channel_id=1, source_target_pairs={{0,4},{1,5},{2,6},{3,7},{4,0},{5,1},{6,2},{7,3},{8,12},{9,13},{10,... | collective-permute-start | bytes 393224 | tf_op jit(solution)/shard_map/ppermute | solution.py:210
  8.2 7.9 %copy-start.2 = (f32[1,64,256]{2,1,0:T(8,128)S(1)}, f32[1,64,256]{2,1,0:T(8,128)}, u32[]{:S(2)}) copy-start(f32[1,64,256]{2,1,0:T(8,128)} %param.3) | copy-start | bytes 196612
  11.1 5.1 %copy-start.1 = (f32[1,64,256]{2,1,0:T(8,128)S(1)}, f32[1,64,256]{2,1,0:T(8,128)}, u32[]{:S(2)}) copy-start(f32[1,64,256]{2,1,0:T(8,128)} %param.4) | copy-start | bytes 196612
  11.1 5.0 %collective-permute-start.2 = (f32[2,64,256]{2,1,0:T(8,128)S(1)}, f32[2,64,256]{2,1,0:T(8,128)S(1)}, u32[]{:S(2)}, u32[]{:S(2)}) collective-permute-start(f32[2,64,256]{2,1,0:T(8,128)S(1)} %collective-permute-done.1.refs_3_), channel_id=1, source_target_pairs={{0,1},{1,0},{2,3},{3,2},{4,5},{5,4},{6,7},{7,6},{8,9},{9,8},{10,11... | collective-permute-start | bytes 393224 | tf_op jit(solution)/shard_map/ppermute | solution.py:210
  12.2 9.3 %collective-permute-start.5 = (f32[2,64,256]{2,1,0:T(8,128)S(1)}, f32[2,64,256]{2,1,0:T(8,128)S(1)}, u32[]{:S(2)}, u32[]{:S(2)}) collective-permute-start(f32[2,64,256]{2,1,0:T(8,128)S(1)} %broadcast_select_fusion.refs_1_), channel_id=1, source_target_pairs={{0,6},{1,7},{2,4},{3,5},{4,2},{5,3},{6,0},{7,1},{8,14},{9,15},{10,... | collective-permute-start | bytes 393224 | tf_op jit(solution)/shard_map/ppermute | solution.py:210
  16.2 7.6 %collective-permute-start.7 = (f32[160,256]{1,0:T(8,128)S(1)}, f32[160,256]{1,0:T(8,128)S(1)}, u32[]{:S(2)}, u32[]{:S(2)}) collective-permute-start(f32[160,256]{1,0:T(8,128)S(1)} %pad_maximum_fusion), channel_id=1, source_target_pairs={{8,0},{9,1},{10,2},{11,3},{4,12},{5,13},{6,14},{7,15},{16,8},{17,9... | collective-permute-start | bytes 491528 | tf_op jit(solution)/shard_map/ppermute | solution.py:263
  17.6 6.3 %collective-permute-start.4 = (f32[2,64,256]{2,1,0:T(8,128)S(1)}, f32[2,64,256]{2,1,0:T(8,128)S(1)}, u32[]{:S(2)}, u32[]{:S(2)}) collective-permute-start(f32[2,64,256]{2,1,0:T(8,128)S(1)} %collective-permute-done.3.refs_5_), channel_id=1, source_target_pairs={{0,1},{1,0},{2,3},{3,2},{4,5},{5,4},{6,7},{7,6},{8,9},{9,8},{10,11... | collective-permute-start | bytes 393224 | tf_op jit(solution)/shard_map/ppermute | solution.py:210
  21.5 6.3 %collective-permute-start.6 = (f32[2,64,256]{2,1,0:T(8,128)S(1)}, f32[2,64,256]{2,1,0:T(8,128)S(1)}, u32[]{:S(2)}, u32[]{:S(2)}) collective-permute-start(f32[2,64,256]{2,1,0:T(8,128)S(1)} %collective-permute-done.5.refs_7_), channel_id=1, source_target_pairs={{0,1},{1,0},{2,3},{3,2},{4,5},{5,4},{6,7},{7,6},{8,9},{9,8},{10,11... | collective-permute-start | bytes 393224 | tf_op jit(solution)/shard_map/ppermute | solution.py:210
  31.8 1.6 %collective-permute-start.8 = (f32[2,32,8,128]{3,2,1,0:T(8,128)S(1)}, f32[2,32,8,128]{3,2,1,0:T(8,128)S(1)}, u32[]{:S(2)}, u32[]{:S(2)}) collective-permute-start(f32[2,32,8,128]{3,2,1,0:T(8,128)S(1)} %get-tuple-element.16), channel_id=1, source_target_pairs={{0,8},{8,0},{16,24},{24,16},{1,9},{9,1},{17,25},{25,17},{2,10},{10... | collective-permute-start | bytes 786440 | tf_op jit(solution)/shard_map/ppermute | solution.py:210
  33.5 5.6 %collective-permute-start.9 = (f32[1,32,8,128]{3,2,1,0:T(8,128)S(1)}, f32[1,32,8,128]{3,2,1,0:T(8,128)S(1)}, u32[]{:S(2)}, u32[]{:S(2)}) collective-permute-start(f32[1,32,8,128]{3,2,1,0:T(8,128)S(1)} %constant_dynamic-slice_fusion), channel_id=1, source_target_pairs={{0,16},{8,24},{16,0},{24,8},{1,17},{9,25},{17,1},{25,9},{2,18},{10... | collective-permute-start | bytes 393224 | tf_op jit(solution)/shard_map/ppermute | solution.py:210

commit v3 on v2

--- a/solution.py
+++ b/solution.py
@@ -125,8 +125,10 @@
             def _(slot=count):
                 here = own_ref if parity == upward else other_ref
                 if far:
-                    halo = halo_ref.at[: 2 * modes].reshape(2, modes, cells)
-                    edge(slot, here, halo, 0.5 * (k_ref[plane] + halo_ref[2 * modes :]))
+                    inner = space_at != (n_space - 1 if upward else 0)
+                    came = jnp.where(inner, halo_ref[...], 0.0)
+                    halo = (came[:modes], came[modes : 2 * modes])
+                    edge(slot, here, halo, 0.5 * (k_ref[plane] + came[2 * modes :]))
                 else:
                     edge(slot, here, None, 0.5 * k_ref[plane])
 
@@ -198,7 +200,7 @@
         scratch_shapes=scratch,
         compiler_params=pltpu.CompilerParams(vmem_limit_bytes=40 << 20),
         cost_estimate=pl.CostEstimate(
-            flops=16 * 2 * 2 * 2 * terms * modes * 2 * modes * cells,
+            flops=1 * 2 * 2 * 2 * terms * modes * 2 * modes * cells,
             bytes_accessed=4 << 20,
             transcendentals=0,
         ),
@@ -227,18 +229,18 @@
     which = lax.broadcasted_iota(jnp.int32, (2, 1, 1), 0)
     own = jnp.where(which == 0, right_modes, adjoint_modes)
     half = pairs // 2
-    column = {half: exchange(own, "term", 2 * half)}
+    column = {}
+    column[half] = exchange(own, "term", 2 * half)
+    for stage in range(1, half):
+        column[stage] = exchange(own, "term", 2 * stage)
+        column[half + stage] = exchange(column[half], "term", 2 * stage)
     blocks = [own, exchange(own, "term", 1)]
     for stage in range(1, half):
-        column[stage] = exchange(own, "term", 2 * stage)
-    for stage in range(half + 1, pairs):
-        column[stage] = exchange(after(own, blocks[1]), "term", 2 * stage)
+        blocks += [column[stage], exchange(column[stage], "term", 1)]
+    ahead = [column[half], exchange(column[half], "term", 1)]
     value = go(0, None)
-    for stage in range(1, half):
-        came = after(column[stage], value)
-        blocks += [came, exchange(came, "term", 1)]
-    came = after(column[half], blocks[2 * half - 1])
-    ahead = [came, exchange(came, "term", 1)]
+    first_value = value
+    blocks = blocks[:2] + [after(x, value) for x in blocks[2:]]
     for stage in range(1, half):
         value = go(stage, value)
     for stage in range(half + 1, pairs):
@@ -249,16 +251,16 @@
     is_low = term_at < n_term // 2
     wanted = jnp.where(is_low, z, (pairs - 1) ^ z)
     takes_own = (y == 0) == is_low
-    rim = blocks[0]
+    rim = after(blocks[0], first_value)
     for j in range(pairs // 2):
         block = jnp.where(takes_own, blocks[2 * j], blocks[2 * j + 1])
         rim = block if j == 0 else jnp.where(wanted == j, block, rim)
     rim_coeff = jnp.where(is_low, conductivity_terms[0], conductivity_terms[-1])
     rim = jnp.concatenate([rim.reshape(2 * modes, cells), rim_coeff], 0)
     route = []
-    for s in range(n_space - 1):
+    for s in range(n_space):
         for t in range(n_term):
-            low, high = s * n_term + t, (s + 1) * n_term + t
+            low, high = s * n_term + t, (s + 1) % n_space * n_term + t
             route.append((high, low) if t < n_term // 2 else (low, high))
     halo = lax.ppermute(rim, ("space", "term"), route)
 

time: 39.9 us -> 36.5 us (0.915)
  starting transfers between devices: 15.6 us -> 13.8 us
  waiting for transfers between devices: 9.72 us -> 8.06 us
    ppermute x9, waiting for transfers between devices: 9.72 us -> 8.05 us  [exchange(): return lax.ppermute(values, axis, [(i, i ^ apart) for i in range(count)])]
    ppermute x1, starting transfers between devices: 1.29 us -> 0.22 us  [local(): halo = lax.ppermute(rim, ('space', 'term'), route)]
    ppermute x9, starting transfers between devices: 14.3 us -> 13.6 us  [exchange(): return lax.ppermute(values, axis, [(i, i ^ apart) for i in range(count)])]
  transfers between devices with their start and end apart: 10 -> 10, of which waited for: 5 -> 6; matrix products, arithmetic and copies ran while one was open for 0% -> 0% of each run, Pallas kernels for 21% -> 23%
where the time goes in v3:
time: 36.5 us; the launch traced here: 36.4 us
  starting transfers between devices  13.8 us (38%)
  Pallas kernels  12.5 us (34%)
  waiting for transfers between devices  8.06 us (22%)
  other arithmetic  1.15 us (3%)
  local copies, waits for them, and re-layouts  0.71 us (2%)
    ppermute x9, starting transfers between devices, exchange(): return lax.ppermute(values, axis, [(i, i ^ apart) for i in range(count)])  13.6 us
    pallas_call x4, Pallas kernels, run_stage(): pl.pallas_call(functools.partial(stage_kernel, stage, first, last, n_term...  12.5 us
    ppermute x9, waiting for transfers between devices, exchange(): return lax.ppermute(values, axis, [(i, i ^ apart) for i in range(count)])  8.05 us
    select_n x1, other arithmetic, local(): own = jnp.where(which == 0, right_modes, adjoint_modes)  0.99 us
  transfers between devices with their start and end apart: 10, of which 6 were waited for; matrix products, arithmetic and copies ran while one was open for 0% of the time, Pallas kernels for 23%

profile of v3, /device:TPU:0, one launch (start us, length us, event | category | flops | bytes accessed | tf_op | source)
XLA Modules:
  0.0 36.4 jit_solution(10424025076086091090)
XLA Ops:
  0.0 1.0 %broadcast_select_fusion.refs_1_ = f32[2,64,256]{2,1,0:T(8,128)S(1)} fusion(f32[64,256]{1,0:T(8,128)} %bitcast.12, f32[64,256]{1,0:T(8,128)} %bitcast.14, pred[2]{0:T(512)(128)(4,1)S(1)} %iota_compare_fusion), kind=kLoop, calls=%fused_computation.4 | loop fusion | flops 32768 | bytes 262146 | tf_op jit(solution)/shard_map/jit(_where)/select_n | solution.py:230
  1.0 3.1 %collective-permute-start.1 = (f32[2,64,256]{2,1,0:T(8,128)S(1)}, f32[2,64,256]{2,1,0:T(8,128)S(1)}, u32[]{:S(2)}, u32[]{:S(2)}) collective-permute-start(f32[2,64,256]{2,1,0:T(8,128)S(1)} %broadcast_select_fusion.refs_1_), channel_id=1, source_target_pairs={{0,2},{1,3},{2,0},{3,1},{4,6},{5,7},{6,4},{7,5},{8,10},{9,11},{10,... | collective-permute-start | bytes 393224 | tf_op jit(solution)/shard_map/ppermute | solution.py:212
  4.1 1.5 %collective-permute-start = (f32[2,64,256]{2,1,0:T(8,128)S(1)}, f32[2,64,256]{2,1,0:T(8,128)S(1)}, u32[]{:S(2)}, u32[]{:S(2)}) collective-permute-start(f32[2,64,256]{2,1,0:T(8,128)S(1)} %broadcast_select_fusion.refs_1_), channel_id=1, source_target_pairs={{0,1},{1,0},{2,3},{3,2},{4,5},{5,4},{6,7},{7,6},{8,9},{9,8},{10,11... | collective-permute-start | bytes 393224 | tf_op jit(solution)/shard_map/ppermute | solution.py:212
  5.6 2.6 %collective-permute-start.3 = (f32[2,64,256]{2,1,0:T(8,128)S(1)}, f32[2,64,256]{2,1,0:T(8,128)S(1)}, u32[]{:S(2)}, u32[]{:S(2)}) collective-permute-start(f32[2,64,256]{2,1,0:T(8,128)S(1)} %broadcast_select_fusion.refs_1_), channel_id=1, source_target_pairs={{0,4},{1,5},{2,6},{3,7},{4,0},{5,1},{6,2},{7,3},{8,12},{9,13},{10,... | collective-permute-start | bytes 393224 | tf_op jit(solution)/shard_map/ppermute | solution.py:212
  8.2 0.0 collective-permute-done.1.refs_3_
  8.2 2.6 %collective-permute-start.2 = (f32[2,64,256]{2,1,0:T(8,128)S(1)}, f32[2,64,256]{2,1,0:T(8,128)S(1)}, u32[]{:S(2)}, u32[]{:S(2)}) collective-permute-start(f32[2,64,256]{2,1,0:T(8,128)S(1)} %collective-permute-done.1.refs_3_), channel_id=1, source_target_pairs={{0,1},{1,0},{2,3},{3,2},{4,5},{5,4},{6,7},{7,6},{8,9},{9,8},{10,11... | collective-permute-start | bytes 393224 | tf_op jit(solution)/shard_map/ppermute | solution.py:212
  10.8 0.0 copy-done
  10.8 0.0 copy-start.1
  10.8 0.0 copy-start.2
  10.8 0.0 collective-permute-done.refs_2_
  10.8 2.9 %shard_map.37.refs_5_ = f32[32,64,128]{2,1,0:T(8,128)S(1)} custom-call(f32[8,32,256]{2,1,0:T(8,128)S(1)} %copy-done, f32[2,64,256]{2,1,0:T(8,128)S(1)} %broadcast_select_fusion.refs_1_, f32[2,64,256]{2,1,0:T(8,128)S(1)} %collective-permute-done.refs_2_), custom_call_target="tpu_custom_call" | custom-call | flops 536870912 | bytes 4194304 | tf_op jit(solution)/shard_map/pallas_call | solution.py:195
  13.7 0.3 collective-permute-done.3.refs_5_
  14.0 0.0 collective-permute-start.5
  14.0 0.0 collective-permute-done.2.refs_4_
  14.0 0.0 copy-done.1
  14.0 0.0 copy-done.2
  14.0 0.1 select_select_fusion
  14.1 0.2 collective-permute-start.7
  14.4 1.6 %collective-permute-start.4 = (f32[2,64,256]{2,1,0:T(8,128)S(1)}, f32[2,64,256]{2,1,0:T(8,128)S(1)}, u32[]{:S(2)}, u32[]{:S(2)}) collective-permute-start(f32[2,64,256]{2,1,0:T(8,128)S(1)} %collective-permute-done.3.refs_5_), channel_id=1, source_target_pairs={{0,1},{1,0},{2,3},{3,2},{4,5},{5,4},{6,7},{7,6},{8,9},{9,8},{10,11... | collective-permute-start | bytes 393224 | tf_op jit(solution)/shard_map/ppermute | solution.py:212
  16.0 2.8 %shard_map.38.refs_8_ = f32[32,64,128]{2,1,0:T(8,128)S(1)} custom-call(f32[8,32,256]{2,1,0:T(8,128)S(1)} %copy-done, f32[2,64,256]{2,1,0:T(8,128)S(1)} %broadcast_select_fusion.refs_1_, f32[2,64,256]{2,1,0:T(8,128)S(1)} %collective-permute-done.refs_2_, f32[2,64,256]{2,1,0:T(8,128)S(1)} %collective-permute-done.1.refs_3_, ...), custom_call_target="tpu_custom_call" | custom-call | flops 536870912 | bytes 4194304 | tf_op jit(solution)/shard_map/pallas_call | solution.py:195
  18.8 0.2 collective-permute-done.5.refs_7_
  19.0 0.6 %collective-permute-start.6 = (f32[2,64,256]{2,1,0:T(8,128)S(1)}, f32[2,64,256]{2,1,0:T(8,128)S(1)}, u32[]{:S(2)}, u32[]{:S(2)}) collective-permute-start(f32[2,64,256]{2,1,0:T(8,128)S(1)} %collective-permute-done.5.refs_7_), channel_id=1, source_target_pairs={{0,1},{1,0},{2,3},{3,2},{4,5},{5,4},{6,7},{7,6},{8,9},{9,8},{10,11... | collective-permute-start | bytes 393224 | tf_op jit(solution)/shard_map/ppermute | solution.py:212
  19.6 0.5 %collective-permute-done.4.refs_6_ = f32[2,64,256]{2,1,0:T(8,128)S(1)} collective-permute-done((f32[2,64,256]{2,1,0:T(8,128)S(1)}, f32[2,64,256]{2,1,0:T(8,128)S(1)}, u32[]{:S(2)}, u32[]{:S(2)}) %collective-permute-start.4) | collective-permute-done | bytes 131104 | tf_op jit(solution)/shard_map/ppermute | solution.py:212
  20.1 0.0 collective-permute-done.7.refs_7_.refs_9_
  20.1 2.8 %shard_map.39.refs_10_ = f32[32,64,128]{2,1,0:T(8,128)S(1)} custom-call(f32[8,32,256]{2,1,0:T(8,128)S(1)} %copy-done, f32[2,64,256]{2,1,0:T(8,128)S(1)} %broadcast_select_fusion.refs_1_, f32[2,64,256]{2,1,0:T(8,128)S(1)} %collective-permute-done.refs_2_, f32[2,64,256]{2,1,0:T(8,128)S(1)} %collective-permute-done.1.refs_3_, ...), custom_call_target="tpu_custom_call" | custom-call | flops 536870912 | bytes 4194304 | tf_op jit(solution)/shard_map/pallas_call | solution.py:195
  23.0 1.5 %collective-permute-done.6.refs_8_ = f32[2,64,256]{2,1,0:T(8,128)S(1)} collective-permute-done((f32[2,64,256]{2,1,0:T(8,128)S(1)}, f32[2,64,256]{2,1,0:T(8,128)S(1)}, u32[]{:S(2)}, u32[]{:S(2)}) %collective-permute-start.6) | collective-permute-done | bytes 131104 | tf_op jit(solution)/shard_map/ppermute | solution.py:212
  24.4 4.0 %shard_map.40 = (f32[2,32,8,128]{3,2,1,0:T(8,128)S(1)}, f32[2,32,8,128]{3,2,1,0:T(8,128)S(1)}) custom-call(f32[8,32,256]{2,1,0:T(8,128)S(1)} %copy-done, f32[2,64,256]{2,1,0:T(8,128)S(1)} %broadcast_select_fusion.refs_1_, f32[2,64,256]{2,1,0:T(8,128)S(1)} %collective-permute-done.refs_2_, f32[2,64,256]{2,1,0:T(8,128)S(1)} %collective-permute-done.1.refs_3_, ...), custom_call_target="tpu_custom_call" | custom-call | flops 536870912 | bytes 4194304 | tf_op jit(solution)/shard_map/pallas_call | solution.py:195
  28.4 0.1 collective-permute-start.8
  28.5 1.5 %collective-permute-done.8 = f32[2,32,8,128]{3,2,1,0:T(8,128)S(1)} collective-permute-done((f32[2,32,8,128]{3,2,1,0:T(8,128)S(1)}, f32[2,32,8,128]{3,2,1,0:T(8,128)S(1)}, u32[]{:S(2)}, u32[]{:S(2)}) %collective-permute-start.8) | collective-permute-done | bytes 262176 | tf_op jit(solution)/shard_map/ppermute | solution.py:212
  30.1 1.6 %collective-permute-start.9 = (f32[1,32,8,128]{3,2,1,0:T(8,128)S(1)}, f32[1,32,8,128]{3,2,1,0:T(8,128)S(1)}, u32[]{:S(2)}, u32[]{:S(2)}) collective-permute-start(f32[1,32,8,128]{3,2,1,0:T(8,128)S(1)} %constant_dynamic-slice_fusion), channel_id=1, source_target_pairs={{0,16},{8,24},{16,0},{24,8},{1,17},{9,25},{17,1},{25,9},{2,18},{10... | collective-permute-start | bytes 393224 | tf_op jit(solution)/shard_map/ppermute | solution.py:212
  31.6 4.0 %collective-permute-done.9 = f32[1,32,8,128]{3,2,1,0:T(8,128)S(1)} collective-permute-done((f32[1,32,8,128]{3,2,1,0:T(8,128)S(1)}, f32[1,32,8,128]{3,2,1,0:T(8,128)S(1)}, u32[]{:S(2)}, u32[]{:S(2)}) %collective-permute-start.9) | collective-permute-done | bytes 131104 | tf_op jit(solution)/shard_map/ppermute | solution.py:212
  35.7 0.7 %copy.6 = f32[4,8,8,128]{3,1,2,0:T(8,128)} copy(f32[4,8,8,128]{3,2,1,0:T(8,128)S(1)} %bitcast.10) | data formatting | bytes 262144
  (7 shorter events, 0.1 us)
Async XLA Ops:
  0.0 10.8 %copy-start = (f32[8,32,256]{2,1,0:T(8,128)S(1)}, f32[8,32,256]{2,1,0:T(8,128)}, u32[]{:S(2)}) copy-start(f32[8,32,256]{2,1,0:T(8,128)} %refs_0_.7) | copy-start | bytes 786436
  1.0 7.2 %collective-permute-start.1 = (f32[2,64,256]{2,1,0:T(8,128)S(1)}, f32[2,64,256]{2,1,0:T(8,128)S(1)}, u32[]{:S(2)}, u32[]{:S(2)}) collective-permute-start(f32[2,64,256]{2,1,0:T(8,128)S(1)} %broadcast_select_fusion.refs_1_), channel_id=1, source_target_pairs={{0,2},{1,3},{2,0},{3,1},{4,6},{5,7},{6,4},{7,5},{8,10},{9,11},{10,... | collective-permute-start | bytes 393224 | tf_op jit(solution)/shard_map/ppermute | solution.py:212
  4.1 6.7 %collective-permute-start = (f32[2,64,256]{2,1,0:T(8,128)S(1)}, f32[2,64,256]{2,1,0:T(8,128)S(1)}, u32[]{:S(2)}, u32[]{:S(2)}) collective-permute-start(f32[2,64,256]{2,1,0:T(8,128)S(1)} %broadcast_select_fusion.refs_1_), channel_id=1, source_target_pairs={{0,1},{1,0},{2,3},{3,2},{4,5},{5,4},{6,7},{7,6},{8,9},{9,8},{10,11... | collective-permute-start | bytes 393224 | tf_op jit(solution)/shard_map/ppermute | solution.py:212
  5.6 8.4 %collective-permute-start.3 = (f32[2,64,256]{2,1,0:T(8,128)S(1)}, f32[2,64,256]{2,1,0:T(8,128)S(1)}, u32[]{:S(2)}, u32[]{:S(2)}) collective-permute-start(f32[2,64,256]{2,1,0:T(8,128)S(1)} %broadcast_select_fusion.refs_1_), channel_id=1, source_target_pairs={{0,4},{1,5},{2,6},{3,7},{4,0},{5,1},{6,2},{7,3},{8,12},{9,13},{10,... | collective-permute-start | bytes 393224 | tf_op jit(solution)/shard_map/ppermute | solution.py:212
  8.2 5.8 %collective-permute-start.2 = (f32[2,64,256]{2,1,0:T(8,128)S(1)}, f32[2,64,256]{2,1,0:T(8,128)S(1)}, u32[]{:S(2)}, u32[]{:S(2)}) collective-permute-start(f32[2,64,256]{2,1,0:T(8,128)S(1)} %collective-permute-done.1.refs_3_), channel_id=1, source_target_pairs={{0,1},{1,0},{2,3},{3,2},{4,5},{5,4},{6,7},{7,6},{8,9},{9,8},{10,11... | collective-permute-start | bytes 393224 | tf_op jit(solution)/shard_map/ppermute | solution.py:212
  10.8 3.2 %copy-start.1 = (f32[1,64,256]{2,1,0:T(8,128)S(1)}, f32[1,64,256]{2,1,0:T(8,128)}, u32[]{:S(2)}) copy-start(f32[1,64,256]{2,1,0:T(8,128)} %param.4) | copy-start | bytes 196612
  10.8 3.2 %copy-start.2 = (f32[1,64,256]{2,1,0:T(8,128)S(1)}, f32[1,64,256]{2,1,0:T(8,128)}, u32[]{:S(2)}) copy-start(f32[1,64,256]{2,1,0:T(8,128)} %param.3) | copy-start | bytes 196612
  14.0 5.0 %collective-permute-start.5 = (f32[2,64,256]{2,1,0:T(8,128)S(1)}, f32[2,64,256]{2,1,0:T(8,128)S(1)}, u32[]{:S(2)}, u32[]{:S(2)}) collective-permute-start(f32[2,64,256]{2,1,0:T(8,128)S(1)} %collective-permute-done.3.refs_5_), channel_id=1, source_target_pairs={{0,2},{1,3},{2,0},{3,1},{4,6},{5,7},{6,4},{7,5},{8,10},{9,11},{10,... | collective-permute-start | bytes 393224 | tf_op jit(solution)/shard_map/ppermute | solution.py:212
  14.1 6.0 %collective-permute-start.7 = (f32[160,256]{1,0:T(8,128)S(1)}, f32[160,256]{1,0:T(8,128)S(1)}, u32[]{:S(2)}, u32[]{:S(2)}) collective-permute-start(f32[160,256]{1,0:T(8,128)S(1)} %pad_maximum_fusion), channel_id=1, source_target_pairs={{8,0},{9,1},{10,2},{11,3},{4,12},{5,13},{6,14},{7,15},{16,8},{17,9... | collective-permute-start | bytes 491528 | tf_op jit(solution)/shard_map/ppermute | solution.py:265
  14.4 5.7 %collective-permute-start.4 = (f32[2,64,256]{2,1,0:T(8,128)S(1)}, f32[2,64,256]{2,1,0:T(8,128)S(1)}, u32[]{:S(2)}, u32[]{:S(2)}) collective-permute-start(f32[2,64,256]{2,1,0:T(8,128)S(1)} %collective-permute-done.3.refs_5_), channel_id=1, source_target_pairs={{0,1},{1,0},{2,3},{3,2},{4,5},{5,4},{6,7},{7,6},{8,9},{9,8},{10,11... | collective-permute-start | bytes 393224 | tf_op jit(solution)/shard_map/ppermute | solution.py:212
  19.0 5.5 %collective-permute-start.6 = (f32[2,64,256]{2,1,0:T(8,128)S(1)}, f32[2,64,256]{2,1,0:T(8,128)S(1)}, u32[]{:S(2)}, u32[]{:S(2)}) collective-permute-start(f32[2,64,256]{2,1,0:T(8,128)S(1)} %collective-permute-done.5.refs_7_), channel_id=1, source_target_pairs={{0,1},{1,0},{2,3},{3,2},{4,5},{5,4},{6,7},{7,6},{8,9},{9,8},{10,11... | collective-permute-start | bytes 393224 | tf_op jit(solution)/shard_map/ppermute | solution.py:212
  28.4 1.6 %collective-permute-start.8 = (f32[2,32,8,128]{3,2,1,0:T(8,128)S(1)}, f32[2,32,8,128]{3,2,1,0:T(8,128)S(1)}, u32[]{:S(2)}, u32[]{:S(2)}) collective-permute-start(f32[2,32,8,128]{3,2,1,0:T(8,128)S(1)} %get-tuple-element.14), channel_id=1, source_target_pairs={{0,8},{8,0},{16,24},{24,16},{1,9},{9,1},{17,25},{25,17},{2,10},{10... | collective-permute-start | bytes 786440 | tf_op jit(solution)/shard_map/ppermute | solution.py:212
  30.1 5.6 %collective-permute-start.9 = (f32[1,32,8,128]{3,2,1,0:T(8,128)S(1)}, f32[1,32,8,128]{3,2,1,0:T(8,128)S(1)}, u32[]{:S(2)}, u32[]{:S(2)}) collective-permute-start(f32[1,32,8,128]{3,2,1,0:T(8,128)S(1)} %constant_dynamic-slice_fusion), channel_id=1, source_target_pairs={{0,16},{8,24},{16,0},{24,8},{1,17},{9,25},{17,1},{25,9},{2,18},{10... | collective-permute-start | bytes 393224 | tf_op jit(solution)/shard_map/ppermute | solution.py:212

commit v4 on v3

v4 whole, which is shorter than its diff:
```python
import functools

import jax
import jax.numpy as jnp
from jax import lax
from jax.experimental import pallas as pl
from jax.experimental.pallas import tpu as pltpu
from jax.sharding import PartitionSpec as P

GY = 32
GROUP = 16
OFFSETS = (GY, -GY, 1, -1)
NT = (((1,), (1,)), ((), ()))
F32 = jnp.float32
BF16 = jnp.bfloat16


def shifted(values, offset):
    width = values.shape[-1]
    lane = lax.broadcasted_iota(jnp.int32, values.shape, values.ndim - 1)
    moved = pltpu.roll(values, (-offset) % width, values.ndim - 1)
    if offset == GY:
        keep = lane < width - GY
    elif offset == -GY:
        keep = lane >= GY
    elif offset == 1:
        keep = lane % GY != GY - 1
    else:
        keep = lane % GY != 0
    return jnp.where(keep, moved, 0.0)


def split(values):
    high = values.astype(BF16)
    return high, (values - high.astype(F32)).astype(BF16)


def pair_kernel(stage, n_term, n_space, first, extra, *refs):
    pairs = n_term // 2
    far = stage >= pairs // 2
    k_ref = refs[0]
    count = 2 * stage + 2 + extra
    blocks = refs[1 : 1 + count]
    rest = list(refs[1 + count :])
    halo_ref = rest.pop(0) if far else None
    before_ref = None if first else rest.pop(0)
    acc_ref, da_ref, kb_ref, w_ref, dz_ref, kz_ref, wz_ref = rest
    modes, cells = blocks[0].shape[1:]
    terms = k_ref.shape[1]
    term_at = lax.axis_index("term")
    z, y = term_at // 2, term_at % 2
    w = z ^ stage
    own_ref, other_ref = blocks[2 * stage], blocks[2 * stage + 1]
    linked = 1 if stage == 1 else 0 if stage == 0 else 1 + extra if pairs == 4 else 2 + extra

    def weights(slot, values):
        both = jnp.concatenate(split(values), 0)
        w_ref[slot] = jnp.concatenate([both, both], 1)

    in_plane = [(own_ref, 2 * w + y), (other_ref, 2 * w + 1 - y)]
    if extra:
        in_plane.append((blocks[-1], 2 * (z ^ (pairs - 1)) + y))
    for m, (ref, plane) in enumerate(in_plane):
        a, k = ref[1], k_ref[plane]
        for d, offset in enumerate(OFFSETS):
            da_ref[4 * m + d] = a - shifted(a, offset)
            kb_ref[4 * m + d] = 0.5 * (k + shifted(k, offset))
        weights(m, ref[0])
    across = 4 * len(in_plane)
    da_ref[across] = own_ref[1] - other_ref[1]
    kb_ref[across] = 0.5 * (k_ref[2 * w + y] + k_ref[2 * w + 1 - y])
    link = across + 1
    if stage > 1:
        def edge(slot, here, there, coeff):
            da_ref[link + slot] = here[1] - there[1]
            kb_ref[link + slot] = coeff
            both = jnp.concatenate(split(here[0] - there[0]), 0)
            w_ref[len(in_plane) + slot] = jnp.concatenate([both, both], 1)

        slot = 0
        visits = [(stage, (0, 1))] + [(pairs - 1, (0,))] * extra
        for at, sides in visits:
            slot = edges(at, sides, slot, n_term, n_space, k_ref, blocks, halo_ref, edge)
        for index in range(linked):
            @pl.when(slot <= index)
            def _():
                da_ref[link + index] = jnp.zeros((modes, cells), F32)
                kb_ref[link + index] = jnp.zeros((terms, cells), F32)
                w_ref[len(in_plane) + index] = jnp.zeros((2 * modes, 2 * cells), BF16)

    if stage == 1:
        upward = jnp.where(w % 2 == 0, 1, 0)
        for direction in (0, 1):
            for parity in (0, 1):
                @pl.when((upward == direction) & (y == parity))
                def _():
                    here = own_ref if parity == direction else other_ref
                    there = blocks[0] if parity == 1 - direction else blocks[1]
                    da_ref[link] = here[1] - there[1]
                    weights(len(in_plane), here[0] - there[0])

        kb_ref[link] = 0.5 * (k_ref[2 * w + upward] + k_ref[2 * w + 3 * upward - 1])

    for r in range(0, modes, GROUP):
        rows = [[] for _ in range(len(in_plane) + linked)]
        da = [da_ref[d, r : r + GROUP, :] for d in range(across + 1 + linked)]
        for q in range(terms):
            part = [da[d] * kb_ref[d, q : q + 1, :] for d in range(across + 1 + linked)]
            for m in range(len(in_plane)):
                total = (part[4 * m] + part[4 * m + 1]) + (part[4 * m + 2] + part[4 * m + 3])
                if m == 0:
                    total = total + part[across]
                elif m == 1:
                    total = total - part[across]
                rows[m].append(total)
            for index in range(linked):
                rows[len(in_plane) + index].append(part[link + index])
        out = product(rows, jnp.concatenate([w_ref[m] for m in range(len(rows))], 1))
        out = out.reshape(terms, GROUP, 2 * modes)
        acc_ref[:, r : r + GROUP] = out if first else before_ref[:, r : r + GROUP] + out

    if stage > 1:
        return

    def edge(slot, here, there, coeff):
        dz_ref[...] = here[1] - there[1]
        kz_ref[...] = coeff
        both = jnp.concatenate(split(here[0] - there[0]), 0)
        wz_ref[...] = jnp.concatenate([both, both], 1)

    slot = edges(stage, (0, 1), 0, n_term, n_space, k_ref, blocks, halo_ref, edge, skip=True)

    @pl.when(slot > 0)
    def _():
        for r in range(0, modes, GROUP):
            dz = dz_ref[r : r + GROUP, :]
            rows = [[dz * kz_ref[q : q + 1, :] for q in range(terms)]]
            out = product(rows, wz_ref[...])
            acc_ref[:, r : r + GROUP] += out.reshape(terms, GROUP, 2 * modes)


def product(rows, weights):
    left = []
    for part in rows:
        left += split(jnp.concatenate(part, 0))
    return lax.dot_general(jnp.concatenate(left, 1), weights, NT, preferred_element_type=F32)


def edges(stage, sides, slot, n_term, n_space, k_ref, blocks, halo_ref, edge, skip=False):
    pairs = n_term // 2
    modes = blocks[0].shape[1]
    term_at, space_at = lax.axis_index("term"), lax.axis_index("space")
    z, y = term_at // 2, term_at % 2
    w = z ^ stage
    far = stage >= pairs // 2
    is_low = term_at < n_term // 2
    for upward in (0, 1):
        near_w = w + 1 if upward else w - 1
        inside = (near_w >= 0) & (near_w < pairs) & (near_w ^ z < stage)
        for parity in (0, 1):
            side = 0 if parity == upward else 1
            if side not in sides:
                continue
            here = blocks[2 * stage + side]
            mine = y == parity
            if not skip:
                for j in range(stage):
                    @pl.when(inside & mine & (near_w ^ z == j))
                    def _(slot=slot):
                        plane = 2 * w + upward
                        beyond = plane + (1 if upward else -1)
                        edge(slot, here, blocks[2 * j + 1 - side], 0.5 * (k_ref[plane] + k_ref[beyond]))

                slot = slot + jnp.where(inside & mine, 1, 0)
            used = mine & (w == (pairs - 1 if upward else 0))
            plane = n_term - 1 if upward else 0
            edge_space = space_at == (n_space - 1 if upward else 0)
            if far:
                used = used & (is_low if upward else jnp.logical_not(is_low))
            else:
                used = used & (jnp.logical_not(is_low) if upward else is_low) & edge_space

            @pl.when(used)
            def _(slot=slot):
                if far:
                    came = jnp.where(edge_space, 0.0, halo_ref[...])
                    halo = (came[:modes], came[modes : 2 * modes])
                    edge(slot, here, halo, 0.5 * (k_ref[plane] + came[2 * modes :]))
                else:
                    edge(slot, here, (0.0, 0.0), 0.5 * k_ref[plane])

            slot = slot + jnp.where(used, 1, 0)
    return slot


def last_kernel(n_term, n_space, mine, *refs):
    pairs = n_term // 2
    k_ref, blocks, rest = refs[0], refs[1 : 1 + n_term], refs[1 + n_term :]
    halo_ref, before_ref, keep_ref, send_ref, acc_ref, da_ref, kb_ref, w_ref = rest
    modes, cells = blocks[0].shape[1:]
    terms = k_ref.shape[1]
    term_at, space_at = lax.axis_index("term"), lax.axis_index("space")
    z, y = term_at // 2, term_at % 2
    w = z ^ (pairs - 1)
    column_ref, other_ref = blocks[-2], blocks[-1]
    a, k = other_ref[1], k_ref[2 * w + 1 - y]
    for d, offset in enumerate(OFFSETS):
        da_ref[d] = a - shifted(a, offset)
        kb_ref[d] = 0.5 * (k + shifted(k, offset))

    def weights(slot, values):
        both = jnp.concatenate(split(values), 0)
        at = 2 * slot * cells
        w_ref[:, at : at + cells] = both
        w_ref[:, at + cells : at + 2 * cells] = both

    weights(0, other_ref[0])
    da_ref[4] = a - column_ref[1]
    kb_ref[4] = 0.5 * (k + k_ref[2 * w + y])
    weights(1, other_ref[0] - column_ref[0])

    def edge(slot, here, there, coeff):
        da_ref[5] = here[1] - there[1]
        kb_ref[5] = coeff
        weights(2, here[0] - there[0])

    edges(pairs - 1, (1,), 0, n_term, n_space, k_ref, blocks, halo_ref, edge)

    side = space_at // 2 % 2
    side = side if mine else 1 - side
    width = modes // n_space
    size = 2 * width
    step = min(GROUP, size)
    for index in range(n_space // 4):
        for r in range(0, size, step):
            start = pl.multiple_of((2 * index + side) * size + r, step)
            da = [da_ref[d, pl.ds(start, step), :] for d in range(6)]
            rows = [[], [], []]
            for q in range(terms):
                part = [da[d] * kb_ref[d, q : q + 1, :] for d in range(6)]
                rows[0].append((part[0] + part[1]) + (part[2] + part[3]))
                rows[1].append(part[4])
                rows[2].append(part[5])
            out = product(rows, w_ref[...]).reshape(terms, step, 2 * modes)
            at = index * size + r
            acc_ref[:, at : at + step] = before_ref[:, pl.ds(start, step)] + out

    core = space_at % 2
    flat_ref = acc_ref.reshape(terms * (modes // 2), 2 * modes)
    lane = lax.broadcasted_iota(jnp.int32, (terms, 2 * modes), 1)
    for index in range(n_space // 4):
        for j in range(width // 2):
            packed = []
            for at in (index * size + 2 * j, index * size + width + 2 * j):
                even = flat_ref[pl.ds(at, terms, stride=modes // 2), :]
                odd = flat_ref[pl.ds(at + 1, terms, stride=modes // 2), :]
                even = even + pltpu.roll(even, modes, 1)
                odd = odd + pltpu.roll(odd, modes, 1)
                packed.append(jnp.where(lane < modes, even, odd))
            to = slice(2 * modes * j, 2 * modes * (j + 1))
            keep_ref[index, :, to] = jnp.where(core == 0, packed[0], packed[1])
            send_ref[index, :, to] = jnp.where(core == 0, packed[1], packed[0])


def call(kernel, operands, out_shape, scratch, flops=1 << 29):
    whole = pl.BlockSpec(memory_space=pltpu.VMEM)
    return pl.pallas_call(
        kernel,
        out_shape=out_shape,
        in_specs=[whole] * len(operands),
        out_specs=jax.tree.map(lambda _: whole, out_shape),
        scratch_shapes=scratch,
        compiler_params=pltpu.CompilerParams(vmem_limit_bytes=40 << 20),
        cost_estimate=pl.CostEstimate(flops=flops, bytes_accessed=flops >> 7, transcendentals=0),
    )(*operands)


def run_pair(stage, n_term, n_space, coeffs, blocks, halo, before):
    modes, cells = blocks[0].shape[1:]
    terms = coeffs.shape[1]
    extra = len(blocks) - 2 * stage - 2
    operands = [coeffs] + list(blocks)
    if halo is not None:
        operands.append(halo)
    if before is not None:
        operands.append(before)
    kernel = functools.partial(pair_kernel, stage, n_term, n_space, before is None, extra)
    scratch = [
        pltpu.VMEM((16, modes, cells), F32),
        pltpu.VMEM((16, terms, cells), F32),
        pltpu.VMEM((6, 2 * modes, 2 * cells), BF16),
        pltpu.VMEM((modes, cells), F32),
        pltpu.VMEM((terms, cells), F32),
        pltpu.VMEM((2 * modes, 2 * cells), BF16),
    ]
    shape = jax.ShapeDtypeStruct((terms, modes, 2 * modes), F32)
    return call(kernel, operands, shape, scratch)


def run_last(mine, n_term, n_space, coeffs, blocks, halo, before):
    modes, cells = blocks[0].shape[1:]
    terms = coeffs.shape[1]
    scratch = [
        pltpu.VMEM((terms, modes // 2, 2 * modes), F32),
        pltpu.VMEM((6, modes, cells), F32),
        pltpu.VMEM((6, terms, cells), F32),
        pltpu.VMEM((2 * modes, 6 * cells), BF16),
    ]
    shape = jax.ShapeDtypeStruct((n_space // 4, terms, modes * modes // n_space), F32)
    kernel = functools.partial(last_kernel, n_term, n_space, mine)
    return call(kernel, [coeffs] + list(blocks) + [halo, before], [shape, shape], scratch, 0 if mine else 1 << 29)


def exchange(values, axis, apart):
    count = lax.axis_size(axis)
    return lax.ppermute(values, axis, [(i, i ^ apart) for i in range(count)])


def local(right_modes, adjoint_modes, conductivity_terms):
    n_term, n_space = lax.axis_size("term"), lax.axis_size("space")
    term_at, space_at = lax.axis_index("term"), lax.axis_index("space")
    pairs = n_term // 2
    z, y = term_at // 2, term_at % 2
    modes, cells = right_modes.shape[1:]
    terms = conductivity_terms.shape[1]

    def after(x, *deps):
        return lax.optimization_barrier((x,) + deps)[0]

    def go(stage, before, halo=None):
        seen = blocks[: 2 * stage + 2]
        if stage == pairs - 2:
            seen = seen + [blocks[-2]]
        return run_pair(stage, n_term, n_space, conductivity_terms, seen, halo, before)

    which = lax.broadcasted_iota(jnp.int32, (2, 1, 1), 0)
    own = jnp.where(which == 0, right_modes, adjoint_modes)
    half = pairs // 2
    column = {}
    column[half] = exchange(own, "term", 2 * half)
    for stage in range(1, half):
        column[stage] = exchange(own, "term", 2 * stage)
        column[half + stage] = exchange(column[half], "term", 2 * stage)
    blocks = [own, exchange(own, "term", 1)]
    for stage in range(1, half):
        blocks += [column[stage], exchange(column[stage], "term", 1)]
    ahead = [column[half], exchange(column[half], "term", 1)]
    value = go(0, None)
    first_value = value
    blocks = blocks[:2] + [after(x, value) for x in blocks[2:]]
    for stage in range(1, half):
        value = go(stage, value)
    for stage in range(half + 1, pairs):
        came = after(column[stage], value)
        ahead += [came, exchange(came, "term", 1)]
    blocks += ahead

    is_low = term_at < n_term // 2
    wanted = jnp.where(is_low, z, (pairs - 1) ^ z)
    takes_own = (y == 0) == is_low
    rim = after(blocks[0], first_value)
    for j in range(pairs // 2):
        block = jnp.where(takes_own, blocks[2 * j], blocks[2 * j + 1])
        rim = block if j == 0 else jnp.where(wanted == j, block, rim)
    rim_coeff = jnp.where(is_low, conductivity_terms[0], conductivity_terms[-1])
    rim = jnp.concatenate([rim.reshape(2 * modes, cells), rim_coeff], 0)
    route = []
    for s in range(n_space):
        for t in range(n_term):
            low, high = s * n_term + t, (s + 1) % n_space * n_term + t
            route.append((high, low) if t < n_term // 2 else (low, high))
    halo = lax.ppermute(rim, ("space", "term"), route)

    for stage in range(half, pairs - 1):
        value = go(stage, value, halo)
    arguments = (n_term, n_space, conductivity_terms, blocks, halo, value)
    keep, send = run_last(False, *arguments)
    leaving = keep + exchange(send, "space", 1)
    away = exchange(leaving, "space", 2)
    value = after(value, leaving)
    keep, send = run_last(True, n_term, n_space, conductivity_terms, blocks, halo, value)
    middle = terms // 2
    came = [exchange(send[:, :middle], "space", 1), exchange(send[:, middle:], "space", 1)]
    total = keep + jnp.concatenate(came, 1) + away
    apart = 4
    while apart < n_space:
        bit = space_at // apart % 2
        halves = total.reshape((total.shape[0] // 2, 2) + total.shape[1:])
        send = lax.dynamic_index_in_dim(halves, 1 - bit, 1, keepdims=False)
        keep = lax.dynamic_index_in_dim(halves, bit, 1, keepdims=False)
        total = keep + exchange(send, "space", apart)
        apart *= 2
    return total[0]


def solution(mesh):
    placed = (
        P(("space", "term"), None, None),
        P(("space", "term"), None, None),
        P("space", "term", None),
    )
    return jax.shard_map(
        local, mesh=mesh, in_specs=placed, out_specs=P("term", "space"), check_vma=False
    )
```

time: 36.5 us -> 33.9 us (0.929)
  waiting for transfers between devices: 8.06 us -> 4.46 us
  local copies, waits for them, and re-layouts: 0.71 us -> 0.03 us
  other arithmetic: 1.15 us -> 1.8 us
  starting transfers between devices: 13.8 us -> 14.4 us
  Pallas kernels: 12.5 us -> 12.9 us
    ppermute x9 -> x11, waiting for transfers between devices: 8.05 us -> 4.46 us  [exchange(): return lax.ppermute(values, axis, [(i, i ^ apart) for i in range(count)])]
    unnamed x7 -> x6, local copies, waits for them, and re-layouts: 0.7 us -> 0.02 us
    squeeze x0 -> x1, other arithmetic: none -> 0.68 us  [local(): return total[0]]
    ppermute x9 -> x11, starting transfers between devices: 13.6 us -> 14.2 us  [exchange(): return lax.ppermute(values, axis, [(i, i ^ apart) for i in range(count)])]
    pallas_call x4 -> x5, Pallas kernels: 12.5 us -> 12.9 us  [call(): pl.pallas_call(kernel, out_shape=out_shape, in_specs=[whole] * len(operan...]
  transfers between devices with their start and end apart: 10 -> 12, of which waited for: 6 -> 7; matrix products, arithmetic and copies ran while one was open for 0% -> 0% of each run, Pallas kernels for 23% -> 34%
where the time goes in v4:
time: 33.9 us; the launch traced here: 33.7 us
  starting transfers between devices  14.4 us (42%)
  Pallas kernels  12.9 us (38%)
  waiting for transfers between devices  4.46 us (13%)
  other arithmetic  1.8 us (5%)
    ppermute x11, starting transfers between devices, exchange(): return lax.ppermute(values, axis, [(i, i ^ apart) for i in range(count)])  14.2 us
    pallas_call x5, Pallas kernels, call(): pl.pallas_call(kernel, out_shape=out_shape, in_specs=[whole] * len(operan...  12.9 us
    ppermute x11, waiting for transfers between devices, exchange(): return lax.ppermute(values, axis, [(i, i ^ apart) for i in range(count)])  4.46 us
    select_n x1, other arithmetic, local(): own = jnp.where(which == 0, right_modes, adjoint_modes)  0.99 us
  transfers between devices with their start and end apart: 12, of which 7 were waited for; matrix products, arithmetic and copies ran while one was open for 0% of the time, Pallas kernels for 34%

profile of v4, /device:TPU:0, one launch (start us, length us, event | category | flops | bytes accessed | tf_op | source)
XLA Modules:
  0.0 33.7 jit_solution(6588290487325519634)
XLA Ops:
  0.0 1.0 %broadcast_select_fusion.refs_1_ = f32[2,64,256]{2,1,0:T(8,128)S(1)} fusion(f32[64,256]{1,0:T(8,128)} %bitcast.8, f32[64,256]{1,0:T(8,128)} %bitcast.10, pred[2]{0:T(512)(128)(4,1)S(1)} %iota_compare_fusion), kind=kLoop, calls=%fused_computation.5 | loop fusion | flops 32768 | bytes 262146 | tf_op jit(solution)/shard_map/jit(_where)/select_n | solution.py:337
  1.0 3.1 %collective-permute-start.1 = (f32[2,64,256]{2,1,0:T(8,128)S(1)}, f32[2,64,256]{2,1,0:T(8,128)S(1)}, u32[]{:S(2)}, u32[]{:S(2)}) collective-permute-start(f32[2,64,256]{2,1,0:T(8,128)S(1)} %broadcast_select_fusion.refs_1_), channel_id=1, source_target_pairs={{0,2},{1,3},{2,0},{3,1},{4,6},{5,7},{6,4},{7,5},{8,10},{9,11},{10,... | collective-permute-start | bytes 393224 | tf_op jit(solution)/shard_map/ppermute | solution.py:316
  4.1 1.5 %collective-permute-start = (f32[2,64,256]{2,1,0:T(8,128)S(1)}, f32[2,64,256]{2,1,0:T(8,128)S(1)}, u32[]{:S(2)}, u32[]{:S(2)}) collective-permute-start(f32[2,64,256]{2,1,0:T(8,128)S(1)} %broadcast_select_fusion.refs_1_), channel_id=1, source_target_pairs={{0,1},{1,0},{2,3},{3,2},{4,5},{5,4},{6,7},{7,6},{8,9},{9,8},{10,11... | collective-permute-start | bytes 393224 | tf_op jit(solution)/shard_map/ppermute | solution.py:316
  5.6 2.6 %collective-permute-start.3 = (f32[2,64,256]{2,1,0:T(8,128)S(1)}, f32[2,64,256]{2,1,0:T(8,128)S(1)}, u32[]{:S(2)}, u32[]{:S(2)}) collective-permute-start(f32[2,64,256]{2,1,0:T(8,128)S(1)} %broadcast_select_fusion.refs_1_), channel_id=1, source_target_pairs={{0,4},{1,5},{2,6},{3,7},{4,0},{5,1},{6,2},{7,3},{8,12},{9,13},{10,... | collective-permute-start | bytes 393224 | tf_op jit(solution)/shard_map/ppermute | solution.py:316
  8.2 0.0 collective-permute-done.1.refs_3_
  8.2 2.6 %collective-permute-start.2 = (f32[2,64,256]{2,1,0:T(8,128)S(1)}, f32[2,64,256]{2,1,0:T(8,128)S(1)}, u32[]{:S(2)}, u32[]{:S(2)}) collective-permute-start(f32[2,64,256]{2,1,0:T(8,128)S(1)} %collective-permute-done.1.refs_3_), channel_id=1, source_target_pairs={{0,1},{1,0},{2,3},{3,2},{4,5},{5,4},{6,7},{7,6},{8,9},{9,8},{10,11... | collective-permute-start | bytes 393224 | tf_op jit(solution)/shard_map/ppermute | solution.py:316
  10.8 0.0 copy-start.1
  10.8 0.0 copy-start.2
  10.8 0.0 collective-permute-done.refs_2_
  10.8 2.9 %shard_map.37.refs_5_ = f32[32,64,128]{2,1,0:T(8,128)S(1)} custom-call(f32[8,32,256]{2,1,0:T(8,128)S(1)} %copy-done, f32[2,64,256]{2,1,0:T(8,128)S(1)} %broadcast_select_fusion.refs_1_, f32[2,64,256]{2,1,0:T(8,128)S(1)} %collective-permute-done.refs_2_), custom_call_target="tpu_custom_call" | custom-call | flops 536870912 | bytes 4194304 | tf_op jit(solution)/shard_map/pallas_call | solution.py:267
  13.7 0.3 collective-permute-done.3.refs_5_
  14.0 0.0 collective-permute-start.5
  14.0 0.1 select_select_fusion
  14.1 0.2 collective-permute-start.7
  14.4 1.6 %collective-permute-start.4 = (f32[2,64,256]{2,1,0:T(8,128)S(1)}, f32[2,64,256]{2,1,0:T(8,128)S(1)}, u32[]{:S(2)}, u32[]{:S(2)}) collective-permute-start(f32[2,64,256]{2,1,0:T(8,128)S(1)} %collective-permute-done.3.refs_5_), channel_id=1, source_target_pairs={{0,1},{1,0},{2,3},{3,2},{4,5},{5,4},{6,7},{7,6},{8,9},{9,8},{10,11... | collective-permute-start | bytes 393224 | tf_op jit(solution)/shard_map/ppermute | solution.py:316
  16.0 2.6 %shard_map.38.refs_9_ = f32[32,64,128]{2,1,0:T(8,128)S(1)} custom-call(f32[8,32,256]{2,1,0:T(8,128)S(1)} %copy-done, f32[2,64,256]{2,1,0:T(8,128)S(1)} %broadcast_select_fusion.refs_1_, f32[2,64,256]{2,1,0:T(8,128)S(1)} %collective-permute-done.refs_2_, f32[2,64,256]{2,1,0:T(8,128)S(1)} %collective-permute-done.1.refs_3_, ...), custom_call_target="tpu_custom_call" | custom-call | flops 536870912 | bytes 4194304 | tf_op jit(solution)/shard_map/pallas_call | solution.py:267
  18.6 0.3 collective-permute-done.5.refs_7_
  19.0 0.6 %collective-permute-start.6 = (f32[2,64,256]{2,1,0:T(8,128)S(1)}, f32[2,64,256]{2,1,0:T(8,128)S(1)}, u32[]{:S(2)}, u32[]{:S(2)}) collective-permute-start(f32[2,64,256]{2,1,0:T(8,128)S(1)} %collective-permute-done.5.refs_7_), channel_id=1, source_target_pairs={{0,1},{1,0},{2,3},{3,2},{4,5},{5,4},{6,7},{7,6},{8,9},{9,8},{10,11... | collective-permute-start | bytes 393224 | tf_op jit(solution)/shard_map/ppermute | solution.py:316
  19.6 0.5 %collective-permute-done.4.refs_6_ = f32[2,64,256]{2,1,0:T(8,128)S(1)} collective-permute-done((f32[2,64,256]{2,1,0:T(8,128)S(1)}, f32[2,64,256]{2,1,0:T(8,128)S(1)}, u32[]{:S(2)}, u32[]{:S(2)}) %collective-permute-start.4) | collective-permute-done | bytes 131104 | tf_op jit(solution)/shard_map/ppermute | solution.py:316
  20.1 4.4 %shard_map.39.refs_10_ = f32[32,64,128]{2,1,0:T(8,128)S(1)} custom-call(f32[8,32,256]{2,1,0:T(8,128)S(1)} %copy-done, f32[2,64,256]{2,1,0:T(8,128)S(1)} %broadcast_select_fusion.refs_1_, f32[2,64,256]{2,1,0:T(8,128)S(1)} %collective-permute-done.refs_2_, f32[2,64,256]{2,1,0:T(8,128)S(1)} %collective-permute-done.1.refs_3_, ...), custom_call_target="tpu_custom_call" | custom-call | flops 536870912 | bytes 4194304 | tf_op jit(solution)/shard_map/pallas_call | solution.py:267
  24.5 0.0 collective-permute-done.6.refs_8_
  24.5 1.5 %shard_map.40 = (f32[1,32,1024]{2,1,0:T(8,128)S(1)}, f32[1,32,1024]{2,1,0:T(8,128)S(1)}) custom-call(f32[8,32,256]{2,1,0:T(8,128)S(1)} %copy-done, f32[2,64,256]{2,1,0:T(8,128)S(1)} %broadcast_select_fusion.refs_1_, f32[2,64,256]{2,1,0:T(8,128)S(1)} %collective-permute-done.refs_2_, f32[2,64,256]{2,1,0:T(8,128)S(1)} %collective-permute-done.1.refs_3_, ...), custom_call_target="tpu_custom_call" | custom-call | flops 536870912 | bytes 4194304 | tf_op jit(solution)/shard_map/pallas_call | solution.py:267
  26.0 0.1 collective-permute-start.8
  26.1 1.3 %collective-permute-done.8 = f32[1,32,1024]{2,1,0:T(8,128)S(1)} collective-permute-done((f32[1,32,1024]{2,1,0:T(8,128)S(1)}, f32[1,32,1024]{2,1,0:T(8,128)S(1)}, u32[]{:S(2)}, u32[]{:S(2)}) %collective-permute-start.8) | collective-permute-done | bytes 131104 | tf_op jit(solution)/shard_map/ppermute | solution.py:316
  27.4 1.6 %collective-permute-start.11 = (f32[1,32,1024]{2,1,0:T(8,128)S(1)}, f32[1,32,1024]{2,1,0:T(8,128)S(1)}, u32[]{:S(2)}, u32[]{:S(2)}) collective-permute-start(f32[1,32,1024]{2,1,0:T(8,128)S(1)} %add.15), channel_id=1, source_target_pairs={{0,16},{8,24},{16,0},{24,8},{1,17},{9,25},{17,1},{25,9},{2,18},{10... | collective-permute-start | bytes 393224 | tf_op jit(solution)/shard_map/ppermute | solution.py:316
  29.0 1.5 %shard_map.41 = (f32[1,32,1024]{2,1,0:T(8,128)S(1)}, f32[1,32,1024]{2,1,0:T(8,128)S(1)}) custom-call(f32[8,32,256]{2,1,0:T(8,128)S(1)} %copy-done, f32[2,64,256]{2,1,0:T(8,128)S(1)} %broadcast_select_fusion.refs_1_, f32[2,64,256]{2,1,0:T(8,128)S(1)} %collective-permute-done.refs_2_, f32[2,64,256]{2,1,0:T(8,128)S(1)} %collective-permute-done.1.refs_3_, ...), custom_call_target="tpu_custom_call" | custom-call | tf_op jit(solution)/shard_map/pallas_call | solution.py:267
  30.5 0.1 collective-permute-start.10
  30.6 0.5 %collective-permute-start.9 = (f32[1,16,1024]{2,1,0:T(8,128)S(1)}, f32[1,16,1024]{2,1,0:T(8,128)S(1)}, u32[]{:S(2)}, u32[]{:S(2)}) collective-permute-start(f32[1,16,1024]{2,1,0:T(8,128)S(1)} %get-tuple-element.21), channel_id=1, source_target_pairs={{0,8},{8,0},{16,24},{24,16},{1,9},{9,1},{17,25},{25,17},{2,10},{10... | collective-permute-start | bytes 196616 | tf_op jit(solution)/shard_map/ppermute | solution.py:316
  31.1 0.7 %collective-permute-done.10 = f32[1,16,1024]{2,1,0:T(8,128)S(1)} collective-permute-done((f32[1,16,1024]{2,1,0:T(8,128)S(1)}, f32[1,16,1024]{2,1,0:T(8,128)S(1)}, u32[]{:S(2)}, u32[]{:S(2)}) %collective-permute-start.10) | collective-permute-done | bytes 65568 | tf_op jit(solution)/shard_map/ppermute | solution.py:316
  31.9 0.2 collective-permute-done.9
  32.0 1.0 %collective-permute-done.11 = f32[1,32,1024]{2,1,0:T(8,128)S(1)} collective-permute-done((f32[1,32,1024]{2,1,0:T(8,128)S(1)}, f32[1,32,1024]{2,1,0:T(8,128)S(1)}, u32[]{:S(2)}, u32[]{:S(2)}) %collective-permute-start.11) | collective-permute-done | bytes 131104 | tf_op jit(solution)/shard_map/ppermute | solution.py:316
  33.1 0.7 %fusion.1 = f32[32,1024]{1,0:T(8,128)} fusion(f32[1,32,1024]{2,1,0:T(8,128)S(1)} %collective-permute-done.11, f32[1,32,1024]{2,1,0:T(8,128)S(1)} %get-tuple-element.19, f32[1,16,1024]{2,1,0:T(8,128)S(1)} %collective-permute-done.10, f32[1,16,1024]{2,1,0:T(8,128)S(1)} %collective-permute-done.9), kind=kLoop, calls=%fused_computation.3 | loop fusion | flops 98304 | bytes 524288 | tf_op jit(solution)/shard_map/squeeze | solution.py:393
  (11 shorter events, 0.1 us)
Async XLA Ops:
  0.0 10.8 %copy-start = (f32[8,32,256]{2,1,0:T(8,128)S(1)}, f32[8,32,256]{2,1,0:T(8,128)}, u32[]{:S(2)}) copy-start(f32[8,32,256]{2,1,0:T(8,128)} %refs_0_.9) | copy-start | bytes 786436
  1.0 7.2 %collective-permute-start.1 = (f32[2,64,256]{2,1,0:T(8,128)S(1)}, f32[2,64,256]{2,1,0:T(8,128)S(1)}, u32[]{:S(2)}, u32[]{:S(2)}) collective-permute-start(f32[2,64,256]{2,1,0:T(8,128)S(1)} %broadcast_select_fusion.refs_1_), channel_id=1, source_target_pairs={{0,2},{1,3},{2,0},{3,1},{4,6},{5,7},{6,4},{7,5},{8,10},{9,11},{10,... | collective-permute-start | bytes 393224 | tf_op jit(solution)/shard_map/ppermute | solution.py:316
  4.1 6.7 %collective-permute-start = (f32[2,64,256]{2,1,0:T(8,128)S(1)}, f32[2,64,256]{2,1,0:T(8,128)S(1)}, u32[]{:S(2)}, u32[]{:S(2)}) collective-permute-start(f32[2,64,256]{2,1,0:T(8,128)S(1)} %broadcast_select_fusion.refs_1_), channel_id=1, source_target_pairs={{0,1},{1,0},{2,3},{3,2},{4,5},{5,4},{6,7},{7,6},{8,9},{9,8},{10,11... | collective-permute-start | bytes 393224 | tf_op jit(solution)/shard_map/ppermute | solution.py:316
  5.6 8.4 %collective-permute-start.3 = (f32[2,64,256]{2,1,0:T(8,128)S(1)}, f32[2,64,256]{2,1,0:T(8,128)S(1)}, u32[]{:S(2)}, u32[]{:S(2)}) collective-permute-start(f32[2,64,256]{2,1,0:T(8,128)S(1)} %broadcast_select_fusion.refs_1_), channel_id=1, source_target_pairs={{0,4},{1,5},{2,6},{3,7},{4,0},{5,1},{6,2},{7,3},{8,12},{9,13},{10,... | collective-permute-start | bytes 393224 | tf_op jit(solution)/shard_map/ppermute | solution.py:316
  8.2 5.8 %collective-permute-start.2 = (f32[2,64,256]{2,1,0:T(8,128)S(1)}, f32[2,64,256]{2,1,0:T(8,128)S(1)}, u32[]{:S(2)}, u32[]{:S(2)}) collective-permute-start(f32[2,64,256]{2,1,0:T(8,128)S(1)} %collective-permute-done.1.refs_3_), channel_id=1, source_target_pairs={{0,1},{1,0},{2,3},{3,2},{4,5},{5,4},{6,7},{7,6},{8,9},{9,8},{10,11... | collective-permute-start | bytes 393224 | tf_op jit(solution)/shard_map/ppermute | solution.py:316
  10.8 3.2 %copy-start.1 = (f32[1,64,256]{2,1,0:T(8,128)S(1)}, f32[1,64,256]{2,1,0:T(8,128)}, u32[]{:S(2)}) copy-start(f32[1,64,256]{2,1,0:T(8,128)} %param.4) | copy-start | bytes 196612
  10.8 3.2 %copy-start.2 = (f32[1,64,256]{2,1,0:T(8,128)S(1)}, f32[1,64,256]{2,1,0:T(8,128)}, u32[]{:S(2)}) copy-start(f32[1,64,256]{2,1,0:T(8,128)} %param.3) | copy-start | bytes 196612
  14.0 5.0 %collective-permute-start.5 = (f32[2,64,256]{2,1,0:T(8,128)S(1)}, f32[2,64,256]{2,1,0:T(8,128)S(1)}, u32[]{:S(2)}, u32[]{:S(2)}) collective-permute-start(f32[2,64,256]{2,1,0:T(8,128)S(1)} %collective-permute-done.3.refs_5_), channel_id=1, source_target_pairs={{0,2},{1,3},{2,0},{3,1},{4,6},{5,7},{6,4},{7,5},{8,10},{9,11},{10,... | collective-permute-start | bytes 393224 | tf_op jit(solution)/shard_map/ppermute | solution.py:316
  14.1 6.0 %collective-permute-start.7 = (f32[160,256]{1,0:T(8,128)S(1)}, f32[160,256]{1,0:T(8,128)S(1)}, u32[]{:S(2)}, u32[]{:S(2)}) collective-permute-start(f32[160,256]{1,0:T(8,128)S(1)} %pad_maximum_fusion), channel_id=1, source_target_pairs={{8,0},{9,1},{10,2},{11,3},{4,12},{5,13},{6,14},{7,15},{16,8},{17,9... | collective-permute-start | bytes 491528 | tf_op jit(solution)/shard_map/ppermute | solution.py:372
  14.4 5.7 %collective-permute-start.4 = (f32[2,64,256]{2,1,0:T(8,128)S(1)}, f32[2,64,256]{2,1,0:T(8,128)S(1)}, u32[]{:S(2)}, u32[]{:S(2)}) collective-permute-start(f32[2,64,256]{2,1,0:T(8,128)S(1)} %collective-permute-done.3.refs_5_), channel_id=1, source_target_pairs={{0,1},{1,0},{2,3},{3,2},{4,5},{5,4},{6,7},{7,6},{8,9},{9,8},{10,11... | collective-permute-start | bytes 393224 | tf_op jit(solution)/shard_map/ppermute | solution.py:316
  19.0 5.5 %collective-permute-start.6 = (f32[2,64,256]{2,1,0:T(8,128)S(1)}, f32[2,64,256]{2,1,0:T(8,128)S(1)}, u32[]{:S(2)}, u32[]{:S(2)}) collective-permute-start(f32[2,64,256]{2,1,0:T(8,128)S(1)} %collective-permute-done.5.refs_7_), channel_id=1, source_target_pairs={{0,1},{1,0},{2,3},{3,2},{4,5},{5,4},{6,7},{7,6},{8,9},{9,8},{10,11... | collective-permute-start | bytes 393224 | tf_op jit(solution)/shard_map/ppermute | solution.py:316
  26.0 1.4 %collective-permute-start.8 = (f32[1,32,1024]{2,1,0:T(8,128)S(1)}, f32[1,32,1024]{2,1,0:T(8,128)S(1)}, u32[]{:S(2)}, u32[]{:S(2)}) collective-permute-start(f32[1,32,1024]{2,1,0:T(8,128)S(1)} %get-tuple-element.17), channel_id=1, source_target_pairs={{0,8},{8,0},{16,24},{24,16},{1,9},{9,1},{17,25},{25,17},{2,10},{10... | collective-permute-start | bytes 393224 | tf_op jit(solution)/shard_map/ppermute | solution.py:316
  27.4 5.6 %collective-permute-start.11 = (f32[1,32,1024]{2,1,0:T(8,128)S(1)}, f32[1,32,1024]{2,1,0:T(8,128)S(1)}, u32[]{:S(2)}, u32[]{:S(2)}) collective-permute-start(f32[1,32,1024]{2,1,0:T(8,128)S(1)} %add.15), channel_id=1, source_target_pairs={{0,16},{8,24},{16,0},{24,8},{1,17},{9,25},{17,1},{25,9},{2,18},{10... | collective-permute-start | bytes 393224 | tf_op jit(solution)/shard_map/ppermute | solution.py:316
  30.5 1.3 %collective-permute-start.10 = (f32[1,16,1024]{2,1,0:T(8,128)S(1)}, f32[1,16,1024]{2,1,0:T(8,128)S(1)}, u32[]{:S(2)}, u32[]{:S(2)}) collective-permute-start(f32[1,16,1024]{2,1,0:T(8,128)S(1)} %get-tuple-element.22), channel_id=1, source_target_pairs={{0,8},{8,0},{16,24},{24,16},{1,9},{9,1},{17,25},{25,17},{2,10},{10... | collective-permute-start | bytes 196616 | tf_op jit(solution)/shard_map/ppermute | solution.py:316
  30.6 1.4 %collective-permute-start.9 = (f32[1,16,1024]{2,1,0:T(8,128)S(1)}, f32[1,16,1024]{2,1,0:T(8,128)S(1)}, u32[]{:S(2)}, u32[]{:S(2)}) collective-permute-start(f32[1,16,1024]{2,1,0:T(8,128)S(1)} %get-tuple-element.21), channel_id=1, source_target_pairs={{0,8},{8,0},{16,24},{24,16},{1,9},{9,1},{17,25},{25,17},{2,10},{10... | collective-permute-start | bytes 196616 | tf_op jit(solution)/shard_map/ppermute | solution.py:316

commit v5 on v4

--- a/solution.py
+++ b/solution.py
@@ -77,11 +77,10 @@
             both = jnp.concatenate(split(here[0] - there[0]), 0)
             w_ref[len(in_plane) + slot] = jnp.concatenate([both, both], 1)
 
-        slot = 0
-        visits = [(stage, (0, 1))] + [(pairs - 1, (0,))] * extra
-        for at, sides in visits:
-            slot = edges(at, sides, slot, n_term, n_space, k_ref, blocks, halo_ref, edge)
-        for index in range(linked):
+        slot = edges(stage, (0, 1), 0, n_term, n_space, k_ref, blocks, halo_ref, edge)
+        if extra:
+            edges(pairs - 1, (0,), linked - 1, n_term, n_space, k_ref, blocks, halo_ref, edge, fixed=True)
+        for index in range(linked - extra):
             @pl.when(slot <= index)
             def _():
                 da_ref[link + index] = jnp.zeros((modes, cells), F32)
@@ -101,23 +100,34 @@
 
         kb_ref[link] = 0.5 * (k_ref[2 * w + upward] + k_ref[2 * w + 3 * upward - 1])
 
-    for r in range(0, modes, GROUP):
-        rows = [[] for _ in range(len(in_plane) + linked)]
-        da = [da_ref[d, r : r + GROUP, :] for d in range(across + 1 + linked)]
+    def add(at, step, planes, links):
+        rows = [[] for _ in range(planes + links)]
+        da = [da_ref[d, at, :] for d in range(link + links)]
         for q in range(terms):
-            part = [da[d] * kb_ref[d, q : q + 1, :] for d in range(across + 1 + linked)]
-            for m in range(len(in_plane)):
+            part = [da[d] * kb_ref[d, q : q + 1, :] for d in range(link + links)]
+            for m in range(planes):
                 total = (part[4 * m] + part[4 * m + 1]) + (part[4 * m + 2] + part[4 * m + 3])
                 if m == 0:
                     total = total + part[across]
                 elif m == 1:
                     total = total - part[across]
                 rows[m].append(total)
-            for index in range(linked):
-                rows[len(in_plane) + index].append(part[link + index])
-        out = product(rows, jnp.concatenate([w_ref[m] for m in range(len(rows))], 1))
-        out = out.reshape(terms, GROUP, 2 * modes)
-        acc_ref[:, r : r + GROUP] = out if first else before_ref[:, r : r + GROUP] + out
+            for index in range(links):
+                rows[planes + index].append(part[link + index])
+        used = list(range(planes)) + [len(in_plane) + index for index in range(links)]
+        out = product(rows, jnp.concatenate([w_ref[m] for m in used], 1))
+        out = out.reshape(terms, step, 2 * modes)
+        acc_ref[:, at] = out if first else before_ref[:, at] + out
+
+    if extra:
+        size = 2 * modes // n_space
+        step = min(GROUP, size)
+        for mine in (0, 1):
+            for at in half_rows(mine, size, step, n_space):
+                add(at, step, 2 if mine else 3, linked - mine)
+    else:
+        for r in range(0, modes, GROUP):
+            add(slice(r, r + GROUP), GROUP, 2, linked)
 
     if stage > 1:
         return
@@ -139,6 +149,16 @@
             acc_ref[:, r : r + GROUP] += out.reshape(terms, GROUP, 2 * modes)
 
 
+def half_rows(mine, size, step, n_space):
+    side = lax.axis_index("space") // 2 % 2
+    side = side if mine else 1 - side
+    return [
+        pl.ds(pl.multiple_of((2 * index + side) * size + r, step), step)
+        for index in range(n_space // 4)
+        for r in range(0, size, step)
+    ]
+
+
 def product(rows, weights):
     left = []
     for part in rows:
@@ -146,7 +166,7 @@
     return lax.dot_general(jnp.concatenate(left, 1), weights, NT, preferred_element_type=F32)
 
 
-def edges(stage, sides, slot, n_term, n_space, k_ref, blocks, halo_ref, edge, skip=False):
+def edges(stage, sides, slot, n_term, n_space, k_ref, blocks, halo_ref, edge, skip=False, fixed=False):
     pairs = n_term // 2
     modes = blocks[0].shape[1]
     term_at, space_at = lax.axis_index("term"), lax.axis_index("space")
@@ -171,7 +191,7 @@
                         beyond = plane + (1 if upward else -1)
                         edge(slot, here, blocks[2 * j + 1 - side], 0.5 * (k_ref[plane] + k_ref[beyond]))
 
-                slot = slot + jnp.where(inside & mine, 1, 0)
+                slot = slot if fixed else slot + jnp.where(inside & mine, 1, 0)
             used = mine & (w == (pairs - 1 if upward else 0))
             plane = n_term - 1 if upward else 0
             edge_space = space_at == (n_space - 1 if upward else 0)
@@ -189,7 +209,7 @@
                 else:
                     edge(slot, here, (0.0, 0.0), 0.5 * k_ref[plane])
 
-            slot = slot + jnp.where(used, 1, 0)
+            slot = slot if fixed else slot + jnp.where(used, 1, 0)
     return slot
 
 
@@ -203,47 +223,56 @@
     z, y = term_at // 2, term_at % 2
     w = z ^ (pairs - 1)
     column_ref, other_ref = blocks[-2], blocks[-1]
-    a, k = other_ref[1], k_ref[2 * w + 1 - y]
-    for d, offset in enumerate(OFFSETS):
-        da_ref[d] = a - shifted(a, offset)
-        kb_ref[d] = 0.5 * (k + shifted(k, offset))
 
     def weights(slot, values):
         both = jnp.concatenate(split(values), 0)
-        at = 2 * slot * cells
-        w_ref[:, at : at + cells] = both
-        w_ref[:, at + cells : at + 2 * cells] = both
-
-    weights(0, other_ref[0])
-    da_ref[4] = a - column_ref[1]
-    kb_ref[4] = 0.5 * (k + k_ref[2 * w + y])
-    weights(1, other_ref[0] - column_ref[0])
+        w_ref[slot] = jnp.concatenate([both, both], 1)
+
+    in_plane = [(other_ref, 2 * w + 1 - y)]
+    if mine:
+        in_plane.append((column_ref, 2 * w + y))
+    planes = len(in_plane)
+    for m, (ref, plane) in enumerate(in_plane):
+        a, k = ref[1], k_ref[plane]
+        for d, offset in enumerate(OFFSETS):
+            da_ref[4 * m + d] = a - shifted(a, offset)
+            kb_ref[4 * m + d] = 0.5 * (k + shifted(k, offset))
+        weights(m, ref[0])
+    across = 4 * planes
+    da_ref[across] = other_ref[1] - column_ref[1]
+    kb_ref[across] = 0.5 * (k_ref[2 * w] + k_ref[2 * w + 1])
+    links = [across + 1]
+    if mine:
+        links.append(across + 2)
+    else:
+        weights(planes + 1, other_ref[0] - column_ref[0])
 
     def edge(slot, here, there, coeff):
-        da_ref[5] = here[1] - there[1]
-        kb_ref[5] = coeff
-        weights(2, here[0] - there[0])
-
-    edges(pairs - 1, (1,), 0, n_term, n_space, k_ref, blocks, halo_ref, edge)
-
-    side = space_at // 2 % 2
-    side = side if mine else 1 - side
+        da_ref[links[slot]] = here[1] - there[1]
+        kb_ref[links[slot]] = coeff
+        weights(planes + slot, here[0] - there[0])
+
+    for slot in range(len(links)):
+        edges(pairs - 1, (1 - slot,), slot, n_term, n_space, k_ref, blocks, halo_ref, edge, fixed=True)
+
+    size = 2 * modes // n_space
     width = modes // n_space
-    size = 2 * width
     step = min(GROUP, size)
-    for index in range(n_space // 4):
-        for r in range(0, size, step):
-            start = pl.multiple_of((2 * index + side) * size + r, step)
-            da = [da_ref[d, pl.ds(start, step), :] for d in range(6)]
-            rows = [[], [], []]
-            for q in range(terms):
-                part = [da[d] * kb_ref[d, q : q + 1, :] for d in range(6)]
-                rows[0].append((part[0] + part[1]) + (part[2] + part[3]))
-                rows[1].append(part[4])
-                rows[2].append(part[5])
-            out = product(rows, w_ref[...]).reshape(terms, step, 2 * modes)
-            at = index * size + r
-            acc_ref[:, at : at + step] = before_ref[:, pl.ds(start, step)] + out
+    for index, at in enumerate(half_rows(mine, size, step, n_space)):
+        da = [da_ref[d, at, :] for d in range(links[-1] + 1)]
+        rows = [[] for _ in range(planes + 2)]
+        for q in range(terms):
+            part = [da[d] * kb_ref[d, q : q + 1, :] for d in range(links[-1] + 1)]
+            for m in range(planes):
+                total = (part[4 * m] + part[4 * m + 1]) + (part[4 * m + 2] + part[4 * m + 3])
+                if mine:
+                    total = total - part[across] if m else total + part[across]
+                rows[m].append(total)
+            for slot, d in enumerate(links if mine else links + [across]):
+                rows[planes + slot].append(part[d])
+        weight = jnp.concatenate([w_ref[m] for m in range(planes + 2)], 1)
+        out = product(rows, weight).reshape(terms, step, 2 * modes)
+        acc_ref[:, index * step : (index + 1) * step] = before_ref[:, at] + out
 
     core = space_at % 2
     flat_ref = acc_ref.reshape(terms * (modes // 2), 2 * modes)
@@ -302,9 +331,9 @@
     terms = coeffs.shape[1]
     scratch = [
         pltpu.VMEM((terms, modes // 2, 2 * modes), F32),
-        pltpu.VMEM((6, modes, cells), F32),
-        pltpu.VMEM((6, terms, cells), F32),
-        pltpu.VMEM((2 * modes, 6 * cells), BF16),
+        pltpu.VMEM((11, modes, cells), F32),
+        pltpu.VMEM((11, terms, cells), F32),
+        pltpu.VMEM((4, 2 * modes, 2 * cells), BF16),
     ]
     shape = jax.ShapeDtypeStruct((n_space // 4, terms, modes * modes // n_space), F32)
     kernel = functools.partial(last_kernel, n_term, n_space, mine)

time: 33.9 us -> 33.8 us (level)
  transfers between devices with their start and end apart: 12 -> 12, of which waited for: 7 -> 8; matrix products, arithmetic and copies ran while one was open for 0% -> 0% of each run, Pallas kernels for 34% -> 33%
where the time goes in v5:
time: 33.8 us; the launch traced here: 33.7 us
  starting transfers between devices  14.4 us (43%)
  Pallas kernels  12.9 us (38%)
  waiting for transfers between devices  4.48 us (13%)
  other arithmetic  1.8 us (5%)
    ppermute x11, starting transfers between devices, exchange(): return lax.ppermute(values, axis, [(i, i ^ apart) for i in range(count)])  14.2 us
    pallas_call x5, Pallas kernels, call(): pl.pallas_call(kernel, out_shape=out_shape, in_specs=[whole] * len(operan...  12.9 us
    ppermute x11, waiting for transfers between devices, exchange(): return lax.ppermute(values, axis, [(i, i ^ apart) for i in range(count)])  4.48 us
    select_n x1, other arithmetic, local(): own = jnp.where(which == 0, right_modes, adjoint_modes)  0.99 us
    squeeze x1, other arithmetic, local(): return total[0]  0.68 us
  transfers between devices with their start and end apart: 12, of which 8 were waited for; matrix products, arithmetic and copies ran while one was open for 0% of the time, Pallas kernels for 33%

profile of v5, /device:TPU:0, one launch (start us, length us, event | category | flops | bytes accessed | tf_op | source)
XLA Modules:
  0.0 33.7 jit_solution(14846843262613807033)
XLA Ops:
  0.0 1.0 %broadcast_select_fusion.refs_1_ = f32[2,64,256]{2,1,0:T(8,128)S(1)} fusion(f32[64,256]{1,0:T(8,128)} %bitcast.8, f32[64,256]{1,0:T(8,128)} %bitcast.10, pred[2]{0:T(512)(128)(4,1)S(1)} %iota_compare_fusion), kind=kLoop, calls=%fused_computation.5 | loop fusion | flops 32768 | bytes 262146 | tf_op jit(solution)/shard_map/jit(_where)/select_n | solution.py:366
  1.0 3.1 %collective-permute-start.1 = (f32[2,64,256]{2,1,0:T(8,128)S(1)}, f32[2,64,256]{2,1,0:T(8,128)S(1)}, u32[]{:S(2)}, u32[]{:S(2)}) collective-permute-start(f32[2,64,256]{2,1,0:T(8,128)S(1)} %broadcast_select_fusion.refs_1_), channel_id=1, source_target_pairs={{0,2},{1,3},{2,0},{3,1},{4,6},{5,7},{6,4},{7,5},{8,10},{9,11},{10,... | collective-permute-start | bytes 393224 | tf_op jit(solution)/shard_map/ppermute | solution.py:345
  4.1 1.5 %collective-permute-start = (f32[2,64,256]{2,1,0:T(8,128)S(1)}, f32[2,64,256]{2,1,0:T(8,128)S(1)}, u32[]{:S(2)}, u32[]{:S(2)}) collective-permute-start(f32[2,64,256]{2,1,0:T(8,128)S(1)} %broadcast_select_fusion.refs_1_), channel_id=1, source_target_pairs={{0,1},{1,0},{2,3},{3,2},{4,5},{5,4},{6,7},{7,6},{8,9},{9,8},{10,11... | collective-permute-start | bytes 393224 | tf_op jit(solution)/shard_map/ppermute | solution.py:345
  5.6 2.6 %collective-permute-start.3 = (f32[2,64,256]{2,1,0:T(8,128)S(1)}, f32[2,64,256]{2,1,0:T(8,128)S(1)}, u32[]{:S(2)}, u32[]{:S(2)}) collective-permute-start(f32[2,64,256]{2,1,0:T(8,128)S(1)} %broadcast_select_fusion.refs_1_), channel_id=1, source_target_pairs={{0,4},{1,5},{2,6},{3,7},{4,0},{5,1},{6,2},{7,3},{8,12},{9,13},{10,... | collective-permute-start | bytes 393224 | tf_op jit(solution)/shard_map/ppermute | solution.py:345
  8.2 2.6 %collective-permute-start.2 = (f32[2,64,256]{2,1,0:T(8,128)S(1)}, f32[2,64,256]{2,1,0:T(8,128)S(1)}, u32[]{:S(2)}, u32[]{:S(2)}) collective-permute-start(f32[2,64,256]{2,1,0:T(8,128)S(1)} %collective-permute-done.1.refs_3_), channel_id=1, source_target_pairs={{0,1},{1,0},{2,3},{3,2},{4,5},{5,4},{6,7},{7,6},{8,9},{9,8},{10,11... | collective-permute-start | bytes 393224 | tf_op jit(solution)/shard_map/ppermute | solution.py:345
  10.8 0.0 copy-start.1
  10.8 0.0 copy-start.2
  10.8 0.0 collective-permute-done.refs_2_
  10.8 2.9 %shard_map.37.refs_5_ = f32[32,64,128]{2,1,0:T(8,128)S(1)} custom-call(f32[8,32,256]{2,1,0:T(8,128)S(1)} %copy-done, f32[2,64,256]{2,1,0:T(8,128)S(1)} %broadcast_select_fusion.refs_1_, f32[2,64,256]{2,1,0:T(8,128)S(1)} %collective-permute-done.refs_2_), custom_call_target="tpu_custom_call" | custom-call | flops 536870912 | bytes 4194304 | tf_op jit(solution)/shard_map/pallas_call | solution.py:296
  13.7 0.3 collective-permute-done.3.refs_5_
  14.0 0.0 collective-permute-start.5
  14.0 0.0 collective-permute-done.2.refs_4_
  14.0 0.1 select_select_fusion
  14.1 0.2 collective-permute-start.7
  14.4 1.6 %collective-permute-start.4 = (f32[2,64,256]{2,1,0:T(8,128)S(1)}, f32[2,64,256]{2,1,0:T(8,128)S(1)}, u32[]{:S(2)}, u32[]{:S(2)}) collective-permute-start(f32[2,64,256]{2,1,0:T(8,128)S(1)} %collective-permute-done.3.refs_5_), channel_id=1, source_target_pairs={{0,1},{1,0},{2,3},{3,2},{4,5},{5,4},{6,7},{7,6},{8,9},{9,8},{10,11... | collective-permute-start | bytes 393224 | tf_op jit(solution)/shard_map/ppermute | solution.py:345
  16.0 2.6 %shard_map.38.refs_9_ = f32[32,64,128]{2,1,0:T(8,128)S(1)} custom-call(f32[8,32,256]{2,1,0:T(8,128)S(1)} %copy-done, f32[2,64,256]{2,1,0:T(8,128)S(1)} %broadcast_select_fusion.refs_1_, f32[2,64,256]{2,1,0:T(8,128)S(1)} %collective-permute-done.refs_2_, f32[2,64,256]{2,1,0:T(8,128)S(1)} %collective-permute-done.1.refs_3_, ...), custom_call_target="tpu_custom_call" | custom-call | flops 536870912 | bytes 4194304 | tf_op jit(solution)/shard_map/pallas_call | solution.py:296
  18.6 0.3 collective-permute-done.5.refs_7_
  19.0 0.6 %collective-permute-start.6 = (f32[2,64,256]{2,1,0:T(8,128)S(1)}, f32[2,64,256]{2,1,0:T(8,128)S(1)}, u32[]{:S(2)}, u32[]{:S(2)}) collective-permute-start(f32[2,64,256]{2,1,0:T(8,128)S(1)} %collective-permute-done.5.refs_7_), channel_id=1, source_target_pairs={{0,1},{1,0},{2,3},{3,2},{4,5},{5,4},{6,7},{7,6},{8,9},{9,8},{10,11... | collective-permute-start | bytes 393224 | tf_op jit(solution)/shard_map/ppermute | solution.py:345
  19.6 0.5 %collective-permute-done.4.refs_6_ = f32[2,64,256]{2,1,0:T(8,128)S(1)} collective-permute-done((f32[2,64,256]{2,1,0:T(8,128)S(1)}, f32[2,64,256]{2,1,0:T(8,128)S(1)}, u32[]{:S(2)}, u32[]{:S(2)}) %collective-permute-start.4) | collective-permute-done | bytes 131104 | tf_op jit(solution)/shard_map/ppermute | solution.py:345
  20.1 3.5 %shard_map.39.refs_10_ = f32[32,64,128]{2,1,0:T(8,128)S(1)} custom-call(f32[8,32,256]{2,1,0:T(8,128)S(1)} %copy-done, f32[2,64,256]{2,1,0:T(8,128)S(1)} %broadcast_select_fusion.refs_1_, f32[2,64,256]{2,1,0:T(8,128)S(1)} %collective-permute-done.refs_2_, f32[2,64,256]{2,1,0:T(8,128)S(1)} %collective-permute-done.1.refs_3_, ...), custom_call_target="tpu_custom_call" | custom-call | flops 536870912 | bytes 4194304 | tf_op jit(solution)/shard_map/pallas_call | solution.py:296
  23.6 0.7 %collective-permute-done.6.refs_8_ = f32[2,64,256]{2,1,0:T(8,128)S(1)} collective-permute-done((f32[2,64,256]{2,1,0:T(8,128)S(1)}, f32[2,64,256]{2,1,0:T(8,128)S(1)}, u32[]{:S(2)}, u32[]{:S(2)}) %collective-permute-start.6) | collective-permute-done | bytes 131104 | tf_op jit(solution)/shard_map/ppermute | solution.py:345
  24.3 1.7 %shard_map.40 = (f32[1,32,1024]{2,1,0:T(8,128)S(1)}, f32[1,32,1024]{2,1,0:T(8,128)S(1)}) custom-call(f32[8,32,256]{2,1,0:T(8,128)S(1)} %copy-done, f32[2,64,256]{2,1,0:T(8,128)S(1)} %broadcast_select_fusion.refs_1_, f32[2,64,256]{2,1,0:T(8,128)S(1)} %collective-permute-done.refs_2_, f32[2,64,256]{2,1,0:T(8,128)S(1)} %collective-permute-done.1.refs_3_, ...), custom_call_target="tpu_custom_call" | custom-call | flops 536870912 | bytes 4194304 | tf_op jit(solution)/shard_map/pallas_call | solution.py:296
  26.0 0.1 collective-permute-start.8
  26.1 1.3 %collective-permute-done.8 = f32[1,32,1024]{2,1,0:T(8,128)S(1)} collective-permute-done((f32[1,32,1024]{2,1,0:T(8,128)S(1)}, f32[1,32,1024]{2,1,0:T(8,128)S(1)}, u32[]{:S(2)}, u32[]{:S(2)}) %collective-permute-start.8) | collective-permute-done | bytes 131104 | tf_op jit(solution)/shard_map/ppermute | solution.py:345
  27.4 1.6 %collective-permute-start.11 = (f32[1,32,1024]{2,1,0:T(8,128)S(1)}, f32[1,32,1024]{2,1,0:T(8,128)S(1)}, u32[]{:S(2)}, u32[]{:S(2)}) collective-permute-start(f32[1,32,1024]{2,1,0:T(8,128)S(1)} %add.15), channel_id=1, source_target_pairs={{0,16},{8,24},{16,0},{24,8},{1,17},{9,25},{17,1},{25,9},{2,18},{10... | collective-permute-start | bytes 393224 | tf_op jit(solution)/shard_map/ppermute | solution.py:345
  29.0 2.2 %shard_map.41 = (f32[1,32,1024]{2,1,0:T(8,128)S(1)}, f32[1,32,1024]{2,1,0:T(8,128)S(1)}) custom-call(f32[8,32,256]{2,1,0:T(8,128)S(1)} %copy-done, f32[2,64,256]{2,1,0:T(8,128)S(1)} %broadcast_select_fusion.refs_1_, f32[2,64,256]{2,1,0:T(8,128)S(1)} %collective-permute-done.refs_2_, f32[2,64,256]{2,1,0:T(8,128)S(1)} %collective-permute-done.1.refs_3_, ...), custom_call_target="tpu_custom_call" | custom-call | tf_op jit(solution)/shard_map/pallas_call | solution.py:296
  31.1 0.1 collective-permute-start.10
  31.2 0.5 %collective-permute-start.9 = (f32[1,16,1024]{2,1,0:T(8,128)S(1)}, f32[1,16,1024]{2,1,0:T(8,128)S(1)}, u32[]{:S(2)}, u32[]{:S(2)}) collective-permute-start(f32[1,16,1024]{2,1,0:T(8,128)S(1)} %get-tuple-element.21), channel_id=1, source_target_pairs={{0,8},{8,0},{16,24},{24,16},{1,9},{9,1},{17,25},{25,17},{2,10},{10... | collective-permute-start | bytes 196616 | tf_op jit(solution)/shard_map/ppermute | solution.py:345
  31.7 0.7 %collective-permute-done.10 = f32[1,16,1024]{2,1,0:T(8,128)S(1)} collective-permute-done((f32[1,16,1024]{2,1,0:T(8,128)S(1)}, f32[1,16,1024]{2,1,0:T(8,128)S(1)}, u32[]{:S(2)}, u32[]{:S(2)}) %collective-permute-start.10) | collective-permute-done | bytes 65568 | tf_op jit(solution)/shard_map/ppermute | solution.py:345
  32.5 0.2 collective-permute-done.9
  32.6 0.4 %collective-permute-done.11 = f32[1,32,1024]{2,1,0:T(8,128)S(1)} collective-permute-done((f32[1,32,1024]{2,1,0:T(8,128)S(1)}, f32[1,32,1024]{2,1,0:T(8,128)S(1)}, u32[]{:S(2)}, u32[]{:S(2)}) %collective-permute-start.11) | collective-permute-done | bytes 131104 | tf_op jit(solution)/shard_map/ppermute | solution.py:345
  33.0 0.7 %fusion.1 = f32[32,1024]{1,0:T(8,128)} fusion(f32[1,32,1024]{2,1,0:T(8,128)S(1)} %collective-permute-done.11, f32[1,32,1024]{2,1,0:T(8,128)S(1)} %get-tuple-element.19, f32[1,16,1024]{2,1,0:T(8,128)S(1)} %collective-permute-done.10, f32[1,16,1024]{2,1,0:T(8,128)S(1)} %collective-permute-done.9), kind=kLoop, calls=%fused_computation.3 | loop fusion | flops 98304 | bytes 524288 | tf_op jit(solution)/shard_map/squeeze | solution.py:422
  (11 shorter events, 0.1 us)
Async XLA Ops:
  0.0 10.8 %copy-start = (f32[8,32,256]{2,1,0:T(8,128)S(1)}, f32[8,32,256]{2,1,0:T(8,128)}, u32[]{:S(2)}) copy-start(f32[8,32,256]{2,1,0:T(8,128)} %refs_0_.9) | copy-start | bytes 786436
  1.0 7.2 %collective-permute-start.1 = (f32[2,64,256]{2,1,0:T(8,128)S(1)}, f32[2,64,256]{2,1,0:T(8,128)S(1)}, u32[]{:S(2)}, u32[]{:S(2)}) collective-permute-start(f32[2,64,256]{2,1,0:T(8,128)S(1)} %broadcast_select_fusion.refs_1_), channel_id=1, source_target_pairs={{0,2},{1,3},{2,0},{3,1},{4,6},{5,7},{6,4},{7,5},{8,10},{9,11},{10,... | collective-permute-start | bytes 393224 | tf_op jit(solution)/shard_map/ppermute | solution.py:345
  4.1 6.7 %collective-permute-start = (f32[2,64,256]{2,1,0:T(8,128)S(1)}, f32[2,64,256]{2,1,0:T(8,128)S(1)}, u32[]{:S(2)}, u32[]{:S(2)}) collective-permute-start(f32[2,64,256]{2,1,0:T(8,128)S(1)} %broadcast_select_fusion.refs_1_), channel_id=1, source_target_pairs={{0,1},{1,0},{2,3},{3,2},{4,5},{5,4},{6,7},{7,6},{8,9},{9,8},{10,11... | collective-permute-start | bytes 393224 | tf_op jit(solution)/shard_map/ppermute | solution.py:345
  5.6 8.4 %collective-permute-start.3 = (f32[2,64,256]{2,1,0:T(8,128)S(1)}, f32[2,64,256]{2,1,0:T(8,128)S(1)}, u32[]{:S(2)}, u32[]{:S(2)}) collective-permute-start(f32[2,64,256]{2,1,0:T(8,128)S(1)} %broadcast_select_fusion.refs_1_), channel_id=1, source_target_pairs={{0,4},{1,5},{2,6},{3,7},{4,0},{5,1},{6,2},{7,3},{8,12},{9,13},{10,... | collective-permute-start | bytes 393224 | tf_op jit(solution)/shard_map/ppermute | solution.py:345
  8.2 5.8 %collective-permute-start.2 = (f32[2,64,256]{2,1,0:T(8,128)S(1)}, f32[2,64,256]{2,1,0:T(8,128)S(1)}, u32[]{:S(2)}, u32[]{:S(2)}) collective-permute-start(f32[2,64,256]{2,1,0:T(8,128)S(1)} %collective-permute-done.1.refs_3_), channel_id=1, source_target_pairs={{0,1},{1,0},{2,3},{3,2},{4,5},{5,4},{6,7},{7,6},{8,9},{9,8},{10,11... | collective-permute-start | bytes 393224 | tf_op jit(solution)/shard_map/ppermute | solution.py:345
  10.8 3.2 %copy-start.1 = (f32[1,64,256]{2,1,0:T(8,128)S(1)}, f32[1,64,256]{2,1,0:T(8,128)}, u32[]{:S(2)}) copy-start(f32[1,64,256]{2,1,0:T(8,128)} %param.4) | copy-start | bytes 196612
  10.8 3.2 %copy-start.2 = (f32[1,64,256]{2,1,0:T(8,128)S(1)}, f32[1,64,256]{2,1,0:T(8,128)}, u32[]{:S(2)}) copy-start(f32[1,64,256]{2,1,0:T(8,128)} %param.3) | copy-start | bytes 196612
  14.0 5.0 %collective-permute-start.5 = (f32[2,64,256]{2,1,0:T(8,128)S(1)}, f32[2,64,256]{2,1,0:T(8,128)S(1)}, u32[]{:S(2)}, u32[]{:S(2)}) collective-permute-start(f32[2,64,256]{2,1,0:T(8,128)S(1)} %collective-permute-done.3.refs_5_), channel_id=1, source_target_pairs={{0,2},{1,3},{2,0},{3,1},{4,6},{5,7},{6,4},{7,5},{8,10},{9,11},{10,... | collective-permute-start | bytes 393224 | tf_op jit(solution)/shard_map/ppermute | solution.py:345
  14.1 6.0 %collective-permute-start.7 = (f32[160,256]{1,0:T(8,128)S(1)}, f32[160,256]{1,0:T(8,128)S(1)}, u32[]{:S(2)}, u32[]{:S(2)}) collective-permute-start(f32[160,256]{1,0:T(8,128)S(1)} %pad_maximum_fusion), channel_id=1, source_target_pairs={{8,0},{9,1},{10,2},{11,3},{4,12},{5,13},{6,14},{7,15},{16,8},{17,9... | collective-permute-start | bytes 491528 | tf_op jit(solution)/shard_map/ppermute | solution.py:401
  14.4 5.7 %collective-permute-start.4 = (f32[2,64,256]{2,1,0:T(8,128)S(1)}, f32[2,64,256]{2,1,0:T(8,128)S(1)}, u32[]{:S(2)}, u32[]{:S(2)}) collective-permute-start(f32[2,64,256]{2,1,0:T(8,128)S(1)} %collective-permute-done.3.refs_5_), channel_id=1, source_target_pairs={{0,1},{1,0},{2,3},{3,2},{4,5},{5,4},{6,7},{7,6},{8,9},{9,8},{10,11... | collective-permute-start | bytes 393224 | tf_op jit(solution)/shard_map/ppermute | solution.py:345
  19.0 5.3 %collective-permute-start.6 = (f32[2,64,256]{2,1,0:T(8,128)S(1)}, f32[2,64,256]{2,1,0:T(8,128)S(1)}, u32[]{:S(2)}, u32[]{:S(2)}) collective-permute-start(f32[2,64,256]{2,1,0:T(8,128)S(1)} %collective-permute-done.5.refs_7_), channel_id=1, source_target_pairs={{0,1},{1,0},{2,3},{3,2},{4,5},{5,4},{6,7},{7,6},{8,9},{9,8},{10,11... | collective-permute-start | bytes 393224 | tf_op jit(solution)/shard_map/ppermute | solution.py:345
  26.0 1.4 %collective-permute-start.8 = (f32[1,32,1024]{2,1,0:T(8,128)S(1)}, f32[1,32,1024]{2,1,0:T(8,128)S(1)}, u32[]{:S(2)}, u32[]{:S(2)}) collective-permute-start(f32[1,32,1024]{2,1,0:T(8,128)S(1)} %get-tuple-element.17), channel_id=1, source_target_pairs={{0,8},{8,0},{16,24},{24,16},{1,9},{9,1},{17,25},{25,17},{2,10},{10... | collective-permute-start | bytes 393224 | tf_op jit(solution)/shard_map/ppermute | solution.py:345
  27.4 5.6 %collective-permute-start.11 = (f32[1,32,1024]{2,1,0:T(8,128)S(1)}, f32[1,32,1024]{2,1,0:T(8,128)S(1)}, u32[]{:S(2)}, u32[]{:S(2)}) collective-permute-start(f32[1,32,1024]{2,1,0:T(8,128)S(1)} %add.15), channel_id=1, source_target_pairs={{0,16},{8,24},{16,0},{24,8},{1,17},{9,25},{17,1},{25,9},{2,18},{10... | collective-permute-start | bytes 393224 | tf_op jit(solution)/shard_map/ppermute | solution.py:345
  31.1 1.3 %collective-permute-start.10 = (f32[1,16,1024]{2,1,0:T(8,128)S(1)}, f32[1,16,1024]{2,1,0:T(8,128)S(1)}, u32[]{:S(2)}, u32[]{:S(2)}) collective-permute-start(f32[1,16,1024]{2,1,0:T(8,128)S(1)} %get-tuple-element.22), channel_id=1, source_target_pairs={{0,8},{8,0},{16,24},{24,16},{1,9},{9,1},{17,25},{25,17},{2,10},{10... | collective-permute-start | bytes 196616 | tf_op jit(solution)/shard_map/ppermute | solution.py:345
  31.2 1.4 %collective-permute-start.9 = (f32[1,16,1024]{2,1,0:T(8,128)S(1)}, f32[1,16,1024]{2,1,0:T(8,128)S(1)}, u32[]{:S(2)}, u32[]{:S(2)}) collective-permute-start(f32[1,16,1024]{2,1,0:T(8,128)S(1)} %get-tuple-element.21), channel_id=1, source_target_pairs={{0,8},{8,0},{16,24},{24,16},{1,9},{9,1},{17,25},{25,17},{2,10},{10... | collective-permute-start | bytes 196616 | tf_op jit(solution)/shard_map/ppermute | solution.py:345

commit v6 on v5

--- a/solution.py
+++ b/solution.py
@@ -272,10 +272,10 @@
                 rows[planes + slot].append(part[d])
         weight = jnp.concatenate([w_ref[m] for m in range(planes + 2)], 1)
         out = product(rows, weight).reshape(terms, step, 2 * modes)
-        acc_ref[:, index * step : (index + 1) * step] = before_ref[:, at] + out
+        acc_ref[:terms, index * step : (index + 1) * step] = before_ref[:, at] + out
 
     core = space_at % 2
-    flat_ref = acc_ref.reshape(terms * (modes // 2), 2 * modes)
+    flat_ref = acc_ref.reshape((terms + 1) * (modes // 2), 2 * modes)
     lane = lax.broadcasted_iota(jnp.int32, (terms, 2 * modes), 1)
     for index in range(n_space // 4):
         for j in range(width // 2):
@@ -330,7 +330,7 @@
     modes, cells = blocks[0].shape[1:]
     terms = coeffs.shape[1]
     scratch = [
-        pltpu.VMEM((terms, modes // 2, 2 * modes), F32),
+        pltpu.VMEM((terms + 1, modes // 2, 2 * modes), F32),
         pltpu.VMEM((11, modes, cells), F32),
         pltpu.VMEM((11, terms, cells), F32),
         pltpu.VMEM((4, 2 * modes, 2 * cells), BF16),

time: 33.8 us -> 33.8 us (level)
  no operation moved by 1% of the time
where the time goes in v6:
time: 33.8 us; the launch traced here: 33.7 us
  starting transfers between devices  14.4 us (43%)
  Pallas kernels  12.9 us (38%)
  waiting for transfers between devices  4.48 us (13%)
  other arithmetic  1.8 us (5%)
    ppermute x11, starting transfers between devices, exchange(): return lax.ppermute(values, axis, [(i, i ^ apart) for i in range(count)])  14.2 us
    pallas_call x5, Pallas kernels, call(): pl.pallas_call(kernel, out_shape=out_shape, in_specs=[whole] * len(operan...  12.9 us
    ppermute x11, waiting for transfers between devices, exchange(): return lax.ppermute(values, axis, [(i, i ^ apart) for i in range(count)])  4.48 us
    select_n x1, other arithmetic, local(): own = jnp.where(which == 0, right_modes, adjoint_modes)  0.99 us
    squeeze x1, other arithmetic, local(): return total[0]  0.68 us
  transfers between devices with their start and end apart: 12, of which 8 were waited for; matrix products, arithmetic and copies ran while one was open for 0% of the time, Pallas kernels for 33%

profile of v6, /device:TPU:0, one launch (start us, length us, event | category | flops | bytes accessed | tf_op | source)
XLA Modules:
  0.0 33.7 jit_solution(8309543010944464392)
XLA Ops:
  0.0 1.0 %broadcast_select_fusion.refs_1_ = f32[2,64,256]{2,1,0:T(8,128)S(1)} fusion(f32[64,256]{1,0:T(8,128)} %bitcast.8, f32[64,256]{1,0:T(8,128)} %bitcast.10, pred[2]{0:T(512)(128)(4,1)S(1)} %iota_compare_fusion), kind=kLoop, calls=%fused_computation.5 | loop fusion | flops 32768 | bytes 262146 | tf_op jit(solution)/shard_map/jit(_where)/select_n | solution.py:366
  1.0 3.1 %collective-permute-start.1 = (f32[2,64,256]{2,1,0:T(8,128)S(1)}, f32[2,64,256]{2,1,0:T(8,128)S(1)}, u32[]{:S(2)}, u32[]{:S(2)}) collective-permute-start(f32[2,64,256]{2,1,0:T(8,128)S(1)} %broadcast_select_fusion.refs_1_), channel_id=1, source_target_pairs={{0,2},{1,3},{2,0},{3,1},{4,6},{5,7},{6,4},{7,5},{8,10},{9,11},{10,... | collective-permute-start | bytes 393224 | tf_op jit(solution)/shard_map/ppermute | solution.py:345
  4.1 1.5 %collective-permute-start = (f32[2,64,256]{2,1,0:T(8,128)S(1)}, f32[2,64,256]{2,1,0:T(8,128)S(1)}, u32[]{:S(2)}, u32[]{:S(2)}) collective-permute-start(f32[2,64,256]{2,1,0:T(8,128)S(1)} %broadcast_select_fusion.refs_1_), channel_id=1, source_target_pairs={{0,1},{1,0},{2,3},{3,2},{4,5},{5,4},{6,7},{7,6},{8,9},{9,8},{10,11... | collective-permute-start | bytes 393224 | tf_op jit(solution)/shard_map/ppermute | solution.py:345
  5.6 2.6 %collective-permute-start.3 = (f32[2,64,256]{2,1,0:T(8,128)S(1)}, f32[2,64,256]{2,1,0:T(8,128)S(1)}, u32[]{:S(2)}, u32[]{:S(2)}) collective-permute-start(f32[2,64,256]{2,1,0:T(8,128)S(1)} %broadcast_select_fusion.refs_1_), channel_id=1, source_target_pairs={{0,4},{1,5},{2,6},{3,7},{4,0},{5,1},{6,2},{7,3},{8,12},{9,13},{10,... | collective-permute-start | bytes 393224 | tf_op jit(solution)/shard_map/ppermute | solution.py:345
  8.2 2.6 %collective-permute-start.2 = (f32[2,64,256]{2,1,0:T(8,128)S(1)}, f32[2,64,256]{2,1,0:T(8,128)S(1)}, u32[]{:S(2)}, u32[]{:S(2)}) collective-permute-start(f32[2,64,256]{2,1,0:T(8,128)S(1)} %collective-permute-done.1.refs_3_), channel_id=1, source_target_pairs={{0,1},{1,0},{2,3},{3,2},{4,5},{5,4},{6,7},{7,6},{8,9},{9,8},{10,11... | collective-permute-start | bytes 393224 | tf_op jit(solution)/shard_map/ppermute | solution.py:345
  10.8 0.0 copy-start.1
  10.8 0.0 copy-start.2
  10.8 0.0 collective-permute-done.refs_2_
  10.8 2.9 %shard_map.37.refs_5_ = f32[32,64,128]{2,1,0:T(8,128)S(1)} custom-call(f32[8,32,256]{2,1,0:T(8,128)S(1)} %copy-done, f32[2,64,256]{2,1,0:T(8,128)S(1)} %broadcast_select_fusion.refs_1_, f32[2,64,256]{2,1,0:T(8,128)S(1)} %collective-permute-done.refs_2_), custom_call_target="tpu_custom_call" | custom-call | flops 536870912 | bytes 4194304 | tf_op jit(solution)/shard_map/pallas_call | solution.py:296
  13.7 0.3 collective-permute-done.3.refs_5_
  14.0 0.0 collective-permute-start.5
  14.0 0.0 collective-permute-done.2.refs_4_
  14.0 0.1 select_select_fusion
  14.1 0.2 collective-permute-start.7
  14.4 1.6 %collective-permute-start.4 = (f32[2,64,256]{2,1,0:T(8,128)S(1)}, f32[2,64,256]{2,1,0:T(8,128)S(1)}, u32[]{:S(2)}, u32[]{:S(2)}) collective-permute-start(f32[2,64,256]{2,1,0:T(8,128)S(1)} %collective-permute-done.3.refs_5_), channel_id=1, source_target_pairs={{0,1},{1,0},{2,3},{3,2},{4,5},{5,4},{6,7},{7,6},{8,9},{9,8},{10,11... | collective-permute-start | bytes 393224 | tf_op jit(solution)/shard_map/ppermute | solution.py:345
  16.0 2.6 %shard_map.38.refs_9_ = f32[32,64,128]{2,1,0:T(8,128)S(1)} custom-call(f32[8,32,256]{2,1,0:T(8,128)S(1)} %copy-done, f32[2,64,256]{2,1,0:T(8,128)S(1)} %broadcast_select_fusion.refs_1_, f32[2,64,256]{2,1,0:T(8,128)S(1)} %collective-permute-done.refs_2_, f32[2,64,256]{2,1,0:T(8,128)S(1)} %collective-permute-done.1.refs_3_, ...), custom_call_target="tpu_custom_call" | custom-call | flops 536870912 | bytes 4194304 | tf_op jit(solution)/shard_map/pallas_call | solution.py:296
  18.6 0.3 collective-permute-done.5.refs_7_
  19.0 0.6 %collective-permute-start.6 = (f32[2,64,256]{2,1,0:T(8,128)S(1)}, f32[2,64,256]{2,1,0:T(8,128)S(1)}, u32[]{:S(2)}, u32[]{:S(2)}) collective-permute-start(f32[2,64,256]{2,1,0:T(8,128)S(1)} %collective-permute-done.5.refs_7_), channel_id=1, source_target_pairs={{0,1},{1,0},{2,3},{3,2},{4,5},{5,4},{6,7},{7,6},{8,9},{9,8},{10,11... | collective-permute-start | bytes 393224 | tf_op jit(solution)/shard_map/ppermute | solution.py:345
  19.6 0.5 %collective-permute-done.4.refs_6_ = f32[2,64,256]{2,1,0:T(8,128)S(1)} collective-permute-done((f32[2,64,256]{2,1,0:T(8,128)S(1)}, f32[2,64,256]{2,1,0:T(8,128)S(1)}, u32[]{:S(2)}, u32[]{:S(2)}) %collective-permute-start.4) | collective-permute-done | bytes 131104 | tf_op jit(solution)/shard_map/ppermute | solution.py:345
  20.1 3.5 %shard_map.39.refs_10_ = f32[32,64,128]{2,1,0:T(8,128)S(1)} custom-call(f32[8,32,256]{2,1,0:T(8,128)S(1)} %copy-done, f32[2,64,256]{2,1,0:T(8,128)S(1)} %broadcast_select_fusion.refs_1_, f32[2,64,256]{2,1,0:T(8,128)S(1)} %collective-permute-done.refs_2_, f32[2,64,256]{2,1,0:T(8,128)S(1)} %collective-permute-done.1.refs_3_, ...), custom_call_target="tpu_custom_call" | custom-call | flops 536870912 | bytes 4194304 | tf_op jit(solution)/shard_map/pallas_call | solution.py:296
  23.6 0.7 %collective-permute-done.6.refs_8_ = f32[2,64,256]{2,1,0:T(8,128)S(1)} collective-permute-done((f32[2,64,256]{2,1,0:T(8,128)S(1)}, f32[2,64,256]{2,1,0:T(8,128)S(1)}, u32[]{:S(2)}, u32[]{:S(2)}) %collective-permute-start.6) | collective-permute-done | bytes 131104 | tf_op jit(solution)/shard_map/ppermute | solution.py:345
  24.3 1.7 %shard_map.40 = (f32[1,32,1024]{2,1,0:T(8,128)S(1)}, f32[1,32,1024]{2,1,0:T(8,128)S(1)}) custom-call(f32[8,32,256]{2,1,0:T(8,128)S(1)} %copy-done, f32[2,64,256]{2,1,0:T(8,128)S(1)} %broadcast_select_fusion.refs_1_, f32[2,64,256]{2,1,0:T(8,128)S(1)} %collective-permute-done.refs_2_, f32[2,64,256]{2,1,0:T(8,128)S(1)} %collective-permute-done.1.refs_3_, ...), custom_call_target="tpu_custom_call" | custom-call | flops 536870912 | bytes 4194304 | tf_op jit(solution)/shard_map/pallas_call | solution.py:296
  26.0 0.1 collective-permute-start.8
  26.1 1.3 %collective-permute-done.8 = f32[1,32,1024]{2,1,0:T(8,128)S(1)} collective-permute-done((f32[1,32,1024]{2,1,0:T(8,128)S(1)}, f32[1,32,1024]{2,1,0:T(8,128)S(1)}, u32[]{:S(2)}, u32[]{:S(2)}) %collective-permute-start.8) | collective-permute-done | bytes 131104 | tf_op jit(solution)/shard_map/ppermute | solution.py:345
  27.4 1.6 %collective-permute-start.11 = (f32[1,32,1024]{2,1,0:T(8,128)S(1)}, f32[1,32,1024]{2,1,0:T(8,128)S(1)}, u32[]{:S(2)}, u32[]{:S(2)}) collective-permute-start(f32[1,32,1024]{2,1,0:T(8,128)S(1)} %add.15), channel_id=1, source_target_pairs={{0,16},{8,24},{16,0},{24,8},{1,17},{9,25},{17,1},{25,9},{2,18},{10... | collective-permute-start | bytes 393224 | tf_op jit(solution)/shard_map/ppermute | solution.py:345
  29.0 2.2 %shard_map.41 = (f32[1,32,1024]{2,1,0:T(8,128)S(1)}, f32[1,32,1024]{2,1,0:T(8,128)S(1)}) custom-call(f32[8,32,256]{2,1,0:T(8,128)S(1)} %copy-done, f32[2,64,256]{2,1,0:T(8,128)S(1)} %broadcast_select_fusion.refs_1_, f32[2,64,256]{2,1,0:T(8,128)S(1)} %collective-permute-done.refs_2_, f32[2,64,256]{2,1,0:T(8,128)S(1)} %collective-permute-done.1.refs_3_, ...), custom_call_target="tpu_custom_call" | custom-call | tf_op jit(solution)/shard_map/pallas_call | solution.py:296
  31.1 0.1 collective-permute-start.10
  31.2 0.5 %collective-permute-start.9 = (f32[1,16,1024]{2,1,0:T(8,128)S(1)}, f32[1,16,1024]{2,1,0:T(8,128)S(1)}, u32[]{:S(2)}, u32[]{:S(2)}) collective-permute-start(f32[1,16,1024]{2,1,0:T(8,128)S(1)} %get-tuple-element.21), channel_id=1, source_target_pairs={{0,8},{8,0},{16,24},{24,16},{1,9},{9,1},{17,25},{25,17},{2,10},{10... | collective-permute-start | bytes 196616 | tf_op jit(solution)/shard_map/ppermute | solution.py:345
  31.7 0.7 %collective-permute-done.10 = f32[1,16,1024]{2,1,0:T(8,128)S(1)} collective-permute-done((f32[1,16,1024]{2,1,0:T(8,128)S(1)}, f32[1,16,1024]{2,1,0:T(8,128)S(1)}, u32[]{:S(2)}, u32[]{:S(2)}) %collective-permute-start.10) | collective-permute-done | bytes 65568 | tf_op jit(solution)/shard_map/ppermute | solution.py:345
  32.5 0.2 collective-permute-done.9
  32.6 0.4 %collective-permute-done.11 = f32[1,32,1024]{2,1,0:T(8,128)S(1)} collective-permute-done((f32[1,32,1024]{2,1,0:T(8,128)S(1)}, f32[1,32,1024]{2,1,0:T(8,128)S(1)}, u32[]{:S(2)}, u32[]{:S(2)}) %collective-permute-start.11) | collective-permute-done | bytes 131104 | tf_op jit(solution)/shard_map/ppermute | solution.py:345
  33.0 0.7 %fusion.1 = f32[32,1024]{1,0:T(8,128)} fusion(f32[1,32,1024]{2,1,0:T(8,128)S(1)} %collective-permute-done.11, f32[1,32,1024]{2,1,0:T(8,128)S(1)} %get-tuple-element.19, f32[1,16,1024]{2,1,0:T(8,128)S(1)} %collective-permute-done.10, f32[1,16,1024]{2,1,0:T(8,128)S(1)} %collective-permute-done.9), kind=kLoop, calls=%fused_computation.3 | loop fusion | flops 98304 | bytes 524288 | tf_op jit(solution)/shard_map/squeeze | solution.py:422
  (11 shorter events, 0.1 us)
Async XLA Ops:
  0.0 10.8 %copy-start = (f32[8,32,256]{2,1,0:T(8,128)S(1)}, f32[8,32,256]{2,1,0:T(8,128)}, u32[]{:S(2)}) copy-start(f32[8,32,256]{2,1,0:T(8,128)} %refs_0_.9) | copy-start | bytes 786436
  1.0 7.2 %collective-permute-start.1 = (f32[2,64,256]{2,1,0:T(8,128)S(1)}, f32[2,64,256]{2,1,0:T(8,128)S(1)}, u32[]{:S(2)}, u32[]{:S(2)}) collective-permute-start(f32[2,64,256]{2,1,0:T(8,128)S(1)} %broadcast_select_fusion.refs_1_), channel_id=1, source_target_pairs={{0,2},{1,3},{2,0},{3,1},{4,6},{5,7},{6,4},{7,5},{8,10},{9,11},{10,... | collective-permute-start | bytes 393224 | tf_op jit(solution)/shard_map/ppermute | solution.py:345
  4.1 6.7 %collective-permute-start = (f32[2,64,256]{2,1,0:T(8,128)S(1)}, f32[2,64,256]{2,1,0:T(8,128)S(1)}, u32[]{:S(2)}, u32[]{:S(2)}) collective-permute-start(f32[2,64,256]{2,1,0:T(8,128)S(1)} %broadcast_select_fusion.refs_1_), channel_id=1, source_target_pairs={{0,1},{1,0},{2,3},{3,2},{4,5},{5,4},{6,7},{7,6},{8,9},{9,8},{10,11... | collective-permute-start | bytes 393224 | tf_op jit(solution)/shard_map/ppermute | solution.py:345
  5.6 8.4 %collective-permute-start.3 = (f32[2,64,256]{2,1,0:T(8,128)S(1)}, f32[2,64,256]{2,1,0:T(8,128)S(1)}, u32[]{:S(2)}, u32[]{:S(2)}) collective-permute-start(f32[2,64,256]{2,1,0:T(8,128)S(1)} %broadcast_select_fusion.refs_1_), channel_id=1, source_target_pairs={{0,4},{1,5},{2,6},{3,7},{4,0},{5,1},{6,2},{7,3},{8,12},{9,13},{10,... | collective-permute-start | bytes 393224 | tf_op jit(solution)/shard_map/ppermute | solution.py:345
  8.2 5.8 %collective-permute-start.2 = (f32[2,64,256]{2,1,0:T(8,128)S(1)}, f32[2,64,256]{2,1,0:T(8,128)S(1)}, u32[]{:S(2)}, u32[]{:S(2)}) collective-permute-start(f32[2,64,256]{2,1,0:T(8,128)S(1)} %collective-permute-done.1.refs_3_), channel_id=1, source_target_pairs={{0,1},{1,0},{2,3},{3,2},{4,5},{5,4},{6,7},{7,6},{8,9},{9,8},{10,11... | collective-permute-start | bytes 393224 | tf_op jit(solution)/shard_map/ppermute | solution.py:345
  10.8 3.2 %copy-start.1 = (f32[1,64,256]{2,1,0:T(8,128)S(1)}, f32[1,64,256]{2,1,0:T(8,128)}, u32[]{:S(2)}) copy-start(f32[1,64,256]{2,1,0:T(8,128)} %param.4) | copy-start | bytes 196612
  10.8 3.2 %copy-start.2 = (f32[1,64,256]{2,1,0:T(8,128)S(1)}, f32[1,64,256]{2,1,0:T(8,128)}, u32[]{:S(2)}) copy-start(f32[1,64,256]{2,1,0:T(8,128)} %param.3) | copy-start | bytes 196612
  14.0 5.0 %collective-permute-start.5 = (f32[2,64,256]{2,1,0:T(8,128)S(1)}, f32[2,64,256]{2,1,0:T(8,128)S(1)}, u32[]{:S(2)}, u32[]{:S(2)}) collective-permute-start(f32[2,64,256]{2,1,0:T(8,128)S(1)} %collective-permute-done.3.refs_5_), channel_id=1, source_target_pairs={{0,2},{1,3},{2,0},{3,1},{4,6},{5,7},{6,4},{7,5},{8,10},{9,11},{10,... | collective-permute-start | bytes 393224 | tf_op jit(solution)/shard_map/ppermute | solution.py:345
  14.1 6.0 %collective-permute-start.7 = (f32[160,256]{1,0:T(8,128)S(1)}, f32[160,256]{1,0:T(8,128)S(1)}, u32[]{:S(2)}, u32[]{:S(2)}) collective-permute-start(f32[160,256]{1,0:T(8,128)S(1)} %pad_maximum_fusion), channel_id=1, source_target_pairs={{8,0},{9,1},{10,2},{11,3},{4,12},{5,13},{6,14},{7,15},{16,8},{17,9... | collective-permute-start | bytes 491528 | tf_op jit(solution)/shard_map/ppermute | solution.py:401
  14.4 5.7 %collective-permute-start.4 = (f32[2,64,256]{2,1,0:T(8,128)S(1)}, f32[2,64,256]{2,1,0:T(8,128)S(1)}, u32[]{:S(2)}, u32[]{:S(2)}) collective-permute-start(f32[2,64,256]{2,1,0:T(8,128)S(1)} %collective-permute-done.3.refs_5_), channel_id=1, source_target_pairs={{0,1},{1,0},{2,3},{3,2},{4,5},{5,4},{6,7},{7,6},{8,9},{9,8},{10,11... | collective-permute-start | bytes 393224 | tf_op jit(solution)/shard_map/ppermute | solution.py:345
  19.0 5.3 %collective-permute-start.6 = (f32[2,64,256]{2,1,0:T(8,128)S(1)}, f32[2,64,256]{2,1,0:T(8,128)S(1)}, u32[]{:S(2)}, u32[]{:S(2)}) collective-permute-start(f32[2,64,256]{2,1,0:T(8,128)S(1)} %collective-permute-done.5.refs_7_), channel_id=1, source_target_pairs={{0,1},{1,0},{2,3},{3,2},{4,5},{5,4},{6,7},{7,6},{8,9},{9,8},{10,11... | collective-permute-start | bytes 393224 | tf_op jit(solution)/shard_map/ppermute | solution.py:345
  26.0 1.4 %collective-permute-start.8 = (f32[1,32,1024]{2,1,0:T(8,128)S(1)}, f32[1,32,1024]{2,1,0:T(8,128)S(1)}, u32[]{:S(2)}, u32[]{:S(2)}) collective-permute-start(f32[1,32,1024]{2,1,0:T(8,128)S(1)} %get-tuple-element.17), channel_id=1, source_target_pairs={{0,8},{8,0},{16,24},{24,16},{1,9},{9,1},{17,25},{25,17},{2,10},{10... | collective-permute-start | bytes 393224 | tf_op jit(solution)/shard_map/ppermute | solution.py:345
  27.4 5.6 %collective-permute-start.11 = (f32[1,32,1024]{2,1,0:T(8,128)S(1)}, f32[1,32,1024]{2,1,0:T(8,128)S(1)}, u32[]{:S(2)}, u32[]{:S(2)}) collective-permute-start(f32[1,32,1024]{2,1,0:T(8,128)S(1)} %add.15), channel_id=1, source_target_pairs={{0,16},{8,24},{16,0},{24,8},{1,17},{9,25},{17,1},{25,9},{2,18},{10... | collective-permute-start | bytes 393224 | tf_op jit(solution)/shard_map/ppermute | solution.py:345
  31.1 1.3 %collective-permute-start.10 = (f32[1,16,1024]{2,1,0:T(8,128)S(1)}, f32[1,16,1024]{2,1,0:T(8,128)S(1)}, u32[]{:S(2)}, u32[]{:S(2)}) collective-permute-start(f32[1,16,1024]{2,1,0:T(8,128)S(1)} %get-tuple-element.22), channel_id=1, source_target_pairs={{0,8},{8,0},{16,24},{24,16},{1,9},{9,1},{17,25},{25,17},{2,10},{10... | collective-permute-start | bytes 196616 | tf_op jit(solution)/shard_map/ppermute | solution.py:345
  31.2 1.4 %collective-permute-start.9 = (f32[1,16,1024]{2,1,0:T(8,128)S(1)}, f32[1,16,1024]{2,1,0:T(8,128)S(1)}, u32[]{:S(2)}, u32[]{:S(2)}) collective-permute-start(f32[1,16,1024]{2,1,0:T(8,128)S(1)} %get-tuple-element.21), channel_id=1, source_target_pairs={{0,8},{8,0},{16,24},{24,16},{1,9},{9,1},{17,25},{25,17},{2,10},{10... | collective-permute-start | bytes 196616 | tf_op jit(solution)/shard_map/ppermute | solution.py:345

commit v7 on v6

--- a/solution.py
+++ b/solution.py
@@ -61,9 +61,13 @@
     if extra:
         in_plane.append((blocks[-1], 2 * (z ^ (pairs - 1)) + y))
     for m, (ref, plane) in enumerate(in_plane):
-        a, k = ref[1], k_ref[plane]
+        k = k_ref[plane]
+        size = 2 * modes // n_space
+        for at in half_rows(0, size, size, n_space) if m == 2 else [slice(0, modes)]:
+            a = ref[1][at] if m < 2 else ref[1, at, :]
+            for d, offset in enumerate(OFFSETS):
+                da_ref[4 * m + d, at, :] = a - shifted(a, offset)
         for d, offset in enumerate(OFFSETS):
-            da_ref[4 * m + d] = a - shifted(a, offset)
             kb_ref[4 * m + d] = 0.5 * (k + shifted(k, offset))
         weights(m, ref[0])
     across = 4 * len(in_plane)
@@ -233,9 +237,12 @@
         in_plane.append((column_ref, 2 * w + y))
     planes = len(in_plane)
     for m, (ref, plane) in enumerate(in_plane):
-        a, k = ref[1], k_ref[plane]
+        k = k_ref[plane]
+        for at in half_rows(mine, 2 * modes // n_space, 2 * modes // n_space, n_space):
+            a = ref[1, at, :]
+            for d, offset in enumerate(OFFSETS):
+                da_ref[4 * m + d, at, :] = a - shifted(a, offset)
         for d, offset in enumerate(OFFSETS):
-            da_ref[4 * m + d] = a - shifted(a, offset)
             kb_ref[4 * m + d] = 0.5 * (k + shifted(k, offset))
         weights(m, ref[0])
     across = 4 * planes

time: 33.8 us -> 33.8 us (level)
  no operation moved by 1% of the time
where the time goes in v7:
time: 33.8 us; the launch traced here: 33.7 us
  starting transfers between devices  14.4 us (43%)
  Pallas kernels  12.7 us (38%)
  waiting for transfers between devices  4.58 us (14%)
  other arithmetic  1.8 us (5%)
    ppermute x11, starting transfers between devices, exchange(): return lax.ppermute(values, axis, [(i, i ^ apart) for i in range(count)])  14.2 us
    pallas_call x5, Pallas kernels, call(): pl.pallas_call(kernel, out_shape=out_shape, in_specs=[whole] * len(operan...  12.7 us
    ppermute x11, waiting for transfers between devices, exchange(): return lax.ppermute(values, axis, [(i, i ^ apart) for i in range(count)])  4.57 us
    select_n x1, other arithmetic, local(): own = jnp.where(which == 0, right_modes, adjoint_modes)  0.99 us
    squeeze x1, other arithmetic, local(): return total[0]  0.68 us
  transfers between devices with their start and end apart: 12, of which 8 were waited for; matrix products, arithmetic and copies ran while one was open for 0% of the time, Pallas kernels for 33%

profile of v7, /device:TPU:0, one launch (start us, length us, event | category | flops | bytes accessed | tf_op | source)
XLA Modules:
  0.0 33.7 jit_solution(4052420322988464165)
XLA Ops:
  0.0 1.0 %broadcast_select_fusion.refs_1_ = f32[2,64,256]{2,1,0:T(8,128)S(1)} fusion(f32[64,256]{1,0:T(8,128)} %bitcast.8, f32[64,256]{1,0:T(8,128)} %bitcast.10, pred[2]{0:T(512)(128)(4,1)S(1)} %iota_compare_fusion), kind=kLoop, calls=%fused_computation.5 | loop fusion | flops 32768 | bytes 262146 | tf_op jit(solution)/shard_map/jit(_where)/select_n | solution.py:373
  1.0 3.1 %collective-permute-start.1 = (f32[2,64,256]{2,1,0:T(8,128)S(1)}, f32[2,64,256]{2,1,0:T(8,128)S(1)}, u32[]{:S(2)}, u32[]{:S(2)}) collective-permute-start(f32[2,64,256]{2,1,0:T(8,128)S(1)} %broadcast_select_fusion.refs_1_), channel_id=1, source_target_pairs={{0,2},{1,3},{2,0},{3,1},{4,6},{5,7},{6,4},{7,5},{8,10},{9,11},{10,... | collective-permute-start | bytes 393224 | tf_op jit(solution)/shard_map/ppermute | solution.py:352
  4.1 1.5 %collective-permute-start = (f32[2,64,256]{2,1,0:T(8,128)S(1)}, f32[2,64,256]{2,1,0:T(8,128)S(1)}, u32[]{:S(2)}, u32[]{:S(2)}) collective-permute-start(f32[2,64,256]{2,1,0:T(8,128)S(1)} %broadcast_select_fusion.refs_1_), channel_id=1, source_target_pairs={{0,1},{1,0},{2,3},{3,2},{4,5},{5,4},{6,7},{7,6},{8,9},{9,8},{10,11... | collective-permute-start | bytes 393224 | tf_op jit(solution)/shard_map/ppermute | solution.py:352
  5.6 2.6 %collective-permute-start.3 = (f32[2,64,256]{2,1,0:T(8,128)S(1)}, f32[2,64,256]{2,1,0:T(8,128)S(1)}, u32[]{:S(2)}, u32[]{:S(2)}) collective-permute-start(f32[2,64,256]{2,1,0:T(8,128)S(1)} %broadcast_select_fusion.refs_1_), channel_id=1, source_target_pairs={{0,4},{1,5},{2,6},{3,7},{4,0},{5,1},{6,2},{7,3},{8,12},{9,13},{10,... | collective-permute-start | bytes 393224 | tf_op jit(solution)/shard_map/ppermute | solution.py:352
  8.2 2.6 %collective-permute-start.2 = (f32[2,64,256]{2,1,0:T(8,128)S(1)}, f32[2,64,256]{2,1,0:T(8,128)S(1)}, u32[]{:S(2)}, u32[]{:S(2)}) collective-permute-start(f32[2,64,256]{2,1,0:T(8,128)S(1)} %collective-permute-done.1.refs_3_), channel_id=1, source_target_pairs={{0,1},{1,0},{2,3},{3,2},{4,5},{5,4},{6,7},{7,6},{8,9},{9,8},{10,11... | collective-permute-start | bytes 393224 | tf_op jit(solution)/shard_map/ppermute | solution.py:352
  10.8 0.0 copy-start.1
  10.8 0.0 copy-start.2
  10.8 0.0 collective-permute-done.refs_2_
  10.8 2.9 %shard_map.37.refs_5_ = f32[32,64,128]{2,1,0:T(8,128)S(1)} custom-call(f32[8,32,256]{2,1,0:T(8,128)S(1)} %copy-done, f32[2,64,256]{2,1,0:T(8,128)S(1)} %broadcast_select_fusion.refs_1_, f32[2,64,256]{2,1,0:T(8,128)S(1)} %collective-permute-done.refs_2_), custom_call_target="tpu_custom_call" | custom-call | flops 536870912 | bytes 4194304 | tf_op jit(solution)/shard_map/pallas_call | solution.py:303
  13.7 0.3 collective-permute-done.3.refs_5_
  14.0 0.0 collective-permute-start.5
  14.0 0.0 collective-permute-done.2.refs_4_
  14.0 0.1 select_select_fusion
  14.1 0.2 collective-permute-start.7
  14.4 1.6 %collective-permute-start.4 = (f32[2,64,256]{2,1,0:T(8,128)S(1)}, f32[2,64,256]{2,1,0:T(8,128)S(1)}, u32[]{:S(2)}, u32[]{:S(2)}) collective-permute-start(f32[2,64,256]{2,1,0:T(8,128)S(1)} %collective-permute-done.3.refs_5_), channel_id=1, source_target_pairs={{0,1},{1,0},{2,3},{3,2},{4,5},{5,4},{6,7},{7,6},{8,9},{9,8},{10,11... | collective-permute-start | bytes 393224 | tf_op jit(solution)/shard_map/ppermute | solution.py:352
  16.0 2.6 %shard_map.38.refs_9_ = f32[32,64,128]{2,1,0:T(8,128)S(1)} custom-call(f32[8,32,256]{2,1,0:T(8,128)S(1)} %copy-done, f32[2,64,256]{2,1,0:T(8,128)S(1)} %broadcast_select_fusion.refs_1_, f32[2,64,256]{2,1,0:T(8,128)S(1)} %collective-permute-done.refs_2_, f32[2,64,256]{2,1,0:T(8,128)S(1)} %collective-permute-done.1.refs_3_, ...), custom_call_target="tpu_custom_call" | custom-call | flops 536870912 | bytes 4194304 | tf_op jit(solution)/shard_map/pallas_call | solution.py:303
  18.6 0.3 collective-permute-done.5.refs_7_
  19.0 0.6 %collective-permute-start.6 = (f32[2,64,256]{2,1,0:T(8,128)S(1)}, f32[2,64,256]{2,1,0:T(8,128)S(1)}, u32[]{:S(2)}, u32[]{:S(2)}) collective-permute-start(f32[2,64,256]{2,1,0:T(8,128)S(1)} %collective-permute-done.5.refs_7_), channel_id=1, source_target_pairs={{0,1},{1,0},{2,3},{3,2},{4,5},{5,4},{6,7},{7,6},{8,9},{9,8},{10,11... | collective-permute-start | bytes 393224 | tf_op jit(solution)/shard_map/ppermute | solution.py:352
  19.6 0.5 %collective-permute-done.4.refs_6_ = f32[2,64,256]{2,1,0:T(8,128)S(1)} collective-permute-done((f32[2,64,256]{2,1,0:T(8,128)S(1)}, f32[2,64,256]{2,1,0:T(8,128)S(1)}, u32[]{:S(2)}, u32[]{:S(2)}) %collective-permute-start.4) | collective-permute-done | bytes 131104 | tf_op jit(solution)/shard_map/ppermute | solution.py:352
  20.1 3.5 %shard_map.39.refs_10_ = f32[32,64,128]{2,1,0:T(8,128)S(1)} custom-call(f32[8,32,256]{2,1,0:T(8,128)S(1)} %copy-done, f32[2,64,256]{2,1,0:T(8,128)S(1)} %broadcast_select_fusion.refs_1_, f32[2,64,256]{2,1,0:T(8,128)S(1)} %collective-permute-done.refs_2_, f32[2,64,256]{2,1,0:T(8,128)S(1)} %collective-permute-done.1.refs_3_, ...), custom_call_target="tpu_custom_call" | custom-call | flops 536870912 | bytes 4194304 | tf_op jit(solution)/shard_map/pallas_call | solution.py:303
  23.6 0.7 %collective-permute-done.6.refs_8_ = f32[2,64,256]{2,1,0:T(8,128)S(1)} collective-permute-done((f32[2,64,256]{2,1,0:T(8,128)S(1)}, f32[2,64,256]{2,1,0:T(8,128)S(1)}, u32[]{:S(2)}, u32[]{:S(2)}) %collective-permute-start.6) | collective-permute-done | bytes 131104 | tf_op jit(solution)/shard_map/ppermute | solution.py:352
  24.3 1.7 %shard_map.40 = (f32[1,32,1024]{2,1,0:T(8,128)S(1)}, f32[1,32,1024]{2,1,0:T(8,128)S(1)}) custom-call(f32[8,32,256]{2,1,0:T(8,128)S(1)} %copy-done, f32[2,64,256]{2,1,0:T(8,128)S(1)} %broadcast_select_fusion.refs_1_, f32[2,64,256]{2,1,0:T(8,128)S(1)} %collective-permute-done.refs_2_, f32[2,64,256]{2,1,0:T(8,128)S(1)} %collective-permute-done.1.refs_3_, ...), custom_call_target="tpu_custom_call" | custom-call | flops 536870912 | bytes 4194304 | tf_op jit(solution)/shard_map/pallas_call | solution.py:303
  25.9 0.1 collective-permute-start.8
  26.0 1.3 %collective-permute-done.8 = f32[1,32,1024]{2,1,0:T(8,128)S(1)} collective-permute-done((f32[1,32,1024]{2,1,0:T(8,128)S(1)}, f32[1,32,1024]{2,1,0:T(8,128)S(1)}, u32[]{:S(2)}, u32[]{:S(2)}) %collective-permute-start.8) | collective-permute-done | bytes 131104 | tf_op jit(solution)/shard_map/ppermute | solution.py:352
  27.4 1.6 %collective-permute-start.11 = (f32[1,32,1024]{2,1,0:T(8,128)S(1)}, f32[1,32,1024]{2,1,0:T(8,128)S(1)}, u32[]{:S(2)}, u32[]{:S(2)}) collective-permute-start(f32[1,32,1024]{2,1,0:T(8,128)S(1)} %add.15), channel_id=1, source_target_pairs={{0,16},{8,24},{16,0},{24,8},{1,17},{9,25},{17,1},{25,9},{2,18},{10... | collective-permute-start | bytes 393224 | tf_op jit(solution)/shard_map/ppermute | solution.py:352
  28.9 2.1 %shard_map.41 = (f32[1,32,1024]{2,1,0:T(8,128)S(1)}, f32[1,32,1024]{2,1,0:T(8,128)S(1)}) custom-call(f32[8,32,256]{2,1,0:T(8,128)S(1)} %copy-done, f32[2,64,256]{2,1,0:T(8,128)S(1)} %broadcast_select_fusion.refs_1_, f32[2,64,256]{2,1,0:T(8,128)S(1)} %collective-permute-done.refs_2_, f32[2,64,256]{2,1,0:T(8,128)S(1)} %collective-permute-done.1.refs_3_, ...), custom_call_target="tpu_custom_call" | custom-call | tf_op jit(solution)/shard_map/pallas_call | solution.py:303
  31.0 0.1 collective-permute-start.10
  31.1 0.5 %collective-permute-start.9 = (f32[1,16,1024]{2,1,0:T(8,128)S(1)}, f32[1,16,1024]{2,1,0:T(8,128)S(1)}, u32[]{:S(2)}, u32[]{:S(2)}) collective-permute-start(f32[1,16,1024]{2,1,0:T(8,128)S(1)} %get-tuple-element.21), channel_id=1, source_target_pairs={{0,8},{8,0},{16,24},{24,16},{1,9},{9,1},{17,25},{25,17},{2,10},{10... | collective-permute-start | bytes 196616 | tf_op jit(solution)/shard_map/ppermute | solution.py:352
  31.6 0.7 %collective-permute-done.10 = f32[1,16,1024]{2,1,0:T(8,128)S(1)} collective-permute-done((f32[1,16,1024]{2,1,0:T(8,128)S(1)}, f32[1,16,1024]{2,1,0:T(8,128)S(1)}, u32[]{:S(2)}, u32[]{:S(2)}) %collective-permute-start.10) | collective-permute-done | bytes 65568 | tf_op jit(solution)/shard_map/ppermute | solution.py:352
  32.4 0.2 collective-permute-done.9
  32.5 0.5 %collective-permute-done.11 = f32[1,32,1024]{2,1,0:T(8,128)S(1)} collective-permute-done((f32[1,32,1024]{2,1,0:T(8,128)S(1)}, f32[1,32,1024]{2,1,0:T(8,128)S(1)}, u32[]{:S(2)}, u32[]{:S(2)}) %collective-permute-start.11) | collective-permute-done | bytes 131104 | tf_op jit(solution)/shard_map/ppermute | solution.py:352
  33.0 0.7 %fusion.1 = f32[32,1024]{1,0:T(8,128)} fusion(f32[1,32,1024]{2,1,0:T(8,128)S(1)} %collective-permute-done.11, f32[1,32,1024]{2,1,0:T(8,128)S(1)} %get-tuple-element.19, f32[1,16,1024]{2,1,0:T(8,128)S(1)} %collective-permute-done.10, f32[1,16,1024]{2,1,0:T(8,128)S(1)} %collective-permute-done.9), kind=kLoop, calls=%fused_computation.3 | loop fusion | flops 98304 | bytes 524288 | tf_op jit(solution)/shard_map/squeeze | solution.py:429
  (11 shorter events, 0.1 us)
Async XLA Ops:
  0.0 10.8 %copy-start = (f32[8,32,256]{2,1,0:T(8,128)S(1)}, f32[8,32,256]{2,1,0:T(8,128)}, u32[]{:S(2)}) copy-start(f32[8,32,256]{2,1,0:T(8,128)} %refs_0_.9) | copy-start | bytes 786436
  1.0 7.2 %collective-permute-start.1 = (f32[2,64,256]{2,1,0:T(8,128)S(1)}, f32[2,64,256]{2,1,0:T(8,128)S(1)}, u32[]{:S(2)}, u32[]{:S(2)}) collective-permute-start(f32[2,64,256]{2,1,0:T(8,128)S(1)} %broadcast_select_fusion.refs_1_), channel_id=1, source_target_pairs={{0,2},{1,3},{2,0},{3,1},{4,6},{5,7},{6,4},{7,5},{8,10},{9,11},{10,... | collective-permute-start | bytes 393224 | tf_op jit(solution)/shard_map/ppermute | solution.py:352
  4.1 6.7 %collective-permute-start = (f32[2,64,256]{2,1,0:T(8,128)S(1)}, f32[2,64,256]{2,1,0:T(8,128)S(1)}, u32[]{:S(2)}, u32[]{:S(2)}) collective-permute-start(f32[2,64,256]{2,1,0:T(8,128)S(1)} %broadcast_select_fusion.refs_1_), channel_id=1, source_target_pairs={{0,1},{1,0},{2,3},{3,2},{4,5},{5,4},{6,7},{7,6},{8,9},{9,8},{10,11... | collective-permute-start | bytes 393224 | tf_op jit(solution)/shard_map/ppermute | solution.py:352
  5.6 8.4 %collective-permute-start.3 = (f32[2,64,256]{2,1,0:T(8,128)S(1)}, f32[2,64,256]{2,1,0:T(8,128)S(1)}, u32[]{:S(2)}, u32[]{:S(2)}) collective-permute-start(f32[2,64,256]{2,1,0:T(8,128)S(1)} %broadcast_select_fusion.refs_1_), channel_id=1, source_target_pairs={{0,4},{1,5},{2,6},{3,7},{4,0},{5,1},{6,2},{7,3},{8,12},{9,13},{10,... | collective-permute-start | bytes 393224 | tf_op jit(solution)/shard_map/ppermute | solution.py:352
  8.2 5.8 %collective-permute-start.2 = (f32[2,64,256]{2,1,0:T(8,128)S(1)}, f32[2,64,256]{2,1,0:T(8,128)S(1)}, u32[]{:S(2)}, u32[]{:S(2)}) collective-permute-start(f32[2,64,256]{2,1,0:T(8,128)S(1)} %collective-permute-done.1.refs_3_), channel_id=1, source_target_pairs={{0,1},{1,0},{2,3},{3,2},{4,5},{5,4},{6,7},{7,6},{8,9},{9,8},{10,11... | collective-permute-start | bytes 393224 | tf_op jit(solution)/shard_map/ppermute | solution.py:352
  10.8 3.2 %copy-start.1 = (f32[1,64,256]{2,1,0:T(8,128)S(1)}, f32[1,64,256]{2,1,0:T(8,128)}, u32[]{:S(2)}) copy-start(f32[1,64,256]{2,1,0:T(8,128)} %param.4) | copy-start | bytes 196612
  10.8 3.2 %copy-start.2 = (f32[1,64,256]{2,1,0:T(8,128)S(1)}, f32[1,64,256]{2,1,0:T(8,128)}, u32[]{:S(2)}) copy-start(f32[1,64,256]{2,1,0:T(8,128)} %param.3) | copy-start | bytes 196612
  14.0 5.0 %collective-permute-start.5 = (f32[2,64,256]{2,1,0:T(8,128)S(1)}, f32[2,64,256]{2,1,0:T(8,128)S(1)}, u32[]{:S(2)}, u32[]{:S(2)}) collective-permute-start(f32[2,64,256]{2,1,0:T(8,128)S(1)} %collective-permute-done.3.refs_5_), channel_id=1, source_target_pairs={{0,2},{1,3},{2,0},{3,1},{4,6},{5,7},{6,4},{7,5},{8,10},{9,11},{10,... | collective-permute-start | bytes 393224 | tf_op jit(solution)/shard_map/ppermute | solution.py:352
  14.1 6.0 %collective-permute-start.7 = (f32[160,256]{1,0:T(8,128)S(1)}, f32[160,256]{1,0:T(8,128)S(1)}, u32[]{:S(2)}, u32[]{:S(2)}) collective-permute-start(f32[160,256]{1,0:T(8,128)S(1)} %pad_maximum_fusion), channel_id=1, source_target_pairs={{8,0},{9,1},{10,2},{11,3},{4,12},{5,13},{6,14},{7,15},{16,8},{17,9... | collective-permute-start | bytes 491528 | tf_op jit(solution)/shard_map/ppermute | solution.py:408
  14.4 5.7 %collective-permute-start.4 = (f32[2,64,256]{2,1,0:T(8,128)S(1)}, f32[2,64,256]{2,1,0:T(8,128)S(1)}, u32[]{:S(2)}, u32[]{:S(2)}) collective-permute-start(f32[2,64,256]{2,1,0:T(8,128)S(1)} %collective-permute-done.3.refs_5_), channel_id=1, source_target_pairs={{0,1},{1,0},{2,3},{3,2},{4,5},{5,4},{6,7},{7,6},{8,9},{9,8},{10,11... | collective-permute-start | bytes 393224 | tf_op jit(solution)/shard_map/ppermute | solution.py:352
  19.0 5.3 %collective-permute-start.6 = (f32[2,64,256]{2,1,0:T(8,128)S(1)}, f32[2,64,256]{2,1,0:T(8,128)S(1)}, u32[]{:S(2)}, u32[]{:S(2)}) collective-permute-start(f32[2,64,256]{2,1,0:T(8,128)S(1)} %collective-permute-done.5.refs_7_), channel_id=1, source_target_pairs={{0,1},{1,0},{2,3},{3,2},{4,5},{5,4},{6,7},{7,6},{8,9},{9,8},{10,11... | collective-permute-start | bytes 393224 | tf_op jit(solution)/shard_map/ppermute | solution.py:352
  25.9 1.4 %collective-permute-start.8 = (f32[1,32,1024]{2,1,0:T(8,128)S(1)}, f32[1,32,1024]{2,1,0:T(8,128)S(1)}, u32[]{:S(2)}, u32[]{:S(2)}) collective-permute-start(f32[1,32,1024]{2,1,0:T(8,128)S(1)} %get-tuple-element.17), channel_id=1, source_target_pairs={{0,8},{8,0},{16,24},{24,16},{1,9},{9,1},{17,25},{25,17},{2,10},{10... | collective-permute-start | bytes 393224 | tf_op jit(solution)/shard_map/ppermute | solution.py:352
  27.4 5.6 %collective-permute-start.11 = (f32[1,32,1024]{2,1,0:T(8,128)S(1)}, f32[1,32,1024]{2,1,0:T(8,128)S(1)}, u32[]{:S(2)}, u32[]{:S(2)}) collective-permute-start(f32[1,32,1024]{2,1,0:T(8,128)S(1)} %add.15), channel_id=1, source_target_pairs={{0,16},{8,24},{16,0},{24,8},{1,17},{9,25},{17,1},{25,9},{2,18},{10... | collective-permute-start | bytes 393224 | tf_op jit(solution)/shard_map/ppermute | solution.py:352
  31.0 1.3 %collective-permute-start.10 = (f32[1,16,1024]{2,1,0:T(8,128)S(1)}, f32[1,16,1024]{2,1,0:T(8,128)S(1)}, u32[]{:S(2)}, u32[]{:S(2)}) collective-permute-start(f32[1,16,1024]{2,1,0:T(8,128)S(1)} %get-tuple-element.22), channel_id=1, source_target_pairs={{0,8},{8,0},{16,24},{24,16},{1,9},{9,1},{17,25},{25,17},{2,10},{10... | collective-permute-start | bytes 196616 | tf_op jit(solution)/shard_map/ppermute | solution.py:352
  31.1 1.4 %collective-permute-start.9 = (f32[1,16,1024]{2,1,0:T(8,128)S(1)}, f32[1,16,1024]{2,1,0:T(8,128)S(1)}, u32[]{:S(2)}, u32[]{:S(2)}) collective-permute-start(f32[1,16,1024]{2,1,0:T(8,128)S(1)} %get-tuple-element.21), channel_id=1, source_target_pairs={{0,8},{8,0},{16,24},{24,16},{1,9},{9,1},{17,25},{25,17},{2,10},{10... | collective-permute-start | bytes 196616 | tf_op jit(solution)/shard_map/ppermute | solution.py:352

commit v8 on v7

--- a/solution.py
+++ b/solution.py
@@ -54,8 +54,7 @@
     linked = 1 if stage == 1 else 0 if stage == 0 else 1 + extra if pairs == 4 else 2 + extra
 
     def weights(slot, values):
-        both = jnp.concatenate(split(values), 0)
-        w_ref[slot] = jnp.concatenate([both, both], 1)
+        w_ref[slot] = jnp.concatenate(split(values), 0)
 
     in_plane = [(own_ref, 2 * w + y), (other_ref, 2 * w + 1 - y)]
     if extra:
@@ -78,8 +77,7 @@
         def edge(slot, here, there, coeff):
             da_ref[link + slot] = here[1] - there[1]
             kb_ref[link + slot] = coeff
-            both = jnp.concatenate(split(here[0] - there[0]), 0)
-            w_ref[len(in_plane) + slot] = jnp.concatenate([both, both], 1)
+            w_ref[len(in_plane) + slot] = jnp.concatenate(split(here[0] - there[0]), 0)
 
         slot = edges(stage, (0, 1), 0, n_term, n_space, k_ref, blocks, halo_ref, edge)
         if extra:
@@ -89,7 +87,7 @@
             def _():
                 da_ref[link + index] = jnp.zeros((modes, cells), F32)
                 kb_ref[link + index] = jnp.zeros((terms, cells), F32)
-                w_ref[len(in_plane) + index] = jnp.zeros((2 * modes, 2 * cells), BF16)
+                w_ref[len(in_plane) + index] = jnp.zeros((2 * modes, cells), BF16)
 
     if stage == 1:
         upward = jnp.where(w % 2 == 0, 1, 0)
@@ -119,7 +117,7 @@
             for index in range(links):
                 rows[planes + index].append(part[link + index])
         used = list(range(planes)) + [len(in_plane) + index for index in range(links)]
-        out = product(rows, jnp.concatenate([w_ref[m] for m in used], 1))
+        out = product(rows, jnp.concatenate([w_ref[m] for m in used for _ in (0, 1)], 1))
         out = out.reshape(terms, step, 2 * modes)
         acc_ref[:, at] = out if first else before_ref[:, at] + out
 
@@ -139,8 +137,7 @@
     def edge(slot, here, there, coeff):
         dz_ref[...] = here[1] - there[1]
         kz_ref[...] = coeff
-        both = jnp.concatenate(split(here[0] - there[0]), 0)
-        wz_ref[...] = jnp.concatenate([both, both], 1)
+        wz_ref[...] = jnp.concatenate(split(here[0] - there[0]), 0)
 
     slot = edges(stage, (0, 1), 0, n_term, n_space, k_ref, blocks, halo_ref, edge, skip=True)
 
@@ -149,7 +146,7 @@
         for r in range(0, modes, GROUP):
             dz = dz_ref[r : r + GROUP, :]
             rows = [[dz * kz_ref[q : q + 1, :] for q in range(terms)]]
-            out = product(rows, wz_ref[...])
+            out = product(rows, jnp.concatenate([wz_ref[...], wz_ref[...]], 1))
             acc_ref[:, r : r + GROUP] += out.reshape(terms, GROUP, 2 * modes)
 
 
@@ -229,8 +226,7 @@
     column_ref, other_ref = blocks[-2], blocks[-1]
 
     def weights(slot, values):
-        both = jnp.concatenate(split(values), 0)
-        w_ref[slot] = jnp.concatenate([both, both], 1)
+        w_ref[slot] = jnp.concatenate(split(values), 0)
 
     in_plane = [(other_ref, 2 * w + 1 - y)]
     if mine:
@@ -277,7 +273,7 @@
                 rows[m].append(total)
             for slot, d in enumerate(links if mine else links + [across]):
                 rows[planes + slot].append(part[d])
-        weight = jnp.concatenate([w_ref[m] for m in range(planes + 2)], 1)
+        weight = jnp.concatenate([w_ref[m] for m in range(planes + 2) for _ in (0, 1)], 1)
         out = product(rows, weight).reshape(terms, step, 2 * modes)
         acc_ref[:terms, index * step : (index + 1) * step] = before_ref[:, at] + out
 
@@ -324,10 +320,10 @@
     scratch = [
         pltpu.VMEM((16, modes, cells), F32),
         pltpu.VMEM((16, terms, cells), F32),
-        pltpu.VMEM((6, 2 * modes, 2 * cells), BF16),
+        pltpu.VMEM((6, 2 * modes, cells), BF16),
         pltpu.VMEM((modes, cells), F32),
         pltpu.VMEM((terms, cells), F32),
-        pltpu.VMEM((2 * modes, 2 * cells), BF16),
+        pltpu.VMEM((2 * modes, cells), BF16),
     ]
     shape = jax.ShapeDtypeStruct((terms, modes, 2 * modes), F32)
     return call(kernel, operands, shape, scratch)
@@ -340,7 +336,7 @@
         pltpu.VMEM((terms + 1, modes // 2, 2 * modes), F32),
         pltpu.VMEM((11, modes, cells), F32),
         pltpu.VMEM((11, terms, cells), F32),
-        pltpu.VMEM((4, 2 * modes, 2 * cells), BF16),
+        pltpu.VMEM((4, 2 * modes, cells), BF16),
     ]
     shape = jax.ShapeDtypeStruct((n_space // 4, terms, modes * modes // n_space), F32)
     kernel = functools.partial(last_kernel, n_term, n_space, mine)

time: 33.8 us -> 33.8 us (level)
  no operation moved by 1% of the time
where the time goes in v8:
time: 33.8 us; the launch traced here: 33.7 us
  starting transfers between devices  14.4 us (43%)
  Pallas kernels  12.7 us (38%)
  waiting for transfers between devices  4.58 us (14%)
  other arithmetic  1.8 us (5%)
    ppermute x11, starting transfers between devices, exchange(): return lax.ppermute(values, axis, [(i, i ^ apart) for i in range(count)])  14.2 us
    pallas_call x5, Pallas kernels, call(): pl.pallas_call(kernel, out_shape=out_shape, in_specs=[whole] * len(operan...  12.7 us
    ppermute x11, waiting for transfers between devices, exchange(): return lax.ppermute(values, axis, [(i, i ^ apart) for i in range(count)])  4.58 us
    select_n x1, other arithmetic, local(): own = jnp.where(which == 0, right_modes, adjoint_modes)  0.99 us
    squeeze x1, other arithmetic, local(): return total[0]  0.68 us
  transfers between devices with their start and end apart: 12, of which 8 were waited for; matrix products, arithmetic and copies ran while one was open for 0% of the time, Pallas kernels for 33%

profile of v8, /device:TPU:0, one launch (start us, length us, event | category | flops | bytes accessed | tf_op | source)
XLA Modules:
  0.0 33.7 jit_solution(131747674658280835)
XLA Ops:
  0.0 1.0 %broadcast_select_fusion.refs_1_ = f32[2,64,256]{2,1,0:T(8,128)S(1)} fusion(f32[64,256]{1,0:T(8,128)} %bitcast.8, f32[64,256]{1,0:T(8,128)} %bitcast.10, pred[2]{0:T(512)(128)(4,1)S(1)} %iota_compare_fusion), kind=kLoop, calls=%fused_computation.5 | loop fusion | flops 32768 | bytes 262146 | tf_op jit(solution)/shard_map/jit(_where)/select_n | solution.py:369
  1.0 3.1 %collective-permute-start.1 = (f32[2,64,256]{2,1,0:T(8,128)S(1)}, f32[2,64,256]{2,1,0:T(8,128)S(1)}, u32[]{:S(2)}, u32[]{:S(2)}) collective-permute-start(f32[2,64,256]{2,1,0:T(8,128)S(1)} %broadcast_select_fusion.refs_1_), channel_id=1, source_target_pairs={{0,2},{1,3},{2,0},{3,1},{4,6},{5,7},{6,4},{7,5},{8,10},{9,11},{10,... | collective-permute-start | bytes 393224 | tf_op jit(solution)/shard_map/ppermute | solution.py:348
  4.1 1.5 %collective-permute-start = (f32[2,64,256]{2,1,0:T(8,128)S(1)}, f32[2,64,256]{2,1,0:T(8,128)S(1)}, u32[]{:S(2)}, u32[]{:S(2)}) collective-permute-start(f32[2,64,256]{2,1,0:T(8,128)S(1)} %broadcast_select_fusion.refs_1_), channel_id=1, source_target_pairs={{0,1},{1,0},{2,3},{3,2},{4,5},{5,4},{6,7},{7,6},{8,9},{9,8},{10,11... | collective-permute-start | bytes 393224 | tf_op jit(solution)/shard_map/ppermute | solution.py:348
  5.6 2.6 %collective-permute-start.3 = (f32[2,64,256]{2,1,0:T(8,128)S(1)}, f32[2,64,256]{2,1,0:T(8,128)S(1)}, u32[]{:S(2)}, u32[]{:S(2)}) collective-permute-start(f32[2,64,256]{2,1,0:T(8,128)S(1)} %broadcast_select_fusion.refs_1_), channel_id=1, source_target_pairs={{0,4},{1,5},{2,6},{3,7},{4,0},{5,1},{6,2},{7,3},{8,12},{9,13},{10,... | collective-permute-start | bytes 393224 | tf_op jit(solution)/shard_map/ppermute | solution.py:348
  8.2 0.0 collective-permute-done.1.refs_3_
  8.2 2.6 %collective-permute-start.2 = (f32[2,64,256]{2,1,0:T(8,128)S(1)}, f32[2,64,256]{2,1,0:T(8,128)S(1)}, u32[]{:S(2)}, u32[]{:S(2)}) collective-permute-start(f32[2,64,256]{2,1,0:T(8,128)S(1)} %collective-permute-done.1.refs_3_), channel_id=1, source_target_pairs={{0,1},{1,0},{2,3},{3,2},{4,5},{5,4},{6,7},{7,6},{8,9},{9,8},{10,11... | collective-permute-start | bytes 393224 | tf_op jit(solution)/shard_map/ppermute | solution.py:348
  10.8 0.0 copy-start.1
  10.8 0.0 copy-start.2
  10.8 0.0 collective-permute-done.refs_2_
  10.8 2.9 %shard_map.37.refs_5_ = f32[32,64,128]{2,1,0:T(8,128)S(1)} custom-call(f32[8,32,256]{2,1,0:T(8,128)S(1)} %copy-done, f32[2,64,256]{2,1,0:T(8,128)S(1)} %broadcast_select_fusion.refs_1_, f32[2,64,256]{2,1,0:T(8,128)S(1)} %collective-permute-done.refs_2_), custom_call_target="tpu_custom_call" | custom-call | flops 536870912 | bytes 4194304 | tf_op jit(solution)/shard_map/pallas_call | solution.py:299
  13.7 0.3 collective-permute-done.3.refs_5_
  14.0 0.0 collective-permute-start.5
  14.0 0.1 select_select_fusion
  14.1 0.2 collective-permute-start.7
  14.4 1.6 %collective-permute-start.4 = (f32[2,64,256]{2,1,0:T(8,128)S(1)}, f32[2,64,256]{2,1,0:T(8,128)S(1)}, u32[]{:S(2)}, u32[]{:S(2)}) collective-permute-start(f32[2,64,256]{2,1,0:T(8,128)S(1)} %collective-permute-done.3.refs_5_), channel_id=1, source_target_pairs={{0,1},{1,0},{2,3},{3,2},{4,5},{5,4},{6,7},{7,6},{8,9},{9,8},{10,11... | collective-permute-start | bytes 393224 | tf_op jit(solution)/shard_map/ppermute | solution.py:348
  16.0 2.6 %shard_map.38.refs_9_ = f32[32,64,128]{2,1,0:T(8,128)S(1)} custom-call(f32[8,32,256]{2,1,0:T(8,128)S(1)} %copy-done, f32[2,64,256]{2,1,0:T(8,128)S(1)} %broadcast_select_fusion.refs_1_, f32[2,64,256]{2,1,0:T(8,128)S(1)} %collective-permute-done.refs_2_, f32[2,64,256]{2,1,0:T(8,128)S(1)} %collective-permute-done.1.refs_3_, ...), custom_call_target="tpu_custom_call" | custom-call | flops 536870912 | bytes 4194304 | tf_op jit(solution)/shard_map/pallas_call | solution.py:299
  18.6 0.3 collective-permute-done.5.refs_7_
  19.0 0.6 %collective-permute-start.6 = (f32[2,64,256]{2,1,0:T(8,128)S(1)}, f32[2,64,256]{2,1,0:T(8,128)S(1)}, u32[]{:S(2)}, u32[]{:S(2)}) collective-permute-start(f32[2,64,256]{2,1,0:T(8,128)S(1)} %collective-permute-done.5.refs_7_), channel_id=1, source_target_pairs={{0,1},{1,0},{2,3},{3,2},{4,5},{5,4},{6,7},{7,6},{8,9},{9,8},{10,11... | collective-permute-start | bytes 393224 | tf_op jit(solution)/shard_map/ppermute | solution.py:348
  19.6 0.5 %collective-permute-done.4.refs_6_ = f32[2,64,256]{2,1,0:T(8,128)S(1)} collective-permute-done((f32[2,64,256]{2,1,0:T(8,128)S(1)}, f32[2,64,256]{2,1,0:T(8,128)S(1)}, u32[]{:S(2)}, u32[]{:S(2)}) %collective-permute-start.4) | collective-permute-done | bytes 131104 | tf_op jit(solution)/shard_map/ppermute | solution.py:348
  20.1 3.5 %shard_map.39.refs_10_ = f32[32,64,128]{2,1,0:T(8,128)S(1)} custom-call(f32[8,32,256]{2,1,0:T(8,128)S(1)} %copy-done, f32[2,64,256]{2,1,0:T(8,128)S(1)} %broadcast_select_fusion.refs_1_, f32[2,64,256]{2,1,0:T(8,128)S(1)} %collective-permute-done.refs_2_, f32[2,64,256]{2,1,0:T(8,128)S(1)} %collective-permute-done.1.refs_3_, ...), custom_call_target="tpu_custom_call" | custom-call | flops 536870912 | bytes 4194304 | tf_op jit(solution)/shard_map/pallas_call | solution.py:299
  23.6 0.7 %collective-permute-done.6.refs_8_ = f32[2,64,256]{2,1,0:T(8,128)S(1)} collective-permute-done((f32[2,64,256]{2,1,0:T(8,128)S(1)}, f32[2,64,256]{2,1,0:T(8,128)S(1)}, u32[]{:S(2)}, u32[]{:S(2)}) %collective-permute-start.6) | collective-permute-done | bytes 131104 | tf_op jit(solution)/shard_map/ppermute | solution.py:348
  24.3 1.6 %shard_map.40 = (f32[1,32,1024]{2,1,0:T(8,128)S(1)}, f32[1,32,1024]{2,1,0:T(8,128)S(1)}) custom-call(f32[8,32,256]{2,1,0:T(8,128)S(1)} %copy-done, f32[2,64,256]{2,1,0:T(8,128)S(1)} %broadcast_select_fusion.refs_1_, f32[2,64,256]{2,1,0:T(8,128)S(1)} %collective-permute-done.refs_2_, f32[2,64,256]{2,1,0:T(8,128)S(1)} %collective-permute-done.1.refs_3_, ...), custom_call_target="tpu_custom_call" | custom-call | flops 536870912 | bytes 4194304 | tf_op jit(solution)/shard_map/pallas_call | solution.py:299
  25.9 0.1 collective-permute-start.8
  26.0 1.3 %collective-permute-done.8 = f32[1,32,1024]{2,1,0:T(8,128)S(1)} collective-permute-done((f32[1,32,1024]{2,1,0:T(8,128)S(1)}, f32[1,32,1024]{2,1,0:T(8,128)S(1)}, u32[]{:S(2)}, u32[]{:S(2)}) %collective-permute-start.8) | collective-permute-done | bytes 131104 | tf_op jit(solution)/shard_map/ppermute | solution.py:348
  27.4 1.6 %collective-permute-start.11 = (f32[1,32,1024]{2,1,0:T(8,128)S(1)}, f32[1,32,1024]{2,1,0:T(8,128)S(1)}, u32[]{:S(2)}, u32[]{:S(2)}) collective-permute-start(f32[1,32,1024]{2,1,0:T(8,128)S(1)} %add.15), channel_id=1, source_target_pairs={{0,16},{8,24},{16,0},{24,8},{1,17},{9,25},{17,1},{25,9},{2,18},{10... | collective-permute-start | bytes 393224 | tf_op jit(solution)/shard_map/ppermute | solution.py:348
  28.9 2.1 %shard_map.41 = (f32[1,32,1024]{2,1,0:T(8,128)S(1)}, f32[1,32,1024]{2,1,0:T(8,128)S(1)}) custom-call(f32[8,32,256]{2,1,0:T(8,128)S(1)} %copy-done, f32[2,64,256]{2,1,0:T(8,128)S(1)} %broadcast_select_fusion.refs_1_, f32[2,64,256]{2,1,0:T(8,128)S(1)} %collective-permute-done.refs_2_, f32[2,64,256]{2,1,0:T(8,128)S(1)} %collective-permute-done.1.refs_3_, ...), custom_call_target="tpu_custom_call" | custom-call | tf_op jit(solution)/shard_map/pallas_call | solution.py:299
  31.0 0.1 collective-permute-start.10
  31.1 0.5 %collective-permute-start.9 = (f32[1,16,1024]{2,1,0:T(8,128)S(1)}, f32[1,16,1024]{2,1,0:T(8,128)S(1)}, u32[]{:S(2)}, u32[]{:S(2)}) collective-permute-start(f32[1,16,1024]{2,1,0:T(8,128)S(1)} %get-tuple-element.21), channel_id=1, source_target_pairs={{0,8},{8,0},{16,24},{24,16},{1,9},{9,1},{17,25},{25,17},{2,10},{10... | collective-permute-start | bytes 196616 | tf_op jit(solution)/shard_map/ppermute | solution.py:348
  31.6 0.7 %collective-permute-done.10 = f32[1,16,1024]{2,1,0:T(8,128)S(1)} collective-permute-done((f32[1,16,1024]{2,1,0:T(8,128)S(1)}, f32[1,16,1024]{2,1,0:T(8,128)S(1)}, u32[]{:S(2)}, u32[]{:S(2)}) %collective-permute-start.10) | collective-permute-done | bytes 65568 | tf_op jit(solution)/shard_map/ppermute | solution.py:348
  32.4 0.2 collective-permute-done.9
  32.5 0.5 %collective-permute-done.11 = f32[1,32,1024]{2,1,0:T(8,128)S(1)} collective-permute-done((f32[1,32,1024]{2,1,0:T(8,128)S(1)}, f32[1,32,1024]{2,1,0:T(8,128)S(1)}, u32[]{:S(2)}, u32[]{:S(2)}) %collective-permute-start.11) | collective-permute-done | bytes 131104 | tf_op jit(solution)/shard_map/ppermute | solution.py:348
  33.0 0.7 %fusion.1 = f32[32,1024]{1,0:T(8,128)} fusion(f32[1,32,1024]{2,1,0:T(8,128)S(1)} %collective-permute-done.11, f32[1,32,1024]{2,1,0:T(8,128)S(1)} %get-tuple-element.19, f32[1,16,1024]{2,1,0:T(8,128)S(1)} %collective-permute-done.10, f32[1,16,1024]{2,1,0:T(8,128)S(1)} %collective-permute-done.9), kind=kLoop, calls=%fused_computation.3 | loop fusion | flops 98304 | bytes 524288 | tf_op jit(solution)/shard_map/squeeze | solution.py:425
  (11 shorter events, 0.1 us)
Async XLA Ops:
  0.0 10.8 %copy-start = (f32[8,32,256]{2,1,0:T(8,128)S(1)}, f32[8,32,256]{2,1,0:T(8,128)}, u32[]{:S(2)}) copy-start(f32[8,32,256]{2,1,0:T(8,128)} %refs_0_.9) | copy-start | bytes 786436
  1.0 7.2 %collective-permute-start.1 = (f32[2,64,256]{2,1,0:T(8,128)S(1)}, f32[2,64,256]{2,1,0:T(8,128)S(1)}, u32[]{:S(2)}, u32[]{:S(2)}) collective-permute-start(f32[2,64,256]{2,1,0:T(8,128)S(1)} %broadcast_select_fusion.refs_1_), channel_id=1, source_target_pairs={{0,2},{1,3},{2,0},{3,1},{4,6},{5,7},{6,4},{7,5},{8,10},{9,11},{10,... | collective-permute-start | bytes 393224 | tf_op jit(solution)/shard_map/ppermute | solution.py:348
  4.1 6.7 %collective-permute-start = (f32[2,64,256]{2,1,0:T(8,128)S(1)}, f32[2,64,256]{2,1,0:T(8,128)S(1)}, u32[]{:S(2)}, u32[]{:S(2)}) collective-permute-start(f32[2,64,256]{2,1,0:T(8,128)S(1)} %broadcast_select_fusion.refs_1_), channel_id=1, source_target_pairs={{0,1},{1,0},{2,3},{3,2},{4,5},{5,4},{6,7},{7,6},{8,9},{9,8},{10,11... | collective-permute-start | bytes 393224 | tf_op jit(solution)/shard_map/ppermute | solution.py:348
  5.6 8.4 %collective-permute-start.3 = (f32[2,64,256]{2,1,0:T(8,128)S(1)}, f32[2,64,256]{2,1,0:T(8,128)S(1)}, u32[]{:S(2)}, u32[]{:S(2)}) collective-permute-start(f32[2,64,256]{2,1,0:T(8,128)S(1)} %broadcast_select_fusion.refs_1_), channel_id=1, source_target_pairs={{0,4},{1,5},{2,6},{3,7},{4,0},{5,1},{6,2},{7,3},{8,12},{9,13},{10,... | collective-permute-start | bytes 393224 | tf_op jit(solution)/shard_map/ppermute | solution.py:348
  8.2 5.8 %collective-permute-start.2 = (f32[2,64,256]{2,1,0:T(8,128)S(1)}, f32[2,64,256]{2,1,0:T(8,128)S(1)}, u32[]{:S(2)}, u32[]{:S(2)}) collective-permute-start(f32[2,64,256]{2,1,0:T(8,128)S(1)} %collective-permute-done.1.refs_3_), channel_id=1, source_target_pairs={{0,1},{1,0},{2,3},{3,2},{4,5},{5,4},{6,7},{7,6},{8,9},{9,8},{10,11... | collective-permute-start | bytes 393224 | tf_op jit(solution)/shard_map/ppermute | solution.py:348
  10.8 3.2 %copy-start.1 = (f32[1,64,256]{2,1,0:T(8,128)S(1)}, f32[1,64,256]{2,1,0:T(8,128)}, u32[]{:S(2)}) copy-start(f32[1,64,256]{2,1,0:T(8,128)} %param.4) | copy-start | bytes 196612
  10.8 3.2 %copy-start.2 = (f32[1,64,256]{2,1,0:T(8,128)S(1)}, f32[1,64,256]{2,1,0:T(8,128)}, u32[]{:S(2)}) copy-start(f32[1,64,256]{2,1,0:T(8,128)} %param.3) | copy-start | bytes 196612
  14.0 5.0 %collective-permute-start.5 = (f32[2,64,256]{2,1,0:T(8,128)S(1)}, f32[2,64,256]{2,1,0:T(8,128)S(1)}, u32[]{:S(2)}, u32[]{:S(2)}) collective-permute-start(f32[2,64,256]{2,1,0:T(8,128)S(1)} %collective-permute-done.3.refs_5_), channel_id=1, source_target_pairs={{0,2},{1,3},{2,0},{3,1},{4,6},{5,7},{6,4},{7,5},{8,10},{9,11},{10,... | collective-permute-start | bytes 393224 | tf_op jit(solution)/shard_map/ppermute | solution.py:348
  14.1 6.0 %collective-permute-start.7 = (f32[160,256]{1,0:T(8,128)S(1)}, f32[160,256]{1,0:T(8,128)S(1)}, u32[]{:S(2)}, u32[]{:S(2)}) collective-permute-start(f32[160,256]{1,0:T(8,128)S(1)} %pad_maximum_fusion), channel_id=1, source_target_pairs={{8,0},{9,1},{10,2},{11,3},{4,12},{5,13},{6,14},{7,15},{16,8},{17,9... | collective-permute-start | bytes 491528 | tf_op jit(solution)/shard_map/ppermute | solution.py:404
  14.4 5.7 %collective-permute-start.4 = (f32[2,64,256]{2,1,0:T(8,128)S(1)}, f32[2,64,256]{2,1,0:T(8,128)S(1)}, u32[]{:S(2)}, u32[]{:S(2)}) collective-permute-start(f32[2,64,256]{2,1,0:T(8,128)S(1)} %collective-permute-done.3.refs_5_), channel_id=1, source_target_pairs={{0,1},{1,0},{2,3},{3,2},{4,5},{5,4},{6,7},{7,6},{8,9},{9,8},{10,11... | collective-permute-start | bytes 393224 | tf_op jit(solution)/shard_map/ppermute | solution.py:348
  19.0 5.3 %collective-permute-start.6 = (f32[2,64,256]{2,1,0:T(8,128)S(1)}, f32[2,64,256]{2,1,0:T(8,128)S(1)}, u32[]{:S(2)}, u32[]{:S(2)}) collective-permute-start(f32[2,64,256]{2,1,0:T(8,128)S(1)} %collective-permute-done.5.refs_7_), channel_id=1, source_target_pairs={{0,1},{1,0},{2,3},{3,2},{4,5},{5,4},{6,7},{7,6},{8,9},{9,8},{10,11... | collective-permute-start | bytes 393224 | tf_op jit(solution)/shard_map/ppermute | solution.py:348
  25.9 1.4 %collective-permute-start.8 = (f32[1,32,1024]{2,1,0:T(8,128)S(1)}, f32[1,32,1024]{2,1,0:T(8,128)S(1)}, u32[]{:S(2)}, u32[]{:S(2)}) collective-permute-start(f32[1,32,1024]{2,1,0:T(8,128)S(1)} %get-tuple-element.17), channel_id=1, source_target_pairs={{0,8},{8,0},{16,24},{24,16},{1,9},{9,1},{17,25},{25,17},{2,10},{10... | collective-permute-start | bytes 393224 | tf_op jit(solution)/shard_map/ppermute | solution.py:348
  27.4 5.6 %collective-permute-start.11 = (f32[1,32,1024]{2,1,0:T(8,128)S(1)}, f32[1,32,1024]{2,1,0:T(8,128)S(1)}, u32[]{:S(2)}, u32[]{:S(2)}) collective-permute-start(f32[1,32,1024]{2,1,0:T(8,128)S(1)} %add.15), channel_id=1, source_target_pairs={{0,16},{8,24},{16,0},{24,8},{1,17},{9,25},{17,1},{25,9},{2,18},{10... | collective-permute-start | bytes 393224 | tf_op jit(solution)/shard_map/ppermute | solution.py:348
  31.0 1.3 %collective-permute-start.10 = (f32[1,16,1024]{2,1,0:T(8,128)S(1)}, f32[1,16,1024]{2,1,0:T(8,128)S(1)}, u32[]{:S(2)}, u32[]{:S(2)}) collective-permute-start(f32[1,16,1024]{2,1,0:T(8,128)S(1)} %get-tuple-element.22), channel_id=1, source_target_pairs={{0,8},{8,0},{16,24},{24,16},{1,9},{9,1},{17,25},{25,17},{2,10},{10... | collective-permute-start | bytes 196616 | tf_op jit(solution)/shard_map/ppermute | solution.py:348
  31.1 1.4 %collective-permute-start.9 = (f32[1,16,1024]{2,1,0:T(8,128)S(1)}, f32[1,16,1024]{2,1,0:T(8,128)S(1)}, u32[]{:S(2)}, u32[]{:S(2)}) collective-permute-start(f32[1,16,1024]{2,1,0:T(8,128)S(1)} %get-tuple-element.21), channel_id=1, source_target_pairs={{0,8},{8,0},{16,24},{24,16},{1,9},{9,1},{17,25},{25,17},{2,10},{10... | collective-permute-start | bytes 196616 | tf_op jit(solution)/shard_map/ppermute | solution.py:348
